TPU v7x, 32 devices: a whole 2x2x4 slice. The times are simulated.
32 devices in a mesh: dp: 8 (over y, x, core), seq: 4 (over z).
Axes of the slice: x: 2, y: 2, z: 4, core: 2. Of those that a mesh axis runs over, the one named last changes fastest.
Arguments:
- tokens: bfloat16 [16, 1024, 1280], P('dp', 'seq'), may hold values from -6 to 6
- protein_lengths: int32 [16, 16], P('dp'), may hold values from 0 to 1024, as said below
- norm1_gain: bfloat16 [2, 1280], P(None, 'dp'), may hold values from 0.099609375 to 1.8984375
- norm1_bias: bfloat16 [2, 1280], P(None, 'dp'), may hold values from -3 to 3
- w_in: bfloat16 [2, 1280, 640], P(None, 'dp', 'seq'), may hold values from -0.15625 to 0.15625
- in_bias: bfloat16 [2, 640], P(None, 'dp'), may hold values from -3 to 3
- norm2_gain: bfloat16 [2, 640], P(None, 'dp'), may hold values from 0.099609375 to 1.8984375
- norm2_bias: bfloat16 [2, 640], P(None, 'dp'), may hold values from -3 to 3
- w_conv: bfloat16 [2, 5, 640, 640], P(None, None, 'dp', 'seq'), may hold values from -0.109375 to 0.109375
- conv_bias: bfloat16 [2, 640], P(None, 'dp'), may hold values from -3 to 3
- norm3_gain: bfloat16 [2, 640], P(None, 'dp'), may hold values from 0.099609375 to 1.8984375
- norm3_bias: bfloat16 [2, 640], P(None, 'dp'), may hold values from -3 to 3
- w_out: bfloat16 [2, 640, 1280], P(None, 'dp', 'seq'), may hold values from -0.3125 to 0.3125
- out_bias: bfloat16 [2, 1280], P(None, 'dp'), may hold values from -2 to 2
- cotangent: bfloat16 [16, 1024, 1280], P('dp', 'seq'), may hold values from -6 to 6
Outputs:
- output: bfloat16 [16, 1024, 1280], P('dp', 'seq')
- input_grad: float32 [16, 1024, 1280], P('dp', 'seq')
- grad_norm1_gain: float32 [2, 1280], P(None, 'dp')
- grad_norm1_bias: float32 [2, 1280], P(None, 'dp')
- grad_w_in: float32 [2, 1280, 640], P(None, 'dp', 'seq')
- grad_in_bias: float32 [2, 640], P(None, 'dp')
- grad_norm2_gain: float32 [2, 640], P(None, 'dp')
- grad_norm2_bias: float32 [2, 640], P(None, 'dp')
- grad_w_conv: float32 [2, 5, 640, 640], P(None, None, 'dp', 'seq')
- grad_conv_bias: float32 [2, 640], P(None, 'dp')
- grad_norm3_gain: float32 [2, 640], P(None, 'dp')
- grad_norm3_bias: float32 [2, 640], P(None, 'dp')
- grad_w_out: float32 [2, 640, 1280], P(None, 'dp', 'seq')
- grad_out_bias: float32 [2, 1280], P(None, 'dp')
Inputs may be any that keep to these rules, and one draw needn't show every extreme that they name: `protein_lengths`: in each row the nonzero lengths come first, each is 30 or more, and together they are at most 1024; in each aligned block of 2 rows, one row holds a protein that begins before position 256 and ends at the row's end.
All inputs are finite; a program needn't handle non-finite values.
Results may differ from a plain program's by a relative error of at most 0.014.
Values may be sent and summed in bfloat16 or wider, within the bound.
No kernel may reach another device: no remote copies, remote signals or barrier semaphores. Data moves between devices by JAX's collectives and lax.ppermute only.
A program may use at most 192 MiB of HBM per device.

v0:
```python
import functools
import math

import jax
import jax.numpy as jnp
from jax import lax
from jax.experimental import pallas as pl
from jax.experimental.pallas import tpu as pltpu
from jax.sharding import PartitionSpec as P

KER = 5
FIRST_DILATION = 64
SECOND_DILATION = 128


epsilon = 1e-05
CUBIC = 0.044715
SLOPE = math.sqrt(2.0 / math.pi)
VECTOR_ROWS = 16


def seq_neighbours(block, width):
    count = lax.axis_size("seq")
    forward = [(i, i + 1) for i in range(count - 1)]
    backward = [(target, source) for source, target in forward]
    low = lax.ppermute(block[:, block.shape[1] - width :], "seq", forward)
    high = lax.ppermute(block[:, :width], "seq", backward)
    return low, high


def normalized(values):
    centred = values - jnp.mean(values, -1, keepdims=True)
    scale = lax.rsqrt(jnp.mean(centred * centred, -1, keepdims=True) + epsilon)
    return centred * scale, scale


def gelu(h):
    return 0.5 * h * (1.0 + jnp.tanh(SLOPE * (h + CUBIC * (h * h * h))))


def norm_gelu(values, gain_vector, bias_vector):
    return gelu(normalized(values)[0] * gain_vector + bias_vector)


def norm_gelu_back(incoming, values, gain_vector, bias_vector):
    n, scale = normalized(values)
    h = n * gain_vector + bias_vector
    square = h * h
    t = jnp.tanh(SLOPE * (h + CUBIC * (square * h)))
    slope = 0.5 * (1.0 + t) + (0.5 * SLOPE) * h * (1.0 - t * t) * (1.0 + (3.0 * CUBIC) * square)
    dh = incoming * slope
    dn = dh * gain_vector
    back = dn - jnp.mean(dn, -1, keepdims=True) - n * jnp.mean(dn * n, -1, keepdims=True)
    return back * scale, column_sum(dh * n), column_sum(dh)


def column_sum(values):
    return jnp.sum(values, axis=0, keepdims=True)


def matmul(left, right):
    return jnp.dot(left, right, preferred_element_type=jnp.float32)


def matmul_back(left, right):
    return lax.dot_general(
        left, right, (((1,), (1,)), ((), ())), preferred_element_type=jnp.float32
    )


def matmul_rows(left, right):
    return lax.dot_general(
        left, right, (((0,), (0,)), ((), ())), preferred_element_type=jnp.float32
    )


def merged(ref):
    parts, rows, columns = ref.shape
    return ref[...].reshape(parts * rows, columns)


def kernel_tap_flags(lengths, token_positions, dilation_step):
    doc_ends = jnp.cumsum(lengths, axis=1)
    row_total = doc_ends[:, -1:]
    where_pos = token_positions[None, :, None]
    finished = doc_ends[:, None, :] <= where_pos
    doc_start = jnp.sum(jnp.where(finished, lengths[:, None, :], 0), axis=2)
    doc_stop = jnp.min(jnp.where(finished, row_total[:, :, None] + 1, doc_ends[:, None, :]), axis=2)
    is_live = token_positions[None, :] < row_total
    flag_list = []
    for tap_index in range(KER):
        target = token_positions[None, :] + (tap_index - KER // 2) * dilation_step
        flag_list.append(is_live & (target >= doc_start) & (target < doc_stop))
    flag_list += [flag_list[-1]] * (8 - KER)
    return jnp.stack(flag_list, axis=2).astype(jnp.bfloat16)


def project_kernel(x_ref, w_ref, wide_ref, narrow_ref, act_one_ref, u_ref, act_two_ref):
    act_one = norm_gelu(
        x_ref[...].astype(jnp.float32), wide_ref[0:1, :], wide_ref[1:2, :]
    ).astype(jnp.bfloat16)
    act_one_ref[...] = act_one
    u = matmul(act_one, merged(w_ref)) + narrow_ref[0:1, :]
    u_ref[...] = u
    act_two_ref[...] = norm_gelu(u, narrow_ref[1:2, :], narrow_ref[2:3, :]).astype(jnp.bfloat16)


def tap_slices(low_ref, own_ref, high_ref, flag_ref, dilation_step):
    length = own_ref.shape[1]
    width = low_ref.shape[1]
    padded = jnp.concatenate([low_ref[0], own_ref[0], high_ref[0]], axis=0)
    for k in range(KER):
        start = width + (k - KER // 2) * dilation_step
        yield k, padded[start : start + length] * flag_ref[0][:, k : k + 1]


def convolve_kernel(
    dilation_step,
    low_ref,
    own_ref,
    high_ref,
    flag_ref,
    x_ref,
    k0_ref,
    k1_ref,
    k2_ref,
    k3_ref,
    k4_ref,
    left_ref,
    right_ref,
    wide_ref,
    narrow_ref,
    tap_ref,
    v_ref,
    act_three_ref,
    next_ref,
):
    taps = (k0_ref, k1_ref, k2_ref, k3_ref, k4_ref)
    hidden = own_ref.shape[2]
    total = narrow_ref[3:4, :]
    for k, piece in tap_slices(low_ref, own_ref, high_ref, flag_ref, dilation_step):
        tap_ref[:, k * hidden : (k + 1) * hidden] = piece
        total = total + matmul(piece, merged(taps[k]))
    v_ref[...] = total
    act_three = norm_gelu(total, narrow_ref[4:5, :], narrow_ref[5:6, :]).astype(jnp.bfloat16)
    act_three_ref[...] = act_three
    for i, half_ref in enumerate((left_ref, right_ref)):
        columns = slice(i * hidden, (i + 1) * hidden)
        branch = matmul(act_three, merged(half_ref)) + wide_ref[2:3, columns]
        next_ref[:, columns] = (x_ref[:, columns].astype(jnp.float32) + branch).astype(
            next_ref.dtype
        )


def out_back_kernel(
    g_ref, v_ref, left_ref, right_ref, narrow_ref, short_ref, gv_ref, narrow_sum_ref, wide_sum_ref
):
    hidden = v_ref.shape[1]

    @pl.when(pl.program_id(0) == 0)
    def _():
        narrow_sum_ref[...] = jnp.zeros_like(narrow_sum_ref)
        wide_sum_ref[...] = jnp.zeros_like(wide_sum_ref)

    short = g_ref[...].astype(jnp.bfloat16)
    short_ref[...] = short
    wide_sum_ref[0:1, :] += column_sum(short.astype(jnp.float32))
    incoming = matmul_back(short[:, :hidden], merged(left_ref))
    incoming = incoming + matmul_back(short[:, hidden:], merged(right_ref))
    gv, gain_sum, bias_sum = norm_gelu_back(
        incoming, v_ref[...], narrow_ref[4:5, :], narrow_ref[5:6, :]
    )
    gv = gv.astype(jnp.bfloat16)
    gv_ref[...] = gv
    narrow_sum_ref[0:1, :] += column_sum(gv.astype(jnp.float32))
    narrow_sum_ref[1:2, :] += gain_sum
    narrow_sum_ref[2:3, :] += bias_sum


def weight_grad_kernel(tap_ref, gv_ref, act_three_ref, short_ref, pack_ref):
    step = pl.program_id(0)

    def store(value):
        pack_ref[...] = value.astype(jnp.bfloat16).reshape(pack_ref.shape)

    @pl.when(step < KER)
    def _():
        store(matmul_rows(tap_ref[...], gv_ref[...]))

    @pl.when(step >= KER)
    def _():
        store(matmul_rows(act_three_ref[...], short_ref[...]))


def conv_back_kernel(
    dilation_step,
    low_ref,
    own_ref,
    high_ref,
    flag_ref,
    u_ref,
    x_ref,
    g_ref,
    k0_ref,
    k1_ref,
    k2_ref,
    k3_ref,
    k4_ref,
    w_ref,
    wide_ref,
    narrow_ref,
    gu_ref,
    next_ref,
    narrow_sum_ref,
    wide_sum_ref,
):
    @pl.when(pl.program_id(0) == 0)
    def _():
        narrow_sum_ref[...] = jnp.zeros_like(narrow_sum_ref)
        wide_sum_ref[...] = jnp.zeros_like(wide_sum_ref)

    taps = (k0_ref, k1_ref, k2_ref, k3_ref, k4_ref)
    total = None
    for k, piece in tap_slices(low_ref, own_ref, high_ref, flag_ref, dilation_step):
        term = matmul_back(piece, merged(taps[KER - 1 - k]))
        total = term if total is None else total + term
    gu, gain_sum, bias_sum = norm_gelu_back(
        total, u_ref[...], narrow_ref[1:2, :], narrow_ref[2:3, :]
    )
    gu = gu.astype(jnp.bfloat16)
    gu_ref[...] = gu
    narrow_sum_ref[0:1, :] += column_sum(gu.astype(jnp.float32))
    narrow_sum_ref[1:2, :] += gain_sum
    narrow_sum_ref[2:3, :] += bias_sum
    gx, gain_sum, bias_sum = norm_gelu_back(
        matmul_back(gu, merged(w_ref)),
        x_ref[...].astype(jnp.float32),
        wide_ref[0:1, :],
        wide_ref[1:2, :],
    )
    next_ref[...] = g_ref[...].astype(jnp.float32) + gx
    wide_sum_ref[0:1, :] += gain_sum
    wide_sum_ref[1:2, :] += bias_sum


def in_grad_kernel(pack_in_ref, act_one_ref, gu_ref, pack_ref):
    value = matmul_rows(act_one_ref[...], gu_ref[...])
    pack_ref[...] = value.astype(jnp.bfloat16).reshape(pack_ref.shape)


def spread(rows, place_ref, hold_ref, own_ref, other_ref):
    chip, core = place_ref[0] // 2, place_ref[0] % 2
    for i in range(own_ref.shape[0]):
        at = 2 * (chip ^ i)
        own_ref[i] = hold_ref[at + core, rows]
        other_ref[i] = hold_ref[at + 1 - core, rows]


def share_grad_kernel(
    place_ref, tap_ref, gv_ref, act_three_ref, short_ref, own_ref, other_ref, hold_ref
):
    step = pl.program_id(0)

    def store(value):
        hold_ref[...] = value.astype(jnp.bfloat16).reshape(hold_ref.shape)

    @pl.when(step < KER)
    def _():
        store(matmul_rows(tap_ref[...], gv_ref[...]))

    @pl.when(step >= KER)
    def _():
        store(matmul_rows(act_three_ref[...], short_ref[...]))

    spread(slice(None), place_ref, hold_ref, own_ref, other_ref)


def share_in_kernel(place_ref, act_one_ref, gu_ref, *refs):
    *sum_refs, own_ref, other_ref, hold_ref = refs
    parts = hold_ref.shape[0]
    hidden = gu_ref.shape[1]
    depth = act_one_ref.shape[1] // parts
    value = matmul_rows(act_one_ref[...], gu_ref[...]).astype(jnp.bfloat16)
    hold_ref[:, :depth, :] = value.reshape(parts, depth, hidden)
    for block in range(len(sum_refs) // 4):
        narrow_a, wide_a, narrow_b, wide_b = (ref[...] for ref in sum_refs[4 * block : 4 * block + 4])
        wide = jnp.concatenate([wide_b[0:2], wide_a[0:1]], axis=0)
        narrow = jnp.concatenate([narrow_b[0:3], narrow_a[0:3]], axis=0)
        narrow_depth = hidden // parts
        for part in range(parts):
            rows = [
                wide[:, part * depth : (part + 1) * depth],
                jnp.concatenate(
                    [
                        narrow[:, part * narrow_depth : (part + 1) * narrow_depth],
                        jnp.zeros((6, depth - narrow_depth), jnp.float32),
                    ],
                    axis=1,
                ),
                jnp.zeros((VECTOR_ROWS - 9, depth), jnp.float32),
            ]
            rows = jnp.concatenate(rows, axis=0)
            rows = jnp.concatenate(
                [rows, jnp.zeros((VECTOR_ROWS, hidden - depth), jnp.float32)], axis=1
            )
            start = depth + block * VECTOR_ROWS
            hold_ref[part, start : start + VECTOR_ROWS, :] = rows.astype(jnp.bfloat16)
    spread(slice(None), place_ref, hold_ref, own_ref, other_ref)


def plus(left, right):
    return left.astype(jnp.float32) + right.astype(jnp.float32)


def first_sum_kernel(cut, count, *refs):
    step = pl.program_id(0)
    keep_a, send_a, keep_b, send_b = refs[2 * count :]
    pieces = [
        plus(own[0], got[0]).astype(jnp.bfloat16) for own, got in zip(refs[:count], refs[count:])
    ]
    total = pieces[0] if count == 1 else jnp.concatenate(pieces, axis=0)
    upper, lower = total[:cut], total[cut:]

    @pl.when(step % 2 == 0)
    def _():
        keep_a[0] = upper

    @pl.when(step % 2 == 1)
    def _():
        send_a[0] = upper

    @pl.when(step < 2)
    def _():
        keep_b[0] = lower

    @pl.when(step >= 2)
    def _():
        send_b[0] = lower


def second_sum_kernel(keep_a, got_a, keep_b, got_b, kept_a, send_a, kept_b, send_b):
    for keep, got, kept, send in (
        (keep_a, got_a, kept_a, send_a),
        (keep_b, got_b, kept_b, send_b),
    ):
        kept[...] = plus(keep[0], got[0]).astype(jnp.bfloat16)
        send[...] = plus(keep[1], got[1]).astype(jnp.bfloat16)


def seq_split_kernel(folded_rows, vector_rows, place_ref, *refs):
    *in_refs, out_ref = refs
    if len(in_refs) == 1:
        total = in_refs[0][...]
    else:
        halves = [plus(in_refs[i][...], in_refs[i + 1][...]) for i in range(0, len(in_refs), 2)]
        total = jnp.concatenate(halves, axis=0)
    total = total.astype(jnp.float32)
    count, rows, width = out_ref.shape
    at, end = folded_rows
    fold = (end - at) // 2
    for s in range(count):
        columns = total[:, s * width : (s + 1) * width]
        if end > at:
            unit = at + (s // 2) * fold
            left = (s % 2) * 2 * width
            pair = total[unit : unit + fold, left : left + 2 * width]
            pieces = [columns[:at], pair[:, :width], pair[:, width:], columns[end:]]
            columns = jnp.concatenate([p for p in pieces if p.shape[0]], axis=0)
        if vector_rows:
            columns = jnp.concatenate(
                [columns[: rows - vector_rows], total[rows - vector_rows :, :width]], axis=0
            )
        out_ref[(s - place_ref[1] + count) % count] = columns.astype(jnp.bfloat16)


def last_sum_kernel(layout, *refs):
    sums = {}
    at = 0
    for name, count in layout:
        own, one, two, three = (ref[...].astype(jnp.float32) for ref in refs[at : at + 4])
        at += 4
        sums[name] = (own + two) + (one + three)
    first_ref, taps_ref, last_ref = refs[at : at + 3]
    vector_refs = refs[at + 3 :]
    depth = taps_ref.shape[2]
    straight = KER * depth
    first_rows = first_ref.shape[1]
    for block, piece in ((0, sums["early"]), (1, sums["late"])):
        for k in range(KER):
            taps_ref[block, k] = piece[k * depth : (k + 1) * depth]
        last_ref[block] = jnp.concatenate(
            [piece[straight : straight + depth], piece[straight + depth : straight + 2 * depth]],
            axis=1,
        )
    rest = sums["early"][straight + 2 * depth :]
    first_ref[0] = rest[first_rows : 2 * first_rows]
    first_ref[1] = rest[:first_rows]
    for block in range(2):
        start = 2 * first_rows + block * VECTOR_ROWS
        for i, ref in enumerate(vector_refs):
            row = rest[start + i : start + i + 1]
            ref[block : block + 1, :] = row[:, : ref.shape[1]]


def tiled(rows, columns):
    return pl.BlockSpec((rows, columns), lambda i: (i, 0))


def fixed(*shape):
    return pl.BlockSpec(shape, lambda i: (0,) * len(shape))


def row_block(shape):
    return pl.BlockSpec((1,) + shape[1:], lambda i: (i, 0, 0))


def pack_block(parts, rows, columns, index):
    return pl.BlockSpec((parts, rows, columns), lambda i: (0, index, 0))


def cost(flops, width):
    return pl.CostEstimate(flops=flops, bytes_accessed=width, transcendentals=0)


def call(kernel, grid, in_specs, out_specs, out_shape, flops, moved, name, aliases=None, scratch=()):
    return pl.pallas_call(
        kernel,
        grid=(grid,),
        in_specs=in_specs,
        out_specs=out_specs,
        out_shape=out_shape,
        scratch_shapes=list(scratch),
        input_output_aliases=aliases or {},
        cost_estimate=cost(flops, moved),
        compiler_params=pltpu.CompilerParams(vmem_limit_bytes=48 * 1024 * 1024),
        name=name,
    )


def shape_of(shape, dtype):
    return jax.ShapeDtypeStruct(shape, dtype)


class Sizes:
    def __init__(self, pack, model, hidden):
        self.parts = pack.shape[0]
        self.model, self.hidden = model, hidden
        self.first_rows = model // self.parts
        self.middle_rows = hidden // self.parts
        self.folds = model // hidden
        self.conv_at = self.first_rows // self.middle_rows
        self.out_at = self.conv_at + KER

    def first(self):
        return pack_block(self.parts, self.first_rows, self.hidden, 0)

    def taps(self):
        return [
            pack_block(self.parts, self.middle_rows, self.hidden, self.conv_at + k)
            for k in range(KER)
        ]

    def last(self):
        return [
            pack_block(self.parts, self.middle_rows, self.hidden, self.out_at + i)
            for i in range(self.folds)
        ]


def project(inputs, weights):
    pack, wide, narrow = weights
    tokens, model = inputs.shape
    hidden = narrow.shape[1]
    sizes = Sizes(pack, model, hidden)
    tile = min(128, tokens)
    return call(
        project_kernel,
        tokens // tile,
        [tiled(tile, model), sizes.first(), fixed(3, model), fixed(6, hidden)],
        [tiled(tile, model), tiled(tile, hidden), tiled(tile, hidden)],
        [
            shape_of((tokens, model), jnp.bfloat16),
            shape_of((tokens, hidden), jnp.float32),
            shape_of((tokens, hidden), jnp.bfloat16),
        ],
        4 * tokens * model * hidden,
        12 * tokens * model,
        "project",
    )(inputs, pack, wide, narrow)


def convolve(act_two, flags, inputs, weights, dilation_step, next_dtype):
    pack, wide, narrow = weights
    rows, length, hidden = act_two.shape
    tokens, model = inputs.shape
    sizes = Sizes(pack, model, hidden)
    low, high = seq_neighbours(act_two, KER // 2 * dilation_step)
    return call(
        functools.partial(convolve_kernel, dilation_step),
        rows,
        [
            row_block(low.shape),
            row_block(act_two.shape),
            row_block(high.shape),
            row_block(flags.shape),
            tiled(length, model),
            *sizes.taps(),
            *sizes.last(),
            fixed(3, model),
            fixed(6, hidden),
        ],
        [
            tiled(length, KER * hidden),
            tiled(length, hidden),
            tiled(length, hidden),
            tiled(length, model),
        ],
        [
            shape_of((tokens, KER * hidden), jnp.bfloat16),
            shape_of((tokens, hidden), jnp.float32),
            shape_of((tokens, hidden), jnp.bfloat16),
            shape_of((tokens, model), next_dtype),
        ],
        2 * tokens * hidden * (KER * hidden + model),
        16 * tokens * model,
        "convolve",
    )(low, act_two, high, flags, inputs, *([pack] * (KER + 2)), wide, narrow)


def out_back(upstream, conv_out, weights):
    pack, wide, narrow = weights
    tokens, model = upstream.shape
    hidden = narrow.shape[1]
    sizes = Sizes(pack, model, hidden)
    tile = min(128, tokens)
    return call(
        out_back_kernel,
        tokens // tile,
        [tiled(tile, model), tiled(tile, hidden), *sizes.last(), fixed(6, hidden)],
        [tiled(tile, model), tiled(tile, hidden), fixed(8, hidden), fixed(8, model)],
        [
            shape_of((tokens, model), jnp.bfloat16),
            shape_of((tokens, hidden), jnp.bfloat16),
            shape_of((8, hidden), jnp.float32),
            shape_of((8, model), jnp.float32),
        ],
        4 * tokens * model * hidden,
        10 * tokens * model,
        "out_back",
    )(upstream, conv_out, pack, pack, narrow)


def weight_grads(tap_rows, gv, act_three, short, pack, conv_at=None):
    tokens, hidden = gv.shape
    model = short.shape[1]
    sizes = Sizes(pack, model, hidden)
    conv_at = sizes.conv_at if conv_at is None else conv_at
    whole = pl.BlockSpec((tokens, hidden), lambda s: (0, 0))
    return call(
        weight_grad_kernel,
        KER + sizes.folds,
        [
            pl.BlockSpec((tokens, hidden), lambda s: (0, jnp.minimum(s, KER - 1))),
            whole,
            whole,
            pl.BlockSpec((tokens, hidden), lambda s: (0, jnp.maximum(s - KER, 0))),
        ],
        pl.BlockSpec(
            (sizes.parts, sizes.middle_rows, hidden), lambda s: (0, conv_at + s, 0)
        ),
        shape_of(pack.shape, jnp.bfloat16),
        2 * tokens * hidden * (KER * hidden + model),
        8 * tokens * model,
        "weight_grads",
    )(tap_rows, gv, act_three, short)


def conv_back(gv, flags, u, inputs, upstream, weights, dilation_step):
    low, high = seq_neighbours(gv, KER // 2 * dilation_step)
    return conv_back_with(low, gv, high, flags, u, inputs, upstream, weights, dilation_step)


def conv_back_with(low, gv, high, flags, u, inputs, upstream, weights, dilation_step):
    pack, wide, narrow = weights
    rows, length, hidden = gv.shape
    tokens, model = inputs.shape
    sizes = Sizes(pack, model, hidden)
    return call(
        functools.partial(conv_back_kernel, dilation_step),
        rows,
        [
            row_block(low.shape),
            row_block(gv.shape),
            row_block(high.shape),
            row_block(flags.shape),
            tiled(length, hidden),
            tiled(length, model),
            tiled(length, model),
            *sizes.taps(),
            sizes.first(),
            fixed(3, model),
            fixed(6, hidden),
        ],
        [tiled(length, hidden), tiled(length, model), fixed(8, hidden), fixed(8, model)],
        [
            shape_of((tokens, hidden), jnp.bfloat16),
            shape_of((tokens, model), jnp.float32),
            shape_of((8, hidden), jnp.float32),
            shape_of((8, model), jnp.float32),
        ],
        2 * tokens * hidden * (KER * hidden + model),
        16 * tokens * model,
        "conv_back",
    )(low, gv, high, flags, u, inputs, upstream, *([pack] * (KER + 1)), wide, narrow)


def in_grads(grad_pack, act_one, gu):
    tokens, model = act_one.shape
    hidden = gu.shape[1]
    sizes = Sizes(grad_pack, model, hidden)
    return call(
        in_grad_kernel,
        1,
        [pl.BlockSpec(memory_space=pl.ANY), fixed(tokens, model), fixed(tokens, hidden)],
        sizes.first(),
        shape_of(grad_pack.shape, jnp.bfloat16),
        2 * tokens * hidden * model,
        4 * tokens * model,
        "in_grads",
        {0: 0},
    )(grad_pack, act_one, gu)


def scalars():
    return pl.BlockSpec(memory_space=pltpu.SMEM)


def place():
    return jnp.stack([lax.axis_index("dp"), lax.axis_index("seq")]).astype(jnp.int32)


def share_grads(where, tap_rows, gv, act_three, short):
    tokens, hidden = gv.shape
    model = short.shape[1]
    parts = lax.axis_size("dp")
    folds = model // hidden
    depth = hidden // parts
    whole = pl.BlockSpec((tokens, hidden), lambda s: (0, 0))
    share = pl.BlockSpec((parts // 2, depth, hidden), lambda s: (0, s, 0))
    shape = shape_of((parts // 2, (KER + folds) * depth, hidden), jnp.bfloat16)
    return call(
        share_grad_kernel,
        KER + folds,
        [
            scalars(),
            pl.BlockSpec((tokens, hidden), lambda s: (0, jnp.minimum(s, KER - 1))),
            whole,
            whole,
            pl.BlockSpec((tokens, hidden), lambda s: (0, jnp.maximum(s - KER, 0))),
        ],
        [share, share],
        [shape, shape],
        2 * tokens * hidden * (KER * hidden + model),
        8 * tokens * model,
        "share_grads",
        scratch=[pltpu.VMEM((parts, depth, hidden), jnp.bfloat16)],
    )(where, tap_rows, gv, act_three, short)


def share_in_grads(where, act_one, gu, sums):
    tokens, model = act_one.shape
    hidden = gu.shape[1]
    parts = lax.axis_size("dp")
    rows = model // parts + len(sums) // 4 * VECTOR_ROWS
    shape = shape_of((parts // 2, rows, hidden), jnp.bfloat16)
    return call(
        share_in_kernel,
        1,
        [scalars()] + [fixed(*array.shape) for array in (act_one, gu, *sums)],
        [fixed(*shape.shape)] * 2,
        [shape, shape],
        2 * tokens * hidden * model,
        4 * tokens * model,
        "share_in_grads",
        scratch=[pltpu.VMEM((parts, rows, hidden), jnp.bfloat16)],
    )(where, act_one, gu, *sums)


def chip_slot(shape, index):
    return pl.BlockSpec((1,) + shape[1:], lambda i: (index(i), 0, 0))


def first_sum(owns, gots):
    hidden = owns[0].shape[2]
    rows = sum(own.shape[1] for own in owns)
    cut = rows // 32 * 16
    a, b = (2, cut, hidden), (2, rows - cut, hidden)
    outs = [
        (a, lambda i: i // 2),
        (a, lambda i: i // 2),
        (b, lambda i: jnp.minimum(i, 1)),
        (b, lambda i: jnp.maximum(i - 2, 0)),
    ]
    return call(
        functools.partial(first_sum_kernel, cut, len(owns)),
        4,
        [chip_slot(array.shape, lambda i: i) for array in (*owns, *gots)],
        [chip_slot(shape, index) for shape, index in outs],
        [shape_of(shape, jnp.bfloat16) for shape, _ in outs],
        4 * rows * hidden,
        24 * rows * hidden,
        "first_sum",
    )(*owns, *gots)


def second_sum(keep_a, got_a, keep_b, got_b):
    ins = (keep_a, got_a, keep_b, got_b)
    outs = [shape_of(array.shape[1:], jnp.bfloat16) for array in ins]
    return call(
        second_sum_kernel,
        1,
        [fixed(*array.shape) for array in ins],
        [fixed(*out.shape) for out in outs],
        outs,
        2 * keep_a.size,
        12 * keep_a.size,
        "second_sum",
    )(*ins)


def seq_split(where, folded_rows, vector_rows, *ins):
    count = lax.axis_size("seq")
    rows = sum(array.shape[0] for array in ins[:: 2 if len(ins) > 1 else 1])
    width = ins[0].shape[1] // count
    shape = (count, rows, width)
    return call(
        functools.partial(seq_split_kernel, folded_rows, vector_rows),
        1,
        [scalars()] + [fixed(*array.shape) for array in ins],
        fixed(*shape),
        shape_of(shape, jnp.bfloat16),
        rows * width * count,
        6 * rows * width * count,
        "seq_split",
    )(where, *ins)


def seq_exchange(split):
    return [split[0]] + [shifted(split[step], step) for step in range(1, split.shape[0])]


def last_sum(pieces, out_shapes):
    flat = [array for _, piece in pieces for array in piece]
    outs = [shape_of(shape, jnp.float32) for shape in out_shapes]
    return call(
        functools.partial(last_sum_kernel, [(name, len(piece)) for name, piece in pieces]),
        1,
        [fixed(*array.shape) for array in flat],
        [fixed(*shape) for shape in out_shapes],
        outs,
        4 * flat[0].size,
        8 * flat[0].size,
        "last_sum",
    )(*flat)


def dp_swapped(block, bit):
    count = lax.axis_size("dp")
    return lax.ppermute(block, "dp", [(i, i ^ (1 << bit)) for i in range(count)])


class Chain:
    def __init__(self, token):
        self.token = token

    def hold(self, *values):
        return lax.optimization_barrier((*values, self.token))[:-1]

    def step(self, function, *values):
        out = function(*self.hold(*values))
        self.token = out[0] if isinstance(out, (list, tuple)) else out
        return out


def shifted(block, step):
    count = lax.axis_size("seq")
    return lax.ppermute(block, "seq", [(i, (i + step) % count) for i in range(count)])


def weight_pack(block_number, device_shards):
    w_in, w_conv, w_out = (device_shards[i][block_number] for i in (2, 6, 10))
    width = w_in.shape[1]
    folds = w_out.shape[1] // width
    pieces = [w_in, w_conv.reshape(-1, width)]
    pieces += [w_out[:, i * width : (i + 1) * width] for i in range(folds)]
    return jnp.concatenate(pieces, axis=0)


def vector_pack(block_number, device_shards, width):
    order = (0, 1, 11, 3, 4, 5, 7, 8, 9)
    rows = [device_shards[i][block_number] for i in order]
    rows = [jnp.pad(row, (0, width - row.shape[0])) for row in rows]
    return jnp.pad(jnp.stack(rows), ((0, VECTOR_ROWS - len(rows)), (0, 0)))


def seq_gathered(packed):
    count = lax.axis_size("seq")
    me = lax.axis_index("seq")
    held = [packed] + [shifted(packed, step) for step in range(1, count)]
    ring = jnp.stack(held[::-1] + held[::-1])
    return lax.dynamic_slice_in_dim(ring, (count - 1 - me) % count, count, axis=0)


def folded_columns(out_parts):
    count, folds, depth, width = out_parts.shape
    per_fold = count // folds
    return (
        out_parts.reshape(folds, per_fold, folds, depth, width)
        .transpose(0, 3, 1, 2, 4)
        .reshape(folds * depth, per_fold * folds * width)
    )


def unfolded_columns(out_rows, folds, count):
    per_fold = count // folds
    depth = out_rows.shape[0] // folds
    width = out_rows.shape[1] // count
    return (
        out_rows.reshape(folds, depth, per_fold, folds, width)
        .transpose(0, 2, 3, 1, 4)
        .reshape(count, folds * depth, width)
    )


def pack_is_aligned(middle_rows):
    return middle_rows % 16 == 0


def gathered_params(block_number, device_shards, after=None):
    w_in, w_conv, w_out = (device_shards[i][block_number] for i in (2, 6, 10))
    first_rows = w_in.shape[0]
    taps, middle_rows, width = w_conv.shape
    folds = w_out.shape[1] // width
    count = lax.axis_size("seq")
    hidden = width * count
    by_seq = seq_gathered(weight_pack(block_number, device_shards))
    straight = first_rows + taps * middle_rows
    total = straight + folds * middle_rows
    upper = by_seq[:, :straight].transpose(1, 0, 2).reshape(straight, hidden)
    lower = folded_columns(by_seq[:, straight:].reshape(count, folds, middle_rows, width))
    vectors = vector_pack(block_number, device_shards, hidden)
    packed = jnp.concatenate([upper, lower, vectors])
    if after is not None:
        packed, after = lax.optimization_barrier((packed, after))
    whole = lax.all_gather(packed, "dp")
    tail = whole[:, total:].astype(jnp.float32)
    wide = tail[:, :3, :first_rows].transpose(1, 0, 2).reshape(3, -1)
    narrow = tail[:, 3:9, :middle_rows].transpose(1, 0, 2).reshape(6, -1)
    if not pack_is_aligned(middle_rows):
        bounds = [0, first_rows]
        bounds += [first_rows + (k + 1) * middle_rows for k in range(taps + folds)]
        whole = jnp.concatenate(
            [whole[:, a:b].reshape(1, -1, hidden) for a, b in zip(bounds, bounds[1:])], axis=1
        )
    return (whole, wide, narrow)


def reduce_dp(grad_pack, wide_grads, narrow_grads):
    parts = lax.axis_size("dp")
    hidden = narrow_grads.shape[1]
    model = wide_grads.shape[1]
    first_rows = model // parts
    middle_rows = hidden // parts
    folds = model // hidden
    total = first_rows + (KER + folds) * middle_rows
    if not pack_is_aligned(middle_rows):
        bounds = [0, model] + [model + (k + 1) * hidden for k in range(KER + folds)]
        grad_pack = jnp.concatenate(
            [grad_pack[0, a:b].reshape(parts, -1, hidden) for a, b in zip(bounds, bounds[1:])]
            + [jnp.zeros((parts, VECTOR_ROWS, hidden), jnp.bfloat16)],
            axis=1,
        )
    vectors = jnp.concatenate(
        [
            jnp.pad(
                block.reshape(-1, parts, rows).transpose(1, 0, 2),
                ((0, 0), (0, 0), (0, hidden - rows)),
            )
            for block, rows in ((wide_grads, first_rows), (narrow_grads, middle_rows))
        ]
        + [jnp.zeros((parts, VECTOR_ROWS - 9, hidden), jnp.float32)],
        axis=1,
    ).astype(jnp.bfloat16)
    grad_pack = lax.dynamic_update_slice(grad_pack, vectors, (0, total, 0))
    return lax.psum_scatter(grad_pack, "dp", scatter_dimension=0, tiled=False)


def reduce_seq(mine, model, hidden):
    parts = lax.axis_size("dp")
    count = lax.axis_size("seq")
    me = lax.axis_index("seq")
    first_rows = model // parts
    middle_rows = hidden // parts
    width = hidden // count
    folds = model // hidden
    straight = first_rows + KER * middle_rows
    total = straight + folds * middle_rows
    upper = mine[:straight].reshape(straight, count, width).transpose(1, 0, 2)
    lower = unfolded_columns(mine[straight:total], folds, count)
    fold = -(-first_rows // width)
    tail = mine[total:, : fold * width].reshape(1, VECTOR_ROWS * fold, width)
    tail = jnp.broadcast_to(tail, (count,) + tail.shape[1:])
    ring = jnp.concatenate([upper, lower, tail], axis=1)
    ring = jnp.concatenate([ring, ring])
    ring = lax.dynamic_slice_in_dim(ring, me, count, axis=0)
    held = [ring[0]] + [shifted(ring[step], step) for step in range(1, count)]
    held = [block.astype(jnp.float32) for block in held]
    while len(held) > 1:
        half = len(held) // 2
        held = [held[i] + held[i + half] for i in range(half)]
    summed = held[0]
    last = summed[straight:total].reshape(folds, middle_rows, width).transpose(1, 0, 2)
    tail = summed[total:].reshape(VECTOR_ROWS, fold * width)
    return (
        summed[:first_rows],
        summed[first_rows:straight].reshape(KER, middle_rows, width),
        last.reshape(middle_rows, folds * width),
        tail[:3, :first_rows],
        tail[3:9, :middle_rows],
    )


def block_forward(inputs, weights, flags, dilation_step, next_dtype):
    rows, length, _ = flags.shape
    act_one, u, act_two = project(inputs, weights)
    tap_rows, conv_out, act_three, output = convolve(
        act_two.reshape(rows, length, -1), flags, inputs, weights, dilation_step, next_dtype
    )
    return output, (act_one, u, tap_rows, conv_out, act_three)


def block_backward(inputs, upstream, weights, kept, flags, dilation_step, before=None):
    act_one, u, tap_rows, conv_out, act_three = kept
    rows, length, _ = flags.shape
    short, gv, narrow_a, wide_a = out_back(upstream, conv_out, weights)
    pack = weights[0]
    grad_shape = shape_of(
        (pack.shape[0], sum(pack_rows(pack, inputs.shape[1], gv.shape[1])), gv.shape[1]),
        jnp.bfloat16,
    )
    grad_pack = weight_grads(tap_rows, gv, act_three, short, grad_shape)
    gu, result, narrow_b, wide_b = conv_back(
        gv.reshape(rows, length, -1), flags, u, inputs, upstream, weights, dilation_step
    )
    if before is not None:
        gu, before = lax.optimization_barrier((gu, before))
    grad_pack = in_grads(grad_pack, act_one, gu)
    wide = jnp.concatenate([wide_b[0:2], wide_a[0:1]])
    narrow = jnp.concatenate([narrow_b[0:3], narrow_a[0:3]])
    return result, reduce_dp(grad_pack, wide, narrow), before


def exchanged_backward(inputs, weights, kept, flags, dilations, cotangent, out_shapes):
    where = place()
    parts = lax.axis_size("dp")
    hidden = weights[1][2].shape[1]
    model = inputs[0].shape[1]
    depth = hidden // parts
    folded = (KER * depth, (KER + model // hidden) * depth)
    rows, length, _ = flags[0].shape

    act_one, u, tap_rows, conv_out, act_three = kept[1]
    short, gv, *out_sums_late = out_back(cotangent, conv_out, weights[1])
    blocks = gv.reshape(rows, length, -1)
    halos = seq_neighbours(blocks, KER // 2 * dilations[1])
    pack_shape = shape_of((parts, folded[1], hidden), jnp.bfloat16)
    pack = weight_grads(tap_rows, gv, act_three, short, pack_shape, 0)
    pack, low, high = lax.optimization_barrier((pack, *halos))
    late_sum = lax.psum_scatter(pack, "dp", scatter_dimension=0, tiled=False)
    gu, middle_grad, *in_sums_late = conv_back_with(
        low, blocks, high, flags[1], u, inputs[1], cotangent, weights[1], dilations[1]
    )
    chain = Chain(gu)
    own_first, other_first = chain.step(
        lambda *values: share_in_grads(where, *values, ()), act_one, gu
    )

    act_one, u, tap_rows, conv_out, act_three = kept[0]
    short, gv, *out_sums = chain.step(
        lambda value: out_back(value, conv_out, weights[0]), middle_grad
    )
    blocks = gv.reshape(rows, length, -1)
    halos = seq_neighbours(blocks, KER // 2 * dilations[0])
    own_taps, other_taps = share_grads(where, tap_rows, gv, act_three, short)
    low, high, own_taps, other_taps, other_first = lax.optimization_barrier(
        (*halos, own_taps, other_taps, other_first)
    )
    got_taps, got_first = dp_swapped(other_taps, 0), dp_swapped(other_first, 0)
    gu, input_grad, *in_sums = chain.step(
        lambda low, high: conv_back_with(
            low, blocks, high, flags[0], u, inputs[0], middle_grad, weights[0], dilations[0]
        ),
        low,
        high,
    )

    def first_round(sums):
        keep_a, send_a, keep_b, send_b = sums
        return keep_a, dp_swapped(send_a, 1), keep_b, dp_swapped(send_b, 2)

    def second_round(sums):
        kept_a, send_a, kept_b, send_b = sums
        return kept_a, dp_swapped(send_a, 2), kept_b, dp_swapped(send_b, 1)

    all_sums = (*out_sums, *in_sums, *out_sums_late, *in_sums_late)
    own, other = chain.step(
        lambda a, b: share_in_grads(where, a, b, all_sums), act_one, gu
    )
    owns = (own_taps, own_first, own)
    gots = (got_taps, got_first, dp_swapped(other, 0))
    main = first_round(
        chain.step(lambda *values: first_sum(values[:3], values[3:]), *owns, *gots)
    )
    late = seq_exchange(chain.step(lambda value: seq_split(where, folded, 0, value), late_sum))
    main, late = lax.optimization_barrier((main, late))
    main = second_round(second_sum(*main))
    main = seq_exchange(seq_split(where, folded, 2 * VECTOR_ROWS, *main))
    return input_grad, last_sum((("early", main), ("late", late)), out_shapes)


def pack_rows(pack, model, hidden):
    parts = pack.shape[0]
    extra = VECTOR_ROWS if pack_is_aligned(hidden // lax.axis_size("dp")) else 0
    return model // parts, (KER * hidden + model) // parts, extra


def local(
    tokens,
    protein_lengths,
    norm1_gain,
    norm1_bias,
    w_in,
    in_bias,
    norm2_gain,
    norm2_bias,
    w_conv,
    conv_bias,
    norm3_gain,
    norm3_bias,
    w_out,
    out_bias,
    cotangent,
):
    device_shards = (
        norm1_gain,
        norm1_bias,
        w_in,
        in_bias,
        norm2_gain,
        norm2_bias,
        w_conv,
        conv_bias,
        norm3_gain,
        norm3_bias,
        w_out,
        out_bias,
    )
    rows, seq_len, model = tokens.shape
    token_positions = lax.axis_index("seq") * seq_len + jnp.arange(seq_len, dtype=jnp.int32)
    early_flags = kernel_tap_flags(protein_lengths, token_positions, FIRST_DILATION)
    later_flags = kernel_tap_flags(protein_lengths, token_positions, SECOND_DILATION)
    early_weights = gathered_params(0, device_shards)
    late_weights = gathered_params(1, device_shards, early_weights[0])
    flat_tokens = tokens.reshape(rows * seq_len, model)
    middle, early_kept = block_forward(
        flat_tokens, early_weights, early_flags, FIRST_DILATION, jnp.float32
    )
    middle, late_weights = lax.optimization_barrier((middle, late_weights))
    output, late_kept = block_forward(
        middle, late_weights, later_flags, SECOND_DILATION, jnp.bfloat16
    )
    hidden = early_weights[2].shape[1]
    if lax.axis_size("dp") == 8 and pack_is_aligned(hidden // 8):
        shapes = [w.shape for w in (w_in, w_conv, w_out, norm1_gain, norm1_bias, out_bias)]
        shapes += [w.shape for w in (in_bias, norm2_gain, norm2_bias)]
        shapes += [w.shape for w in (conv_bias, norm3_gain, norm3_bias)]
        input_grad, grads = exchanged_backward(
            (flat_tokens, middle),
            (early_weights, late_weights),
            (early_kept, late_kept),
            (early_flags, later_flags),
            (FIRST_DILATION, SECOND_DILATION),
            cotangent.reshape(rows * seq_len, model),
            shapes,
        )
        order = (3, 4, 0, 6, 7, 8, 1, 9, 10, 11, 2, 5)
        return (
            output.reshape(tokens.shape),
            input_grad.reshape(tokens.shape),
            *(grads[i] for i in order),
        )
    middle_grad, mine_late, _ = block_backward(
        middle,
        cotangent.reshape(rows * seq_len, model),
        late_weights,
        late_kept,
        later_flags,
        SECOND_DILATION,
    )
    input_grad, mine_early, mine_late = block_backward(
        flat_tokens,
        middle_grad,
        early_weights,
        early_kept,
        early_flags,
        FIRST_DILATION,
        mine_late,
    )
    reduced_late = reduce_seq(mine_late, model, hidden)
    reduced_early = reduce_seq(mine_early, model, hidden)
    first_early, middle_early, last_early, wide_early, narrow_early = reduced_early
    first_late, middle_late, last_late, wide_late, narrow_late = reduced_late
    return (
        output.reshape(tokens.shape),
        input_grad.reshape(tokens.shape),
        jnp.stack([wide_early[0], wide_late[0]]),
        jnp.stack([wide_early[1], wide_late[1]]),
        jnp.stack([first_early, first_late]),
        jnp.stack([narrow_early[0], narrow_late[0]]),
        jnp.stack([narrow_early[1], narrow_late[1]]),
        jnp.stack([narrow_early[2], narrow_late[2]]),
        jnp.stack([middle_early, middle_late]),
        jnp.stack([narrow_early[3], narrow_late[3]]),
        jnp.stack([narrow_early[4], narrow_late[4]]),
        jnp.stack([narrow_early[5], narrow_late[5]]),
        jnp.stack([last_early, last_late]),
        jnp.stack([wide_early[2], wide_late[2]]),
    )


def solution(mesh):
    placed = (
        P("dp", "seq", None),
        P("dp", None),
        P(None, "dp"),
        P(None, "dp"),
        P(None, "dp", "seq"),
        P(None, "dp"),
        P(None, "dp"),
        P(None, "dp"),
        P(None, None, "dp", "seq"),
        P(None, "dp"),
        P(None, "dp"),
        P(None, "dp"),
        P(None, "dp", "seq"),
        P(None, "dp"),
        P("dp", "seq", None),
    )
    return jax.shard_map(
        local,
        mesh=mesh,
        in_specs=placed,
        out_specs=(
            P("dp", "seq", None),
            P("dp", "seq", None),
            P(None, "dp"),
            P(None, "dp"),
            P(None, "dp", "seq"),
            P(None, "dp"),
            P(None, "dp"),
            P(None, "dp"),
            P(None, None, "dp", "seq"),
            P(None, "dp"),
            P(None, "dp"),
            P(None, "dp"),
            P(None, "dp", "seq"),
            P(None, "dp"),
        ),
        check_vma=False,
    )
```

profile of v0, /device:TPU:17, one launch (start us, length us, event | category | flops | bytes accessed | tf_op | source)
XLA Modules:
  0.0 382.5 jit_solution(18288960158977103707)
XLA Ops:
  20.1 23.3 %collective-permute-done = bf16[720,160]{1,0:T(8,128)(2,1)S(1)} collective-permute-done((bf16[720,160]{1,0:T(8,128)(2,1)S(1)}, bf16[720,160]{1,0:T(8,128)(2,1)S(1)}, u32[]{:S(2)}, u32[]{:S(2)}) %collective-permute-start) | collective-permute-done | bytes 230432 | tf_op jit(solution)/shard_map/ppermute | solution.py:787
  51.4 6.2 %collective-permute-done.5 = bf16[720,160]{1,0:T(8,128)(2,1)S(1)} collective-permute-done((bf16[720,160]{1,0:T(8,128)(2,1)S(1)}, bf16[720,160]{1,0:T(8,128)(2,1)S(1)}, u32[]{:S(2)}, u32[]{:S(2)}) %collective-permute-start.5) | collective-permute-done | bytes 230432 | tf_op jit(solution)/shard_map/ppermute | solution.py:787
  58.5 21.8 %collective-permute-done.6 = bf16[720,160]{1,0:T(8,128)(2,1)S(1)} collective-permute-done((bf16[720,160]{1,0:T(8,128)(2,1)S(1)}, bf16[720,160]{1,0:T(8,128)(2,1)S(1)}, u32[]{:S(2)}, u32[]{:S(2)}) %collective-permute-start.6) | collective-permute-done | bytes 230432 | tf_op jit(solution)/shard_map/ppermute | solution.py:787
  90.6 9.4 %all-gather.5.cloned.1.call-done = bf16[5888,640]{1,0:T(8,128)(2,1)} async-done(((bf16[736,640]{1,0:T(8,128)(2,1)}), bf16[5888,640]{1,0:T(8,128)(2,1)}) %all-gather.5.cloned.1.call-update) | async-done | bytes 7536656 | tf_op jit(solution)/shard_map/all_gather | solution.py:855
  103.4 5.6 %project.2 = (bf16[512,1280]{1,0:T(8,128)(2,1)S(1)}, f32[512,640]{1,0:T(8,128)S(1)}, bf16[512,640]{1,0:T(8,128)(2,1)S(1)}) custom-call(bf16[512,1280]{1,0:T(8,128)(2,1)S(1)} %bitcast.113, bf16[8,736,640]{2,1,0:T(8,128)(2,1)} %bitcast.130, f32[3,1280]{1,0:T(4,128)S(1)} %reshape.830.wide_ref, f32[6,640]{1,0:T(8,128)S(1)} %reshape.831.narrow_ref), custom_call_target="tpu_custom_call" | custom-call | flops 1677721600 | bytes 7864320 | tf_op jit(solution)/shard_map/project/pallas_call | solution.py:476
  124.0 9.3 %convolve.2 = (bf16[512,3200]{1,0:T(8,128)(2,1)}, f32[512,640]{1,0:T(8,128)S(1)}, bf16[512,640]{1,0:T(8,128)(2,1)S(1)}, f32[512,1280]{1,0:T(8,128)}) custom-call(bf16[2,128,640]{2,1,0:T(8,128)(2,1)S(1)} %collective-permute-done.3.low_ref, bf16[2,256,640]{2,1,0:T(8,128)(2,1)S(1)} %bitcast.122, bf16[2,128,640]{2,1,0:T(8,128)(2,1)S(1)} %collective-permute-done.4.high_ref, ...), custom_call_target="tpu_custom_call" | custom-call | flops 2936012800 | bytes 10485760 | tf_op jit(solution)/shard_map/convolve/pallas_call | solution.py:498
  135.3 18.0 %all-gather.7.cloned.1.call-done = bf16[5888,640]{1,0:T(8,128)(2,1)} async-done(((bf16[736,640]{1,0:T(8,128)(2,1)}), bf16[5888,640]{1,0:T(8,128)(2,1)}) %all-gather.7.cloned.1.call-update) | async-done | bytes 7536656 | tf_op jit(solution)/shard_map/all_gather | solution.py:855
  156.2 5.5 %project.3 = (bf16[512,1280]{1,0:T(8,128)(2,1)S(1)}, f32[512,640]{1,0:T(8,128)S(1)}, bf16[512,640]{1,0:T(8,128)(2,1)S(1)}) custom-call(f32[512,1280]{1,0:T(8,128)S(1)} %copy-done, bf16[8,736,640]{2,1,0:T(8,128)(2,1)} %bitcast.147, f32[3,1280]{1,0:T(4,128)S(1)} %reshape.835.wide_ref, f32[6,640]{1,0:T(8,128)S(1)} %reshape.836.narrow_ref), custom_call_target="tpu_custom_call" | custom-call | flops 1677721600 | bytes 7864320 | tf_op jit(solution)/shard_map/project/pallas_call | solution.py:476
  166.0 4.1 %collective-permute-start.8 = (bf16[2,256,640]{2,1,0:T(8,128)(2,1)S(1)}, bf16[2,256,640]{2,1,0:T(8,128)(2,1)}, u32[]{:S(2)}, u32[]{:S(2)}) collective-permute-start(bf16[2,256,640]{2,1,0:T(8,128)(2,1)S(1)} %bitcast.127), channel_id=1, source_target_pairs={{0,1},{1,2},{2,3},{4,5},{5,6},{6,7},{8,9},{9,10},{10,11},{12,13},{... | collective-permute-start | bytes 1966088 | tf_op jit(solution)/shard_map/ppermute | solution.py:26
  171.0 10.9 %collective-permute-done.9.high_ref = bf16[2,256,640]{2,1,0:T(8,128)(2,1)} collective-permute-done((bf16[2,256,640]{2,1,0:T(8,128)(2,1)S(1)}, bf16[2,256,640]{2,1,0:T(8,128)(2,1)}, u32[]{:S(2)}, u32[]{:S(2)}) %collective-permute-start.9) | collective-permute-done | bytes 655392 | tf_op jit(solution)/shard_map/ppermute | solution.py:27
  185.3 9.6 %convolve.3 = (bf16[512,3200]{1,0:T(8,128)(2,1)}, f32[512,640]{1,0:T(8,128)S(1)}, bf16[512,640]{1,0:T(8,128)(2,1)S(1)}, bf16[512,1280]{1,0:T(8,128)(2,1)}) custom-call(bf16[2,256,640]{2,1,0:T(8,128)(2,1)} %collective-permute-done.8.low_ref, bf16[2,256,640]{2,1,0:T(8,128)(2,1)S(1)} %bitcast.128, bf16[2,256,640]{2,1,0:T(8,128)(2,1)} %collective-permute-done.9.high_ref, ...), custom_call_target="tpu_custom_call" | custom-call | flops 2936012800 | bytes 10485760 | tf_op jit(solution)/shard_map/convolve/pallas_call | solution.py:498
  194.8 4.9 %out_back.2 = (bf16[512,1280]{1,0:T(8,128)(2,1)S(1)}, bf16[512,640]{1,0:T(8,128)(2,1)S(1)}, f32[8,640]{1,0:T(8,128)S(1)}, f32[8,1280]{1,0:T(8,128)S(1)}) custom-call(bf16[512,1280]{1,0:T(8,128)(2,1)S(1)} %bitcast.116, f32[512,640]{1,0:T(8,128)S(1)} %get-tuple-element.115.v_ref, bf16[8,736,640]{2,1,0:T(8,128)(2,1)} %bitcast.155, ...), custom_call_target="tpu_custom_call" | custom-call | flops 1677721600 | bytes 6553600 | tf_op jit(solution)/shard_map/out_back/pallas_call | solution.py:536
  203.2 4.0 %collective-permute-start.10 = (bf16[2,256,640]{2,1,0:T(8,128)(2,1)S(1)}, bf16[2,256,640]{2,1,0:T(8,128)(2,1)}, u32[]{:S(2)}, u32[]{:S(2)}) collective-permute-start(bf16[2,256,640]{2,1,0:T(8,128)(2,1)S(1)} %bitcast.119), channel_id=1, source_target_pairs={{0,1},{1,2},{2,3},{4,5},{5,6},{6,7},{8,9},{9,10},{10,11},{12,13},{... | collective-permute-start | bytes 1966088 | tf_op jit(solution)/shard_map/ppermute | solution.py:26
  207.1 6.9 %weight_grads.1 = bf16[8,560,640]{2,1,0:T(8,128)(2,1)} custom-call(bf16[512,3200]{1,0:T(8,128)(2,1)S(1)} %copy-done.4, bf16[512,640]{1,0:T(8,128)(2,1)S(1)} %get-tuple-element.116.gv_ref, bf16[512,640]{1,0:T(8,128)(2,1)S(1)} %get-tuple-element.117.act_three_ref, bf16[512,1280]{1,0:T(8,128)(2,1)S(1)} %get-tuple-element.118.short_ref), custom_call_target="tpu_custom_call" | custom-call | flops 2936012800 | bytes 5242880 | tf_op jit(solution)/shard_map/weight_grads/pallas_call | solution.py:559
  214.0 3.8 collective-permute-done.11.high_ref
  222.6 12.7 %conv_back.2 = (bf16[512,640]{1,0:T(8,128)(2,1)S(1)}, f32[512,1280]{1,0:T(8,128)}, f32[8,640]{1,0:T(8,128)S(1)}, f32[8,1280]{1,0:T(8,128)S(1)}) custom-call(bf16[2,256,640]{2,1,0:T(8,128)(2,1)} %collective-permute-done.10.low_ref, bf16[2,256,640]{2,1,0:T(8,128)(2,1)S(1)} %bitcast.120, bf16[2,256,640]{2,1,0:T(8,128)(2,1)} %collective-permute-done.11.high_ref, ...), custom_call_target="tpu_custom_call" | custom-call | flops 2936012800 | bytes 10485760 | tf_op jit(solution)/shard_map/conv_back/pallas_call | solution.py:588
  237.2 5.0 %out_back.3 = (bf16[512,1280]{1,0:T(8,128)(2,1)S(1)}, bf16[512,640]{1,0:T(8,128)(2,1)S(1)}, f32[8,640]{1,0:T(8,128)S(1)}, f32[8,1280]{1,0:T(8,128)S(1)}) custom-call(f32[512,1280]{1,0:T(8,128)S(1)} %copy-done.2, f32[512,640]{1,0:T(8,128)S(1)} %copy-done.9, bf16[8,736,640]{2,1,0:T(8,128)(2,1)} %bitcast.138, bf16[8,736,640]{2,1,0:T(8,128)(2,1)} %bitcast.139, ...), custom_call_target="tpu_custom_call" | custom-call | flops 1677721600 | bytes 6553600 | tf_op jit(solution)/shard_map/out_back/pallas_call | solution.py:536
  248.1 9.0 %share_grads.1 = (bf16[4,560,640]{2,1,0:T(8,128)(2,1)S(1)}, bf16[4,560,640]{2,1,0:T(8,128)(2,1)}) custom-call(s32[2]{0:T(128)S(1)} %pad_add_fusion.place_ref, bf16[512,3200]{1,0:T(8,128)(2,1)} %get-tuple-element.131.tap_ref, bf16[512,640]{1,0:T(8,128)(2,1)S(1)} %get-tuple-element.130.gv_ref, bf16[512,640]{1,0:T(8,128)(2,1)S(1)} %copy-done.29, ...), custom_call_target="tpu_custom_call" | custom-call | flops 2936012800 | bytes 5242880 | tf_op jit(solution)/shard_map/share_grads/pallas_call | solution.py:651
  261.5 12.5 %conv_back.3 = (bf16[512,640]{1,0:T(8,128)(2,1)S(1)}, f32[512,1280]{1,0:T(8,128)}, f32[8,640]{1,0:T(8,128)S(1)}, f32[8,1280]{1,0:T(8,128)S(1)}) custom-call(bf16[2,128,640]{2,1,0:T(8,128)(2,1)S(1)} %collective-permute-done.12.low_ref, bf16[2,256,640]{2,1,0:T(8,128)(2,1)S(1)} %bitcast.124, bf16[2,128,640]{2,1,0:T(8,128)(2,1)S(1)} %collective-permute-done.13.high_ref, ...), custom_call_target="tpu_custom_call" | custom-call | flops 2936012800 | bytes 10485760 | tf_op jit(solution)/shard_map/conv_back/pallas_call | solution.py:588
  279.7 5.8 %first_sum.1 = (bf16[2,448,640]{2,1,0:T(8,128)(2,1)S(1)}, bf16[2,448,640]{2,1,0:T(8,128)(2,1)}, bf16[2,464,640]{2,1,0:T(8,128)(2,1)}, bf16[2,464,640]{2,1,0:T(8,128)(2,1)}) custom-call(bf16[4,560,640]{2,1,0:T(8,128)(2,1)} %copy-done.5, bf16[4,160,640]{2,1,0:T(8,128)(2,1)S(1)} %get-tuple-element.161.refs_1_, ...), custom_call_target="tpu_custom_call" | custom-call | flops 2334720 | bytes 14008320 | tf_op jit(solution)/shard_map/first_sum/pallas_call | solution.py:704
  290.8 22.5 %collective-permute-done.17.got_a = bf16[2,448,640]{2,1,0:T(8,128)(2,1)S(1)} collective-permute-done((bf16[2,448,640]{2,1,0:T(8,128)(2,1)}, bf16[2,448,640]{2,1,0:T(8,128)(2,1)S(1)}, u32[]{:S(2)}, u32[]{:S(2)}) %collective-permute-start.17) | collective-permute-done | bytes 1146912 | tf_op jit(solution)/shard_map/ppermute | solution.py:769
  319.6 13.2 %collective-permute-done.22.refs_1_ = bf16[448,640]{1,0:T(8,128)(2,1)S(1)} collective-permute-done((bf16[448,640]{1,0:T(8,128)(2,1)S(1)}, bf16[448,640]{1,0:T(8,128)(2,1)S(1)}, u32[]{:S(2)}, u32[]{:S(2)}) %collective-permute-start.22) | collective-permute-done | bytes 573472 | tf_op jit(solution)/shard_map/ppermute | solution.py:769
  335.6 9.1 %collective-permute-done.26.refs_3_ = bf16[912,160]{1,0:T(8,128)(2,1)S(1)} collective-permute-done((bf16[912,160]{1,0:T(8,128)(2,1)S(1)}, bf16[912,160]{1,0:T(8,128)(2,1)S(1)}, u32[]{:S(2)}, u32[]{:S(2)}) %collective-permute-start.26) | collective-permute-done | bytes 291872 | tf_op jit(solution)/shard_map/ppermute | solution.py:787
  344.8 28.1 %collective-permute-done.25.refs_2_ = bf16[912,160]{1,0:T(8,128)(2,1)S(1)} collective-permute-done((bf16[912,160]{1,0:T(8,128)(2,1)S(1)}, bf16[912,160]{1,0:T(8,128)(2,1)S(1)}, u32[]{:S(2)}, u32[]{:S(2)}) %collective-permute-start.25) | collective-permute-done | bytes 291872 | tf_op jit(solution)/shard_map/ppermute | solution.py:787
  (255 shorter events, 106.5 us)
Async XLA Ops:
  7.2 92.8 %all-gather.5.cloned.1.call-start = ((), (), s32[]{:S(2)}) async-start(), calls=%async_computation.2 | async-start | bytes 8478720 | tf_op jit(solution)/shard_map/all_gather | solution.py:855
  10.3 33.2 %collective-permute-start.2 = (bf16[720,160]{1,0:T(8,128)(2,1)S(1)}, bf16[720,160]{1,0:T(8,128)(2,1)S(1)}, u32[]{:S(2)}, u32[]{:S(2)}) collective-permute-start(bf16[720,160]{1,0:T(8,128)(2,1)S(1)} %pad_maximum_fusion), channel_id=1, source_target_pairs={{0,1},{1,2},{2,3},{3,0},{4,5},{5,6},{6,7},{7,4},{8,9},{9,10},{10,1... | collective-permute-start | bytes 691208 | tf_op jit(solution)/shard_map/ppermute | solution.py:787
  11.6 31.8 %collective-permute-start.1 = (bf16[720,160]{1,0:T(8,128)(2,1)S(1)}, bf16[720,160]{1,0:T(8,128)(2,1)S(1)}, u32[]{:S(2)}, u32[]{:S(2)}) collective-permute-start(bf16[720,160]{1,0:T(8,128)(2,1)S(1)} %pad_maximum_fusion), channel_id=1, source_target_pairs={{0,2},{1,3},{2,0},{3,1},{4,6},{5,7},{6,4},{7,5},{8,10},{9,11},{10,... | collective-permute-start | bytes 691208 | tf_op jit(solution)/shard_map/ppermute | solution.py:787
  11.7 31.7 %collective-permute-start = (bf16[720,160]{1,0:T(8,128)(2,1)S(1)}, bf16[720,160]{1,0:T(8,128)(2,1)S(1)}, u32[]{:S(2)}, u32[]{:S(2)}) collective-permute-start(bf16[720,160]{1,0:T(8,128)(2,1)S(1)} %pad_maximum_fusion), channel_id=1, source_target_pairs={{0,3},{1,0},{2,1},{3,2},{4,7},{5,4},{6,5},{7,6},{8,11},{9,8},{10,9... | collective-permute-start | bytes 691208 | tf_op jit(solution)/shard_map/ppermute | solution.py:787
  46.7 106.5 %all-gather.7.cloned.1.call-start = ((), (), s32[]{:S(2)}) async-start(), calls=%async_computation.3 | async-start | bytes 8478720 | tf_op jit(solution)/shard_map/all_gather | solution.py:855
  49.1 32.0 %collective-permute-start.7 = (bf16[720,160]{1,0:T(8,128)(2,1)S(1)}, bf16[720,160]{1,0:T(8,128)(2,1)S(1)}, u32[]{:S(2)}, u32[]{:S(2)}) collective-permute-start(bf16[720,160]{1,0:T(8,128)(2,1)S(1)} %pad_maximum_fusion.1), channel_id=1, source_target_pairs={{0,1},{1,2},{2,3},{3,0},{4,5},{5,6},{6,7},{7,4},{8,9},{9,10},{10,1... | collective-permute-start | bytes 691208 | tf_op jit(solution)/shard_map/ppermute | solution.py:787
  49.1 31.2 %collective-permute-start.6 = (bf16[720,160]{1,0:T(8,128)(2,1)S(1)}, bf16[720,160]{1,0:T(8,128)(2,1)S(1)}, u32[]{:S(2)}, u32[]{:S(2)}) collective-permute-start(bf16[720,160]{1,0:T(8,128)(2,1)S(1)} %pad_maximum_fusion.1), channel_id=1, source_target_pairs={{0,2},{1,3},{2,0},{3,1},{4,6},{5,7},{6,4},{7,5},{8,10},{9,11},{10,... | collective-permute-start | bytes 691208 | tf_op jit(solution)/shard_map/ppermute | solution.py:787
  101.3 185.9 %reduce-scatter.2.cloned.1.call-start = ((), (), s32[]{:S(2)}) async-start(), calls=%async_computation.1 | async-start | bytes 6451200 | tf_op jit(solution)/shard_map/reduce_scatter | solution.py:979
  163.9 18.1 %collective-permute-start.9 = (bf16[2,256,640]{2,1,0:T(8,128)(2,1)S(1)}, bf16[2,256,640]{2,1,0:T(8,128)(2,1)}, u32[]{:S(2)}, u32[]{:S(2)}) collective-permute-start(bf16[2,256,640]{2,1,0:T(8,128)(2,1)S(1)} %bitcast.126), channel_id=1, source_target_pairs={{1,0},{2,1},{3,2},{5,4},{6,5},{7,6},{9,8},{10,9},{11,10},{13,12},{... | collective-permute-start | bytes 1966088 | tf_op jit(solution)/shard_map/ppermute | solution.py:27
  166.0 17.8 %collective-permute-start.8 = (bf16[2,256,640]{2,1,0:T(8,128)(2,1)S(1)}, bf16[2,256,640]{2,1,0:T(8,128)(2,1)}, u32[]{:S(2)}, u32[]{:S(2)}) collective-permute-start(bf16[2,256,640]{2,1,0:T(8,128)(2,1)S(1)} %bitcast.127), channel_id=1, source_target_pairs={{0,1},{1,2},{2,3},{4,5},{5,6},{6,7},{8,9},{9,10},{10,11},{12,13},{... | collective-permute-start | bytes 1966088 | tf_op jit(solution)/shard_map/ppermute | solution.py:26
  201.0 16.8 %collective-permute-start.11 = (bf16[2,256,640]{2,1,0:T(8,128)(2,1)S(1)}, bf16[2,256,640]{2,1,0:T(8,128)(2,1)}, u32[]{:S(2)}, u32[]{:S(2)}) collective-permute-start(bf16[2,256,640]{2,1,0:T(8,128)(2,1)S(1)} %bitcast.118), channel_id=1, source_target_pairs={{1,0},{2,1},{3,2},{5,4},{6,5},{7,6},{9,8},{10,9},{11,10},{13,12},{... | collective-permute-start | bytes 1966088 | tf_op jit(solution)/shard_map/ppermute | solution.py:27
  203.2 16.6 %collective-permute-start.10 = (bf16[2,256,640]{2,1,0:T(8,128)(2,1)S(1)}, bf16[2,256,640]{2,1,0:T(8,128)(2,1)}, u32[]{:S(2)}, u32[]{:S(2)}) collective-permute-start(bf16[2,256,640]{2,1,0:T(8,128)(2,1)S(1)} %bitcast.119), channel_id=1, source_target_pairs={{0,1},{1,2},{2,3},{4,5},{5,6},{6,7},{8,9},{9,10},{10,11},{12,13},{... | collective-permute-start | bytes 1966088 | tf_op jit(solution)/shard_map/ppermute | solution.py:26
  242.3 16.5 %collective-permute-start.13 = (bf16[2,128,640]{2,1,0:T(8,128)(2,1)S(1)}, bf16[2,128,640]{2,1,0:T(8,128)(2,1)S(1)}, u32[]{:S(2)}, u32[]{:S(2)}) collective-permute-start(bf16[2,128,640]{2,1,0:T(8,128)(2,1)S(1)} %get-tuple-element.212), channel_id=1, source_target_pairs={{1,0},{2,1},{3,2},{5,4},{6,5},{7,6},{9,8},{10,9},{11,10},{13,12},{... | collective-permute-start | bytes 983048 | tf_op jit(solution)/shard_map/ppermute | solution.py:27
  244.5 14.3 %collective-permute-start.12 = (bf16[2,128,640]{2,1,0:T(8,128)(2,1)S(1)}, bf16[2,128,640]{2,1,0:T(8,128)(2,1)S(1)}, u32[]{:S(2)}, u32[]{:S(2)}) collective-permute-start(bf16[2,128,640]{2,1,0:T(8,128)(2,1)S(1)} %get-tuple-element.213), channel_id=1, source_target_pairs={{0,1},{1,2},{2,3},{4,5},{5,6},{6,7},{8,9},{9,10},{10,11},{12,13},{... | collective-permute-start | bytes 983048 | tf_op jit(solution)/shard_map/ppermute | solution.py:26
  258.8 20.9 %collective-permute-start.14 = (bf16[4,560,640]{2,1,0:T(8,128)(2,1)}, bf16[4,560,640]{2,1,0:T(8,128)(2,1)}, u32[]{:S(2)}, u32[]{:S(2)}) collective-permute-start(bf16[4,560,640]{2,1,0:T(8,128)(2,1)} %get-tuple-element.157), channel_id=1, source_target_pairs={{0,4},{4,0},{8,12},{12,8},{16,20},{20,16},{24,28},{28,24},{1,5},{5... | collective-permute-start | bytes 8601608 | tf_op jit(solution)/shard_map/ppermute | solution.py:769
  285.6 28.0 %collective-permute-start.18 = (bf16[2,464,640]{2,1,0:T(8,128)(2,1)}, bf16[2,464,640]{2,1,0:T(8,128)(2,1)}, u32[]{:S(2)}, u32[]{:S(2)}) collective-permute-start(bf16[2,464,640]{2,1,0:T(8,128)(2,1)} %get-tuple-element.169), channel_id=1, source_target_pairs={{0,16},{4,20},{8,24},{12,28},{16,0},{20,4},{24,8},{28,12},{1,17},{... | collective-permute-start | bytes 3563528 | tf_op jit(solution)/shard_map/ppermute | solution.py:769
  286.5 26.8 %collective-permute-start.17 = (bf16[2,448,640]{2,1,0:T(8,128)(2,1)}, bf16[2,448,640]{2,1,0:T(8,128)(2,1)S(1)}, u32[]{:S(2)}, u32[]{:S(2)}) collective-permute-start(bf16[2,448,640]{2,1,0:T(8,128)(2,1)} %get-tuple-element.167), channel_id=1, source_target_pairs={{0,8},{4,12},{8,0},{12,4},{16,24},{20,28},{24,16},{28,20},{1,9},{5... | collective-permute-start | bytes 3440648 | tf_op jit(solution)/shard_map/ppermute | solution.py:769
  289.3 24.3 %collective-permute-start.21 = (bf16[560,160]{1,0:T(8,128)(2,1)S(1)}, bf16[560,160]{1,0:T(8,128)(2,1)S(1)}, u32[]{:S(2)}, u32[]{:S(2)}) collective-permute-start(bf16[560,160]{1,0:T(8,128)(2,1)S(1)} %get-tuple-element.208), channel_id=1, source_target_pairs={{0,3},{1,0},{2,1},{3,2},{4,7},{5,4},{6,5},{7,6},{8,11},{9,8},{10,9... | collective-permute-start | bytes 537608 | tf_op jit(solution)/shard_map/ppermute | solution.py:787
  289.4 24.2 %collective-permute-start.20 = (bf16[560,160]{1,0:T(8,128)(2,1)S(1)}, bf16[560,160]{1,0:T(8,128)(2,1)S(1)}, u32[]{:S(2)}, u32[]{:S(2)}) collective-permute-start(bf16[560,160]{1,0:T(8,128)(2,1)S(1)} %get-tuple-element.209), channel_id=1, source_target_pairs={{0,2},{1,3},{2,0},{3,1},{4,6},{5,7},{6,4},{7,5},{8,10},{9,11},{10,... | collective-permute-start | bytes 537608 | tf_op jit(solution)/shard_map/ppermute | solution.py:787
  290.7 25.8 %collective-permute-start.19 = (bf16[560,160]{1,0:T(8,128)(2,1)S(1)}, bf16[560,160]{1,0:T(8,128)(2,1)S(1)}, u32[]{:S(2)}, u32[]{:S(2)}) collective-permute-start(bf16[560,160]{1,0:T(8,128)(2,1)S(1)} %get-tuple-element.210), channel_id=1, source_target_pairs={{0,1},{1,2},{2,3},{3,0},{4,5},{5,6},{6,7},{7,4},{8,9},{9,10},{10,1... | collective-permute-start | bytes 537608 | tf_op jit(solution)/shard_map/ppermute | solution.py:787
  318.3 14.6 %collective-permute-start.23 = (bf16[464,640]{1,0:T(8,128)(2,1)S(1)}, bf16[464,640]{1,0:T(8,128)(2,1)S(1)}, u32[]{:S(2)}, u32[]{:S(2)}) collective-permute-start(bf16[464,640]{1,0:T(8,128)(2,1)S(1)} %get-tuple-element.179), channel_id=1, source_target_pairs={{0,8},{4,12},{8,0},{12,4},{16,24},{20,28},{24,16},{28,20},{1,9},{5... | collective-permute-start | bytes 1781768 | tf_op jit(solution)/shard_map/ppermute | solution.py:769
  319.0 13.7 %collective-permute-start.22 = (bf16[448,640]{1,0:T(8,128)(2,1)S(1)}, bf16[448,640]{1,0:T(8,128)(2,1)S(1)}, u32[]{:S(2)}, u32[]{:S(2)}) collective-permute-start(bf16[448,640]{1,0:T(8,128)(2,1)S(1)} %get-tuple-element.177), channel_id=1, source_target_pairs={{0,16},{4,20},{8,24},{12,28},{16,0},{20,4},{24,8},{28,12},{1,17},{... | collective-permute-start | bytes 1720328 | tf_op jit(solution)/shard_map/ppermute | solution.py:769
  334.2 38.7 %collective-permute-start.25 = (bf16[912,160]{1,0:T(8,128)(2,1)S(1)}, bf16[912,160]{1,0:T(8,128)(2,1)S(1)}, u32[]{:S(2)}, u32[]{:S(2)}) collective-permute-start(bf16[912,160]{1,0:T(8,128)(2,1)S(1)} %get-tuple-element.205), channel_id=1, source_target_pairs={{0,2},{1,3},{2,0},{3,1},{4,6},{5,7},{6,4},{7,5},{8,10},{9,11},{10,... | collective-permute-start | bytes 875528 | tf_op jit(solution)/shard_map/ppermute | solution.py:787
  334.3 40.1 %collective-permute-start.24 = (bf16[912,160]{1,0:T(8,128)(2,1)S(1)}, bf16[912,160]{1,0:T(8,128)(2,1)S(1)}, u32[]{:S(2)}, u32[]{:S(2)}) collective-permute-start(bf16[912,160]{1,0:T(8,128)(2,1)S(1)} %get-tuple-element.206), channel_id=1, source_target_pairs={{0,1},{1,2},{2,3},{3,0},{4,5},{5,6},{6,7},{7,4},{8,9},{9,10},{10,1... | collective-permute-start | bytes 875528 | tf_op jit(solution)/shard_map/ppermute | solution.py:787
  (46 other events, 383.3 us)
Sparse Core Ops, SparseCore 0:
  46.8 53.0 all-gather.4
  102.4 50.7 all-gather.6
  219.9 64.4 reduce-scatter.1
where the time goes:
time: 388 us; the launch traced here: 382 us
  waiting for transfers between devices  182 us (47%)
  Pallas kernels  96 us (25%)
  local copies, waits for them, and re-layouts  43.4 us (11%)
  starting transfers between devices  38.9 us (10%)
  between operations  14.8 us (4%)
  other arithmetic  6.98 us (2%)
    ppermute x12, waiting for transfers between devices, shifted(): lax.ppermute(block, 'seq', [(i, (i + step) % count) for i in range(count)])  92.8 us
    ppermute x7, waiting for transfers between devices, dp_swapped(): return lax.ppermute(block, 'dp', [(i, i ^ 1 << bit) for i in range(count)])  39.3 us
    all_gather x2, waiting for transfers between devices, gathered_params(): whole = lax.all_gather(packed, 'dp')  27.4 us
    pallas_call x2, Pallas kernels, conv_back_with(): call(functools.partial(conv_back_kernel, dilation_step), rows, [row_block...  25.1 us
    unnamed x92, local copies, waits for them, and re-layouts  20.6 us
    pallas_call x2, Pallas kernels, convolve(): call(functools.partial(convolve_kernel, dilation_step), rows, [row_block(...  18.9 us
    ppermute x4, waiting for transfers between devices, seq_neighbours(): high = lax.ppermute(block[:, :width], 'seq', backward)  17.3 us
    ppermute x4, starting transfers between devices, seq_neighbours(): low = lax.ppermute(block[:, block.shape[1] - width:], 'seq', forward)  14.8 us
  transfers between devices with their start and end apart: 30, of which 20 were waited for; matrix products, arithmetic and copies ran while one was open for 7% of the time, Pallas kernels for 19%

commit v1 on v0

--- a/solution.py
+++ b/solution.py
@@ -347,6 +347,22 @@
         send[...] = plus(keep[1], got[1]).astype(jnp.bfloat16)
 
 
+def lane_packed(rows, depth, count):
+    missing = count * depth - rows.shape[0]
+    if missing:
+        rows = jnp.concatenate([rows, jnp.zeros((missing, rows.shape[1]), rows.dtype)], axis=0)
+    return jnp.concatenate([rows[i * depth : (i + 1) * depth] for i in range(count)], axis=1)
+
+
+def lane_unpacked(packed, count):
+    width = packed.shape[1] // count
+    return jnp.concatenate([packed[:, i * width : (i + 1) * width] for i in range(count)], axis=0)
+
+
+def packed_depth(rows, count):
+    return -(-rows // (16 * count)) * 16
+
+
 def seq_split_kernel(folded_rows, vector_rows, place_ref, *refs):
     *in_refs, out_ref = refs
     if len(in_refs) == 1:
@@ -355,7 +371,8 @@
         halves = [plus(in_refs[i][...], in_refs[i + 1][...]) for i in range(0, len(in_refs), 2)]
         total = jnp.concatenate(halves, axis=0)
     total = total.astype(jnp.float32)
-    count, rows, width = out_ref.shape
+    count, width = out_ref.shape[0], total.shape[1] // out_ref.shape[0]
+    rows = total.shape[0]
     at, end = folded_rows
     fold = (end - at) // 2
     for s in range(count):
@@ -370,7 +387,8 @@
             columns = jnp.concatenate(
                 [columns[: rows - vector_rows], total[rows - vector_rows :, :width]], axis=0
             )
-        out_ref[(s - place_ref[1] + count) % count] = columns.astype(jnp.bfloat16)
+        packed = lane_packed(columns, out_ref.shape[1], count)
+        out_ref[(s - place_ref[1] + count) % count] = packed.astype(jnp.bfloat16)
 
 
 def last_sum_kernel(layout, *refs):
@@ -379,7 +397,7 @@
     for name, count in layout:
         own, one, two, three = (ref[...].astype(jnp.float32) for ref in refs[at : at + 4])
         at += 4
-        sums[name] = (own + two) + (one + three)
+        sums[name] = lane_unpacked((own + two) + (one + three), 4)
     first_ref, taps_ref, last_ref = refs[at : at + 3]
     vector_refs = refs[at + 3 :]
     depth = taps_ref.shape[2]
@@ -402,6 +420,72 @@
             ref[block : block + 1, :] = row[:, : ref.shape[1]]
 
 
+def main_pack_kernel(w_conv, w_out, early_ref, late_ref):
+    width = w_conv.shape[3]
+    count = early_ref.shape[1] // width
+    for block, ref in ((0, early_ref), (1, late_ref)):
+        rows = [w_conv[block, k] for k in range(KER)]
+        rows += [w_out[block][:, :width], w_out[block][:, width:]]
+        ref[...] = lane_packed(jnp.concatenate(rows, axis=0), ref.shape[0], count)
+
+
+def lead_pack_kernel(w_in, wide, narrow, lead_ref, vector_ref):
+    count = lead_ref.shape[1] // w_in.shape[2]
+    lead = jnp.concatenate([w_in[0], w_in[1]], axis=0)
+    lead_ref[...] = lane_packed(lead, lead_ref.shape[0], count)
+    hidden = vector_ref.shape[1]
+    for block in range(2):
+        rows = []
+        for ref in (wide, narrow):
+            part = ref[block].astype(jnp.float32)
+            rows.append(
+                jnp.concatenate(
+                    [part, jnp.zeros((part.shape[0], hidden - part.shape[1]), jnp.float32)], axis=1
+                )
+            )
+        rows.append(jnp.zeros((VECTOR_ROWS - 9, hidden), jnp.float32))
+        start = block * VECTOR_ROWS
+        vector_ref[start : start + VECTOR_ROWS, :] = jnp.concatenate(rows, axis=0).astype(
+            jnp.bfloat16
+        )
+
+
+def seq_join_kernel(folded_rows, vector_rows, place_ref, *refs):
+    *in_refs, out_ref, hold_ref = refs
+    vector_in = in_refs.pop() if vector_rows else None
+    count = len(in_refs)
+    for step, ref in enumerate(in_refs):
+        hold_ref[(place_ref[1] - step + count) % count] = ref[...]
+    shares = [lane_unpacked(hold_ref[s], count) for s in range(count)]
+    rows = out_ref.shape[0] - vector_rows
+    at, end = folded_rows
+    if at:
+        out_ref[:at, :] = jnp.concatenate([share[:at] for share in shares], axis=1)
+    if end > at:
+        fold = (end - at) // 2
+        for half in range(2):
+            columns = []
+            for share in shares[half * count // 2 : (half + 1) * count // 2]:
+                columns += [share[at : at + fold], share[at + fold : end]]
+            start = at + half * fold
+            out_ref[start : start + fold, :] = jnp.concatenate(columns, axis=1)
+    if vector_in is not None:
+        out_ref[rows:, :] = vector_in[...]
+
+
+def place_kernel(place_ref, *refs):
+    *in_refs, out_ref = refs
+    chip, core = place_ref[0] // 2, place_ref[0] % 2
+    cut = in_refs[0].shape[1]
+    for at, share_core in ((0, core), (4, 1 - core)):
+        near_a, far_a, near_b, far_b = in_refs[at : at + 4]
+        for i in range(2):
+            out_ref[2 * (chip ^ i) + share_core, :cut] = near_a[i]
+            out_ref[2 * (chip ^ (2 + i)) + share_core, :cut] = far_a[i]
+            out_ref[2 * (chip ^ (2 * i)) + share_core, cut:] = near_b[i]
+            out_ref[2 * (chip ^ (2 * i + 1)) + share_core, cut:] = far_b[i]
+
+
 def tiled(rows, columns):
     return pl.BlockSpec((rows, columns), lambda i: (i, 0))
 
@@ -432,13 +516,40 @@
         scratch_shapes=list(scratch),
         input_output_aliases=aliases or {},
         cost_estimate=cost(flops, moved),
-        compiler_params=pltpu.CompilerParams(vmem_limit_bytes=48 * 1024 * 1024),
+        compiler_params=pltpu.CompilerParams(vmem_limit_bytes=32 * 1024 * 1024),
         name=name,
     )
 
 
 def shape_of(shape, dtype):
     return jax.ShapeDtypeStruct(shape, dtype)
+
+
+class Weights:
+    def __init__(self, first, taps, last, wide, narrow):
+        self.first, self.taps, self.last = first, taps, last
+        self.wide, self.narrow = wide, narrow
+        self.model, self.hidden = wide.shape[1], narrow.shape[1]
+
+    def first_spec(self):
+        array, index = self.first
+        return pack_block(array.shape[0], self.model // array.shape[0], self.hidden, index)
+
+    def specs(self, units):
+        return [
+            pack_block(array.shape[0], self.hidden // array.shape[0], self.hidden, index)
+            for array, index in units
+        ]
+
+
+def arrays(units):
+    return [array for array, _ in units]
+
+
+def pack_weights(pack, wide, narrow):
+    folds = wide.shape[1] // narrow.shape[1]
+    units = [(pack, folds + i) for i in range(KER + folds)]
+    return Weights((pack, 0), units[:KER], units[KER:], wide, narrow)
 
 
 class Sizes:
@@ -449,34 +560,19 @@
         self.middle_rows = hidden // self.parts
         self.folds = model // hidden
         self.conv_at = self.first_rows // self.middle_rows
-        self.out_at = self.conv_at + KER
 
     def first(self):
         return pack_block(self.parts, self.first_rows, self.hidden, 0)
 
-    def taps(self):
-        return [
-            pack_block(self.parts, self.middle_rows, self.hidden, self.conv_at + k)
-            for k in range(KER)
-        ]
-
-    def last(self):
-        return [
-            pack_block(self.parts, self.middle_rows, self.hidden, self.out_at + i)
-            for i in range(self.folds)
-        ]
-
 
 def project(inputs, weights):
-    pack, wide, narrow = weights
     tokens, model = inputs.shape
-    hidden = narrow.shape[1]
-    sizes = Sizes(pack, model, hidden)
+    hidden = weights.hidden
     tile = min(128, tokens)
     return call(
         project_kernel,
         tokens // tile,
-        [tiled(tile, model), sizes.first(), fixed(3, model), fixed(6, hidden)],
+        [tiled(tile, model), weights.first_spec(), fixed(3, model), fixed(6, hidden)],
         [tiled(tile, model), tiled(tile, hidden), tiled(tile, hidden)],
         [
             shape_of((tokens, model), jnp.bfloat16),
@@ -486,14 +582,12 @@
         4 * tokens * model * hidden,
         12 * tokens * model,
         "project",
-    )(inputs, pack, wide, narrow)
+    )(inputs, weights.first[0], weights.wide, weights.narrow)
 
 
 def convolve(act_two, flags, inputs, weights, dilation_step, next_dtype):
-    pack, wide, narrow = weights
     rows, length, hidden = act_two.shape
     tokens, model = inputs.shape
-    sizes = Sizes(pack, model, hidden)
     low, high = seq_neighbours(act_two, KER // 2 * dilation_step)
     return call(
         functools.partial(convolve_kernel, dilation_step),
@@ -504,8 +598,7 @@
             row_block(high.shape),
             row_block(flags.shape),
             tiled(length, model),
-            *sizes.taps(),
-            *sizes.last(),
+            *weights.specs(weights.taps + weights.last),
             fixed(3, model),
             fixed(6, hidden),
         ],
@@ -524,19 +617,31 @@
         2 * tokens * hidden * (KER * hidden + model),
         16 * tokens * model,
         "convolve",
-    )(low, act_two, high, flags, inputs, *([pack] * (KER + 2)), wide, narrow)
+    )(
+        low,
+        act_two,
+        high,
+        flags,
+        inputs,
+        *arrays(weights.taps + weights.last),
+        weights.wide,
+        weights.narrow,
+    )
 
 
 def out_back(upstream, conv_out, weights):
-    pack, wide, narrow = weights
     tokens, model = upstream.shape
-    hidden = narrow.shape[1]
-    sizes = Sizes(pack, model, hidden)
+    hidden = weights.hidden
     tile = min(128, tokens)
     return call(
         out_back_kernel,
         tokens // tile,
-        [tiled(tile, model), tiled(tile, hidden), *sizes.last(), fixed(6, hidden)],
+        [
+            tiled(tile, model),
+            tiled(tile, hidden),
+            *weights.specs(weights.last),
+            fixed(6, hidden),
+        ],
         [tiled(tile, model), tiled(tile, hidden), fixed(8, hidden), fixed(8, model)],
         [
             shape_of((tokens, model), jnp.bfloat16),
@@ -547,7 +652,7 @@
         4 * tokens * model * hidden,
         10 * tokens * model,
         "out_back",
-    )(upstream, conv_out, pack, pack, narrow)
+    )(upstream, conv_out, *arrays(weights.last), weights.narrow)
 
 
 def weight_grads(tap_rows, gv, act_three, short, pack, conv_at=None):
@@ -581,10 +686,8 @@
 
 
 def conv_back_with(low, gv, high, flags, u, inputs, upstream, weights, dilation_step):
-    pack, wide, narrow = weights
     rows, length, hidden = gv.shape
     tokens, model = inputs.shape
-    sizes = Sizes(pack, model, hidden)
     return call(
         functools.partial(conv_back_kernel, dilation_step),
         rows,
@@ -596,8 +699,8 @@
             tiled(length, hidden),
             tiled(length, model),
             tiled(length, model),
-            *sizes.taps(),
-            sizes.first(),
+            *weights.specs(weights.taps),
+            weights.first_spec(),
             fixed(3, model),
             fixed(6, hidden),
         ],
@@ -611,7 +714,19 @@
         2 * tokens * hidden * (KER * hidden + model),
         16 * tokens * model,
         "conv_back",
-    )(low, gv, high, flags, u, inputs, upstream, *([pack] * (KER + 1)), wide, narrow)
+    )(
+        low,
+        gv,
+        high,
+        flags,
+        u,
+        inputs,
+        upstream,
+        *arrays(weights.taps),
+        weights.first[0],
+        weights.wide,
+        weights.narrow,
+    )
 
 
 def in_grads(grad_pack, act_one, gu):
@@ -731,16 +846,16 @@
 def seq_split(where, folded_rows, vector_rows, *ins):
     count = lax.axis_size("seq")
     rows = sum(array.shape[0] for array in ins[:: 2 if len(ins) > 1 else 1])
-    width = ins[0].shape[1] // count
-    shape = (count, rows, width)
+    hidden = ins[0].shape[1]
+    shape = (count, packed_depth(rows, count), hidden)
     return call(
         functools.partial(seq_split_kernel, folded_rows, vector_rows),
         1,
         [scalars()] + [fixed(*array.shape) for array in ins],
         fixed(*shape),
         shape_of(shape, jnp.bfloat16),
-        rows * width * count,
-        6 * rows * width * count,
+        rows * hidden,
+        6 * rows * hidden,
         "seq_split",
     )(where, *ins)
 
@@ -862,7 +977,7 @@
         whole = jnp.concatenate(
             [whole[:, a:b].reshape(1, -1, hidden) for a, b in zip(bounds, bounds[1:])], axis=1
         )
-    return (whole, wide, narrow)
+    return pack_weights(whole, wide, narrow)
 
 
 def reduce_dp(grad_pack, wide_grads, narrow_grads):
@@ -943,7 +1058,7 @@
     act_one, u, tap_rows, conv_out, act_three = kept
     rows, length, _ = flags.shape
     short, gv, narrow_a, wide_a = out_back(upstream, conv_out, weights)
-    pack = weights[0]
+    pack = weights.first[0]
     grad_shape = shape_of(
         (pack.shape[0], sum(pack_rows(pack, inputs.shape[1], gv.shape[1])), gv.shape[1]),
         jnp.bfloat16,
@@ -960,10 +1075,132 @@
     return result, reduce_dp(grad_pack, wide, narrow), before
 
 
+def main_pack(w_conv, w_out):
+    count = lax.axis_size("seq")
+    depth, width = w_conv.shape[2:]
+    rows = packed_depth((KER + w_out.shape[2] // width) * depth, count)
+    out = shape_of((rows, width * count), jnp.bfloat16)
+    return call(
+        main_pack_kernel,
+        1,
+        [fixed(*w_conv.shape), fixed(*w_out.shape)],
+        [fixed(*out.shape)] * 2,
+        [out, out],
+        out.size,
+        8 * out.size,
+        "main_pack",
+    )(w_conv, w_out)
+
+
+def lead_pack(w_in, wide, narrow):
+    count = lax.axis_size("seq")
+    hidden = w_in.shape[2] * count
+    ins = (w_in, jnp.stack(wide, axis=1), jnp.stack(narrow, axis=1))
+    rows = packed_depth(2 * w_in.shape[1], count)
+    outs = [shape_of((n, hidden), jnp.bfloat16) for n in (rows, 2 * VECTOR_ROWS)]
+    return call(
+        lead_pack_kernel,
+        1,
+        [fixed(*array.shape) for array in ins],
+        [fixed(*out.shape) for out in outs],
+        outs,
+        rows * hidden,
+        8 * rows * hidden,
+        "lead_pack",
+    )(*ins)
+
+
+def seq_shares(packed):
+    return [packed] + [shifted(packed, step) for step in range(1, lax.axis_size("seq"))]
+
+
+def seq_join(where, folded_rows, held, vectors=None):
+    count = len(held)
+    packed = held[0]
+    extra = [] if vectors is None else [vectors]
+    vector_rows = 0 if vectors is None else vectors.shape[0]
+    rows = folded_rows[1] + vector_rows
+    hidden = packed.shape[1]
+    return call(
+        functools.partial(seq_join_kernel, folded_rows, vector_rows),
+        1,
+        [scalars()] + [fixed(*array.shape) for array in held + extra],
+        fixed(rows, hidden),
+        shape_of((rows, hidden), jnp.bfloat16),
+        rows * hidden,
+        4 * rows * hidden,
+        "seq_join",
+        scratch=[pltpu.VMEM((count,) + packed.shape, jnp.bfloat16)],
+    )(where, *held, *extra)
+
+
+class Exchange:
+    def __init__(self, block):
+        self.block = block
+        self.cut = block.shape[0] // 32 * 16
+        a, b = block[: self.cut], block[self.cut :]
+        got_a, got_b = lax.optimization_barrier((dp_swapped(a, 1), dp_swapped(b, 2)))
+        self.near = (jnp.stack([a, got_a]), jnp.stack([b, got_b]))
+
+    def finish(self, where, beside):
+        rows, hidden = self.block.shape
+        near_a, near_b = self.near
+        far_a, far_b, *beside = lax.optimization_barrier(
+            (dp_swapped(near_a, 2), dp_swapped(near_b, 1), *beside)
+        )
+        near = (near_a, far_a, near_b, far_b)
+        ins = near + tuple(dp_swapped(share, 0) for share in near)
+        parts = lax.axis_size("dp")
+        return call(
+            place_kernel,
+            1,
+            [scalars()] + [fixed(*array.shape) for array in ins],
+            fixed(parts, rows, hidden),
+            shape_of((parts, rows, hidden), jnp.bfloat16),
+            parts * rows * hidden,
+            4 * parts * rows * hidden,
+            "place",
+        )(where, *ins), beside
+
+
+def after(value, *earlier):
+    return lax.optimization_barrier((value, *earlier))[0]
+
+
+def exchanged_weights(where, shards):
+    w_in, w_conv, w_out = shards[2], shards[6], shards[10]
+    first_rows = w_in.shape[1]
+    depth, width = w_conv.shape[2:]
+    folds = w_out.shape[2] // width
+    folded = (KER * depth, (KER + folds) * depth)
+    plain = (2 * first_rows, 2 * first_rows)
+    early, late = main_pack(w_conv, w_out)
+    wide = [shards[i] for i in (0, 1, 11)]
+    lead, vectors = lead_pack(w_in, wide, [shards[i] for i in (3, 4, 5, 7, 8, 9)])
+
+    early = seq_join(where, folded, seq_shares(early))
+    early_whole = lax.all_gather(early, "dp")
+    exchange = Exchange(seq_join(where, plain, seq_shares(after(lead, early)), vectors))
+    late = seq_shares(after(late, *exchange.near))
+    lead, late = exchange.finish(where, late)
+    late = seq_join(where, folded, late)
+    late_whole = lax.all_gather(after(late, early_whole), "dp")
+
+    tail = lead[:, 2 * first_rows :].astype(jnp.float32)
+    out = []
+    for block, whole in ((0, early_whole), (1, late_whole)):
+        start = block * VECTOR_ROWS
+        wide = tail[:, start : start + 3, :first_rows].transpose(1, 0, 2).reshape(3, -1)
+        narrow = tail[:, start + 3 : start + 9, :depth].transpose(1, 0, 2).reshape(6, -1)
+        units = [(whole, i) for i in range(KER + folds)]
+        out.append(Weights((lead, block), units[:KER], units[KER:], wide, narrow))
+    return out
+
+
 def exchanged_backward(inputs, weights, kept, flags, dilations, cotangent, out_shapes):
     where = place()
     parts = lax.axis_size("dp")
-    hidden = weights[1][2].shape[1]
+    hidden = weights[1].hidden
     model = inputs[0].shape[1]
     depth = hidden // parts
     folded = (KER * depth, (KER + model // hidden) * depth)
@@ -1069,18 +1306,22 @@
     token_positions = lax.axis_index("seq") * seq_len + jnp.arange(seq_len, dtype=jnp.int32)
     early_flags = kernel_tap_flags(protein_lengths, token_positions, FIRST_DILATION)
     later_flags = kernel_tap_flags(protein_lengths, token_positions, SECOND_DILATION)
-    early_weights = gathered_params(0, device_shards)
-    late_weights = gathered_params(1, device_shards, early_weights[0])
+    parts = lax.axis_size("dp")
+    fast = parts == 8 and pack_is_aligned(in_bias.shape[1])
+    if fast:
+        early_weights, late_weights = exchanged_weights(place(), device_shards)
+    else:
+        early_weights = gathered_params(0, device_shards)
+        late_weights = gathered_params(1, device_shards, early_weights.first[0])
     flat_tokens = tokens.reshape(rows * seq_len, model)
     middle, early_kept = block_forward(
         flat_tokens, early_weights, early_flags, FIRST_DILATION, jnp.float32
     )
-    middle, late_weights = lax.optimization_barrier((middle, late_weights))
     output, late_kept = block_forward(
         middle, late_weights, later_flags, SECOND_DILATION, jnp.bfloat16
     )
-    hidden = early_weights[2].shape[1]
-    if lax.axis_size("dp") == 8 and pack_is_aligned(hidden // 8):
+    hidden = early_weights.hidden
+    if fast:
         shapes = [w.shape for w in (w_in, w_conv, w_out, norm1_gain, norm1_bias, out_bias)]
         shapes += [w.shape for w in (in_bias, norm2_gain, norm2_bias)]
         shapes += [w.shape for w in (conv_bias, norm3_gain, norm3_bias)]

time: 388 us -> 335 us (0.86)
  waiting for transfers between devices: 182 us -> 139 us
  Pallas kernels: 96 us -> 81.2 us
  starting transfers between devices: 38.9 us -> 50 us
  other arithmetic: 6.98 us -> 2.8 us
    ppermute x12 -> x15, waiting for transfers between devices: 92.8 us -> 67.3 us  [shifted(): lax.ppermute(block, 'seq', [(i, (i + step) % count) for i in range(count)])]
    all_gather x2, waiting for transfers between devices: 27.4 us -> 8.16 us  [the longest x1 8.16 us: exchanged_weights(): early_whole = lax.all_gather(early, 'dp')]
    unnamed x92 -> x142, local copies, waits for them, and re-layouts: 20.6 us -> 35.8 us
    ppermute x4, waiting for transfers between devices: 17.3 us -> 11 us  [seq_neighbours(): high = lax.ppermute(block[:, :width], 'seq', backward)]
    squeeze x8 -> x0, local copies, waits for them, and re-layouts: 6.22 us -> none  [the longest x6 4.41 us: vector_pack(): rows = [device_shards[i][block_number] for i in order]]
    ppermute x12 -> x15, starting transfers between devices: 9.14 us -> 15.1 us  [shifted(): lax.ppermute(block, 'seq', [(i, (i + step) % count) for i in range(count)])]
    pallas_call x2, Pallas kernels: 25.1 us -> 19.2 us  [conv_back_with(): call(functools.partial(conv_back_kernel, dilation_step), rows, [row_block...]
    pallas_call x2, Pallas kernels: 18.9 us -> 13.5 us  [convolve(): call(functools.partial(convolve_kernel, dilation_step), rows, [row_block(...]
  transfers between devices with their start and end apart: 30 -> 41, of which waited for: 20 -> 28; matrix products, arithmetic and copies ran while one was open for 7% -> 3% of each run, Pallas kernels for 19% -> 19%
where the time goes in v1:
time: 335 us; the launch traced here: 332 us
  waiting for transfers between devices  139 us (41%)
  Pallas kernels  81.2 us (24%)
  starting transfers between devices  50 us (15%)
  local copies, waits for them, and re-layouts  44.4 us (13%)
  between operations  14.7 us (4%)
    ppermute x15, waiting for transfers between devices, shifted(): lax.ppermute(block, 'seq', [(i, (i + step) % count) for i in range(count)])  67.3 us
    ppermute x15, waiting for transfers between devices, dp_swapped(): return lax.ppermute(block, 'dp', [(i, i ^ 1 << bit) for i in range(count)])  44.4 us
    unnamed x142, local copies, waits for them, and re-layouts  35.8 us
    pallas_call x2, Pallas kernels, conv_back_with(): call(functools.partial(conv_back_kernel, dilation_step), rows, [row_block...  19.2 us
    ppermute x4, starting transfers between devices, seq_neighbours(): low = lax.ppermute(block[:, block.shape[1] - width:], 'seq', forward)  15.5 us
    ppermute x15, starting transfers between devices, shifted(): lax.ppermute(block, 'seq', [(i, (i + step) % count) for i in range(count)])  15.1 us
    pallas_call x2, Pallas kernels, convolve(): call(functools.partial(convolve_kernel, dilation_step), rows, [row_block(...  13.5 us
    ppermute x15, starting transfers between devices, dp_swapped(): return lax.ppermute(block, 'dp', [(i, i ^ 1 << bit) for i in range(count)])  11.5 us
  transfers between devices with their start and end apart: 41, of which 28 were waited for; matrix products, arithmetic and copies ran while one was open for 3% of the time, Pallas kernels for 19%

profile of v1, /device:TPU:17, one launch (start us, length us, event | category | flops | bytes accessed | tf_op | source)
XLA Modules:
  0.0 331.8 jit_solution(40177950344749276)
XLA Ops:
  15.0 10.3 %collective-permute-done.1.refs_2_ = bf16[144,640]{1,0:T(8,128)(2,1)S(1)} collective-permute-done((bf16[144,640]{1,0:T(8,128)(2,1)S(1)}, bf16[144,640]{1,0:T(8,128)(2,1)S(1)}, u32[]{:S(2)}, u32[]{:S(2)}) %collective-permute-start.1) | collective-permute-done | bytes 184352 | tf_op jit(solution)/shard_map/ppermute | solution.py:902
  36.0 5.4 %collective-permute-done.3.refs_1_ = bf16[80,640]{1,0:T(8,128)(2,1)S(1)} collective-permute-done((bf16[80,640]{1,0:T(8,128)(2,1)S(1)}, bf16[80,640]{1,0:T(8,128)(2,1)S(1)}, u32[]{:S(2)}, u32[]{:S(2)}) %collective-permute-start.3) | collective-permute-done | bytes 102432 | tf_op jit(solution)/shard_map/ppermute | solution.py:902
  44.9 9.3 %collective-permute-done.7 = bf16[176,640]{1,0:T(8,128)(2,1)S(1)} collective-permute-done((bf16[176,640]{1,0:T(8,128)(2,1)S(1)}, bf16[176,640]{1,0:T(8,128)(2,1)S(1)}, u32[]{:S(2)}, u32[]{:S(2)}) %collective-permute-start.7) | collective-permute-done | bytes 225312 | tf_op jit(solution)/shard_map/ppermute | solution.py:884
  60.7 9.9 %collective-permute-done.11.refs_2_ = bf16[144,640]{1,0:T(8,128)(2,1)S(1)} collective-permute-done((bf16[144,640]{1,0:T(8,128)(2,1)S(1)}, bf16[144,640]{1,0:T(8,128)(2,1)S(1)}, u32[]{:S(2)}, u32[]{:S(2)}) %collective-permute-start.11) | collective-permute-done | bytes 184352 | tf_op jit(solution)/shard_map/ppermute | solution.py:902
  70.7 4.6 %collective-permute-done.10.refs_1_ = bf16[144,640]{1,0:T(8,128)(2,1)S(1)} collective-permute-done((bf16[144,640]{1,0:T(8,128)(2,1)S(1)}, bf16[144,640]{1,0:T(8,128)(2,1)S(1)}, u32[]{:S(2)}, u32[]{:S(2)}) %collective-permute-start.10) | collective-permute-done | bytes 184352 | tf_op jit(solution)/shard_map/ppermute | solution.py:902
  77.3 8.2 %all-gather.5.cloned.1.call-done = bf16[4480,640]{1,0:T(8,128)(2,1)} async-done(((bf16[560,640]{1,0:T(8,128)(2,1)}), bf16[4480,640]{1,0:T(8,128)(2,1)}) %all-gather.5.cloned.1.call-update) | async-done | bytes 5734416 | tf_op jit(solution)/shard_map/all_gather | solution.py:1182
  96.3 4.3 %project.2 = (bf16[512,1280]{1,0:T(8,128)(2,1)S(1)}, f32[512,640]{1,0:T(8,128)S(1)}, bf16[512,640]{1,0:T(8,128)(2,1)S(1)}) custom-call(bf16[512,1280]{1,0:T(8,128)(2,1)S(1)} %bitcast.86, bf16[8,352,640]{2,1,0:T(8,128)(2,1)S(1)} %copy-done.5, f32[3,1280]{1,0:T(4,128)S(1)} %reshape.816.wide_ref, f32[6,640]{1,0:T(8,128)S(1)} %reshape.817.narrow_ref), custom_call_target="tpu_custom_call" | custom-call | flops 1677721600 | bytes 7864320 | tf_op jit(solution)/shard_map/project/pallas_call | solution.py:572
  122.3 6.0 %convolve.2 = (bf16[512,3200]{1,0:T(8,128)(2,1)S(1)}, f32[512,640]{1,0:T(8,128)S(1)}, bf16[512,640]{1,0:T(8,128)(2,1)S(1)}, f32[512,1280]{1,0:T(8,128)S(1)}) custom-call(bf16[2,128,640]{2,1,0:T(8,128)(2,1)S(1)} %copy-done.31, bf16[2,256,640]{2,1,0:T(8,128)(2,1)S(1)} %bitcast.93, bf16[2,128,640]{2,1,0:T(8,128)(2,1)S(1)} %copy-done.29, ...), custom_call_target="tpu_custom_call" | custom-call | flops 2936012800 | bytes 10485760 | tf_op jit(solution)/shard_map/convolve/pallas_call | solution.py:592
  128.4 4.2 %project.3 = (bf16[512,1280]{1,0:T(8,128)(2,1)S(1)}, f32[512,640]{1,0:T(8,128)S(1)}, bf16[512,640]{1,0:T(8,128)(2,1)S(1)}) custom-call(f32[512,1280]{1,0:T(8,128)S(1)} %get-tuple-element.126.x_ref, bf16[8,352,640]{2,1,0:T(8,128)(2,1)S(1)} %copy-done.6, f32[3,1280]{1,0:T(4,128)S(1)} %reshape.819.wide_ref, f32[6,640]{1,0:T(8,128)S(1)} %reshape.820.narrow_ref), custom_call_target="tpu_custom_call" | custom-call | flops 1677721600 | bytes 7864320 | tf_op jit(solution)/shard_map/project/pallas_call | solution.py:572
  136.7 4.4 %collective-permute-start.19 = (bf16[2,256,640]{2,1,0:T(8,128)(2,1)S(1)}, bf16[2,256,640]{2,1,0:T(8,128)(2,1)}, u32[]{:S(2)}, u32[]{:S(2)}) collective-permute-start(bf16[2,256,640]{2,1,0:T(8,128)(2,1)S(1)} %bitcast.98), channel_id=1, source_target_pairs={{0,1},{1,2},{2,3},{4,5},{5,6},{6,7},{8,9},{9,10},{10,11},{12,13},{... | collective-permute-start | bytes 1966088 | tf_op jit(solution)/shard_map/ppermute | solution.py:26
  144.1 7.9 %collective-permute-done.20.high_ref = bf16[2,256,640]{2,1,0:T(8,128)(2,1)} collective-permute-done((bf16[2,256,640]{2,1,0:T(8,128)(2,1)S(1)}, bf16[2,256,640]{2,1,0:T(8,128)(2,1)}, u32[]{:S(2)}, u32[]{:S(2)}) %collective-permute-start.20) | collective-permute-done | bytes 655392 | tf_op jit(solution)/shard_map/ppermute | solution.py:27
  158.0 7.5 %convolve.3 = (bf16[512,3200]{1,0:T(8,128)(2,1)S(1)}, f32[512,640]{1,0:T(8,128)S(1)}, bf16[512,640]{1,0:T(8,128)(2,1)S(1)}, bf16[512,1280]{1,0:T(8,128)(2,1)}) custom-call(bf16[2,256,640]{2,1,0:T(8,128)(2,1)} %collective-permute-done.19.low_ref, bf16[2,256,640]{2,1,0:T(8,128)(2,1)S(1)} %bitcast.99, bf16[2,256,640]{2,1,0:T(8,128)(2,1)} %collective-permute-done.20.high_ref, ...), custom_call_target="tpu_custom_call" | custom-call | flops 2936012800 | bytes 10485760 | tf_op jit(solution)/shard_map/convolve/pallas_call | solution.py:592
  172.2 4.2 %collective-permute-start.21 = (bf16[2,256,640]{2,1,0:T(8,128)(2,1)S(1)}, bf16[2,256,640]{2,1,0:T(8,128)(2,1)}, u32[]{:S(2)}, u32[]{:S(2)}) collective-permute-start(bf16[2,256,640]{2,1,0:T(8,128)(2,1)S(1)} %bitcast.90), channel_id=1, source_target_pairs={{0,1},{1,2},{2,3},{4,5},{5,6},{6,7},{8,9},{9,10},{10,11},{12,13},{... | collective-permute-start | bytes 1966088 | tf_op jit(solution)/shard_map/ppermute | solution.py:26
  176.4 6.1 %weight_grads.1 = bf16[8,560,640]{2,1,0:T(8,128)(2,1)S(1)} custom-call(bf16[512,3200]{1,0:T(8,128)(2,1)S(1)} %get-tuple-element.134.tap_ref, bf16[512,640]{1,0:T(8,128)(2,1)S(1)} %get-tuple-element.136.gv_ref, bf16[512,640]{1,0:T(8,128)(2,1)S(1)} %get-tuple-element.137.act_three_ref, bf16[512,1280]{1,0:T(8,128)(2,1)S(1)} %get-tuple-element.138.short_ref), custom_call_target="tpu_custom_call" | custom-call | flops 2936012800 | bytes 5242880 | tf_op jit(solution)/shard_map/weight_grads/pallas_call | solution.py:664
  197.7 9.4 %conv_back.2 = (bf16[512,640]{1,0:T(8,128)(2,1)S(1)}, f32[512,1280]{1,0:T(8,128)S(1)}, f32[8,640]{1,0:T(8,128)S(1)}, f32[8,1280]{1,0:T(8,128)S(1)}) custom-call(bf16[2,256,640]{2,1,0:T(8,128)(2,1)} %collective-permute-done.21.low_ref, bf16[2,256,640]{2,1,0:T(8,128)(2,1)S(1)} %bitcast.91, bf16[2,256,640]{2,1,0:T(8,128)(2,1)} %collective-permute-done.22.high_ref, ...), custom_call_target="tpu_custom_call" | custom-call | flops 2936012800 | bytes 10485760 | tf_op jit(solution)/shard_map/conv_back/pallas_call | solution.py:691
  209.7 3.6 %out_back.3 = (bf16[512,1280]{1,0:T(8,128)(2,1)S(1)}, bf16[512,640]{1,0:T(8,128)(2,1)S(1)}, f32[8,640]{1,0:T(8,128)S(1)}, f32[8,1280]{1,0:T(8,128)S(1)}) custom-call(f32[512,1280]{1,0:T(8,128)S(1)} %get-tuple-element.148.g_ref, f32[512,640]{1,0:T(8,128)S(1)} %copy-done.16, bf16[8,560,640]{2,1,0:T(8,128)(2,1)S(1)} %bitcast.63, ...), custom_call_target="tpu_custom_call" | custom-call | flops 1677721600 | bytes 6553600 | tf_op jit(solution)/shard_map/out_back/pallas_call | solution.py:636
  215.4 3.6 %collective-permute-start.23 = (bf16[2,128,640]{2,1,0:T(8,128)(2,1)S(1)}, bf16[2,128,640]{2,1,0:T(8,128)(2,1)S(1)}, u32[]{:S(2)}, u32[]{:S(2)}) collective-permute-start(bf16[2,128,640]{2,1,0:T(8,128)(2,1)S(1)} %get-tuple-element.227), channel_id=1, source_target_pairs={{0,1},{1,2},{2,3},{4,5},{5,6},{6,7},{8,9},{9,10},{10,11},{12,13},{... | collective-permute-start | bytes 983048 | tf_op jit(solution)/shard_map/ppermute | solution.py:26
  219.1 7.7 %share_grads.1 = (bf16[4,560,640]{2,1,0:T(8,128)(2,1)S(1)}, bf16[4,560,640]{2,1,0:T(8,128)(2,1)}) custom-call(s32[2]{0:T(128)S(1)} %pad_add_fusion.place_ref, bf16[512,3200]{1,0:T(8,128)(2,1)S(1)} %copy-done.40, bf16[512,640]{1,0:T(8,128)(2,1)S(1)} %get-tuple-element.150.gv_ref, bf16[512,640]{1,0:T(8,128)(2,1)S(1)} %copy-done.44, ...), custom_call_target="tpu_custom_call" | custom-call | flops 2936012800 | bytes 5242880 | tf_op jit(solution)/shard_map/share_grads/pallas_call | solution.py:766
  230.3 9.8 %conv_back.3 = (bf16[512,640]{1,0:T(8,128)(2,1)S(1)}, f32[512,1280]{1,0:T(8,128)}, f32[8,640]{1,0:T(8,128)S(1)}, f32[8,1280]{1,0:T(8,128)S(1)}) custom-call(bf16[2,128,640]{2,1,0:T(8,128)(2,1)S(1)} %collective-permute-done.23.low_ref, bf16[2,256,640]{2,1,0:T(8,128)(2,1)S(1)} %bitcast.95, bf16[2,128,640]{2,1,0:T(8,128)(2,1)S(1)} %collective-permute-done.24.high_ref, ...), custom_call_target="tpu_custom_call" | custom-call | flops 2936012800 | bytes 10485760 | tf_op jit(solution)/shard_map/conv_back/pallas_call | solution.py:691
  255.4 3.8 %collective-permute-start.31 = (bf16[144,640]{1,0:T(8,128)(2,1)S(1)}, bf16[144,640]{1,0:T(8,128)(2,1)S(1)}, u32[]{:S(2)}, u32[]{:S(2)}) collective-permute-start(bf16[144,640]{1,0:T(8,128)(2,1)S(1)} %get-tuple-element.223), channel_id=1, source_target_pairs={{0,2},{1,3},{2,0},{3,1},{4,6},{5,7},{6,4},{7,5},{8,10},{9,11},{10,... | collective-permute-start | bytes 552968 | tf_op jit(solution)/shard_map/ppermute | solution.py:902
  259.2 17.6 %collective-permute-done.28.got_a = bf16[2,448,640]{2,1,0:T(8,128)(2,1)} collective-permute-done((bf16[2,448,640]{2,1,0:T(8,128)(2,1)}, bf16[2,448,640]{2,1,0:T(8,128)(2,1)}, u32[]{:S(2)}, u32[]{:S(2)}) %collective-permute-start.28) | collective-permute-done | bytes 1146912 | tf_op jit(solution)/shard_map/ppermute | solution.py:884
  280.2 12.7 %collective-permute-done.33.refs_1_ = bf16[448,640]{1,0:T(8,128)(2,1)S(1)} collective-permute-done((bf16[448,640]{1,0:T(8,128)(2,1)S(1)}, bf16[448,640]{1,0:T(8,128)(2,1)S(1)}, u32[]{:S(2)}, u32[]{:S(2)}) %collective-permute-start.33) | collective-permute-done | bytes 573472 | tf_op jit(solution)/shard_map/ppermute | solution.py:884
  301.5 18.0 %collective-permute-done.36.refs_2_ = bf16[240,640]{1,0:T(8,128)(2,1)S(1)} collective-permute-done((bf16[240,640]{1,0:T(8,128)(2,1)S(1)}, bf16[240,640]{1,0:T(8,128)(2,1)S(1)}, u32[]{:S(2)}, u32[]{:S(2)}) %collective-permute-start.36) | collective-permute-done | bytes 307232 | tf_op jit(solution)/shard_map/ppermute | solution.py:902
  319.5 4.4 %collective-permute-done.35.refs_1_ = bf16[240,640]{1,0:T(8,128)(2,1)S(1)} collective-permute-done((bf16[240,640]{1,0:T(8,128)(2,1)S(1)}, bf16[240,640]{1,0:T(8,128)(2,1)S(1)}, u32[]{:S(2)}, u32[]{:S(2)}) %collective-permute-start.35) | collective-permute-done | bytes 307232 | tf_op jit(solution)/shard_map/ppermute | solution.py:902
  (272 shorter events, 134.2 us)
Async XLA Ops:
  7.2 78.3 %all-gather.5.cloned.1.call-start = ((), (), s32[]{:S(2)}) async-start(), calls=%async_computation.2 | async-start | bytes 6451200 | tf_op jit(solution)/shard_map/all_gather | solution.py:1182
  9.6 15.6 %collective-permute-start.1 = (bf16[144,640]{1,0:T(8,128)(2,1)S(1)}, bf16[144,640]{1,0:T(8,128)(2,1)S(1)}, u32[]{:S(2)}, u32[]{:S(2)}) collective-permute-start(bf16[144,640]{1,0:T(8,128)(2,1)S(1)} %get-tuple-element.116.refs_0_), channel_id=1, source_target_pairs={{0,2},{1,3},{2,0},{3,1},{4,6},{5,7},{6,4},{7,5},{8,10},{9,11},{10,... | collective-permute-start | bytes 552968 | tf_op jit(solution)/shard_map/ppermute | solution.py:902
  12.8 15.5 %collective-permute-start = (bf16[144,640]{1,0:T(8,128)(2,1)S(1)}, bf16[144,640]{1,0:T(8,128)(2,1)S(1)}, u32[]{:S(2)}, u32[]{:S(2)}) collective-permute-start(bf16[144,640]{1,0:T(8,128)(2,1)S(1)} %get-tuple-element.116.refs_0_), channel_id=1, source_target_pairs={{0,1},{1,2},{2,3},{3,0},{4,5},{5,6},{6,7},{7,4},{8,9},{9,10},{10,1... | collective-permute-start | bytes 552968 | tf_op jit(solution)/shard_map/ppermute | solution.py:902
  30.3 123.6 %all-gather.7.cloned.1.call-start = ((), (), s32[]{:S(2)}) async-start(), calls=%async_computation.3 | async-start | bytes 6451200 | tf_op jit(solution)/shard_map/all_gather | solution.py:1187
  54.3 21.1 %collective-permute-start.9 = (bf16[2,176,640]{2,1,0:T(8,128)(2,1)S(1)}, bf16[2,176,640]{2,1,0:T(8,128)(2,1)S(1)}, u32[]{:S(2)}, u32[]{:S(2)}) collective-permute-start(bf16[2,176,640]{2,1,0:T(8,128)(2,1)S(1)} %pad_maximum_fusion.1.refs_2_), channel_id=1, source_target_pairs={{0,8},{4,12},{8,0},{12,4},{16,24},{20,28},{24,16},{28,20},{1,9},{5... | collective-permute-start | bytes 1351688 | tf_op jit(solution)/shard_map/ppermute | solution.py:884
  55.7 19.6 %collective-permute-start.8 = (bf16[2,176,640]{2,1,0:T(8,128)(2,1)S(1)}, bf16[2,176,640]{2,1,0:T(8,128)(2,1)S(1)}, u32[]{:S(2)}, u32[]{:S(2)}) collective-permute-start(bf16[2,176,640]{2,1,0:T(8,128)(2,1)S(1)} %pad_maximum_fusion.refs_0_), channel_id=1, source_target_pairs={{0,16},{4,20},{8,24},{12,28},{16,0},{20,4},{24,8},{28,12},{1,17},{... | collective-permute-start | bytes 1351688 | tf_op jit(solution)/shard_map/ppermute | solution.py:884
  56.2 14.5 %collective-permute-start.11 = (bf16[144,640]{1,0:T(8,128)(2,1)S(1)}, bf16[144,640]{1,0:T(8,128)(2,1)S(1)}, u32[]{:S(2)}, u32[]{:S(2)}) collective-permute-start(bf16[144,640]{1,0:T(8,128)(2,1)S(1)} %get-tuple-element.128.refs_0_), channel_id=1, source_target_pairs={{0,2},{1,3},{2,0},{3,1},{4,6},{5,7},{6,4},{7,5},{8,10},{9,11},{10,... | collective-permute-start | bytes 552968 | tf_op jit(solution)/shard_map/ppermute | solution.py:902
  58.2 17.1 %collective-permute-start.10 = (bf16[144,640]{1,0:T(8,128)(2,1)S(1)}, bf16[144,640]{1,0:T(8,128)(2,1)S(1)}, u32[]{:S(2)}, u32[]{:S(2)}) collective-permute-start(bf16[144,640]{1,0:T(8,128)(2,1)S(1)} %get-tuple-element.128.refs_0_), channel_id=1, source_target_pairs={{0,1},{1,2},{2,3},{3,0},{4,5},{5,6},{6,7},{7,4},{8,9},{9,10},{10,1... | collective-permute-start | bytes 552968 | tf_op jit(solution)/shard_map/ppermute | solution.py:902
  85.5 167.5 %reduce-scatter.2.cloned.1.call-start = ((), (), s32[]{:S(2)}) async-start(), calls=%async_computation.1 | async-start | bytes 6451200 | tf_op jit(solution)/shard_map/reduce_scatter | solution.py:1216
  134.7 17.3 %collective-permute-start.20 = (bf16[2,256,640]{2,1,0:T(8,128)(2,1)S(1)}, bf16[2,256,640]{2,1,0:T(8,128)(2,1)}, u32[]{:S(2)}, u32[]{:S(2)}) collective-permute-start(bf16[2,256,640]{2,1,0:T(8,128)(2,1)S(1)} %bitcast.97), channel_id=1, source_target_pairs={{1,0},{2,1},{3,2},{5,4},{6,5},{7,6},{9,8},{10,9},{11,10},{13,12},{... | collective-permute-start | bytes 1966088 | tf_op jit(solution)/shard_map/ppermute | solution.py:27
  136.7 17.3 %collective-permute-start.19 = (bf16[2,256,640]{2,1,0:T(8,128)(2,1)S(1)}, bf16[2,256,640]{2,1,0:T(8,128)(2,1)}, u32[]{:S(2)}, u32[]{:S(2)}) collective-permute-start(bf16[2,256,640]{2,1,0:T(8,128)(2,1)S(1)} %bitcast.98), channel_id=1, source_target_pairs={{0,1},{1,2},{2,3},{4,5},{5,6},{6,7},{8,9},{9,10},{10,11},{12,13},{... | collective-permute-start | bytes 1966088 | tf_op jit(solution)/shard_map/ppermute | solution.py:26
  170.3 16.3 %collective-permute-start.22 = (bf16[2,256,640]{2,1,0:T(8,128)(2,1)S(1)}, bf16[2,256,640]{2,1,0:T(8,128)(2,1)}, u32[]{:S(2)}, u32[]{:S(2)}) collective-permute-start(bf16[2,256,640]{2,1,0:T(8,128)(2,1)S(1)} %bitcast.89), channel_id=1, source_target_pairs={{1,0},{2,1},{3,2},{5,4},{6,5},{7,6},{9,8},{10,9},{11,10},{13,12},{... | collective-permute-start | bytes 1966088 | tf_op jit(solution)/shard_map/ppermute | solution.py:27
  172.2 16.4 %collective-permute-start.21 = (bf16[2,256,640]{2,1,0:T(8,128)(2,1)S(1)}, bf16[2,256,640]{2,1,0:T(8,128)(2,1)}, u32[]{:S(2)}, u32[]{:S(2)}) collective-permute-start(bf16[2,256,640]{2,1,0:T(8,128)(2,1)S(1)} %bitcast.90), channel_id=1, source_target_pairs={{0,1},{1,2},{2,3},{4,5},{5,6},{6,7},{8,9},{9,10},{10,11},{12,13},{... | collective-permute-start | bytes 1966088 | tf_op jit(solution)/shard_map/ppermute | solution.py:26
  213.4 13.5 %collective-permute-start.24 = (bf16[2,128,640]{2,1,0:T(8,128)(2,1)S(1)}, bf16[2,128,640]{2,1,0:T(8,128)(2,1)S(1)}, u32[]{:S(2)}, u32[]{:S(2)}) collective-permute-start(bf16[2,128,640]{2,1,0:T(8,128)(2,1)S(1)} %get-tuple-element.226), channel_id=1, source_target_pairs={{1,0},{2,1},{3,2},{5,4},{6,5},{7,6},{9,8},{10,9},{11,10},{13,12},{... | collective-permute-start | bytes 983048 | tf_op jit(solution)/shard_map/ppermute | solution.py:27
  226.8 19.1 %collective-permute-start.25 = (bf16[4,560,640]{2,1,0:T(8,128)(2,1)}, bf16[4,560,640]{2,1,0:T(8,128)(2,1)S(1)}, u32[]{:S(2)}, u32[]{:S(2)}) collective-permute-start(bf16[4,560,640]{2,1,0:T(8,128)(2,1)} %get-tuple-element.177), channel_id=1, source_target_pairs={{0,4},{4,0},{8,12},{12,8},{16,20},{20,16},{24,28},{28,24},{1,5},{5... | collective-permute-start | bytes 8601608 | tf_op jit(solution)/shard_map/ppermute | solution.py:884
  249.3 27.9 %collective-permute-start.29 = (bf16[2,464,640]{2,1,0:T(8,128)(2,1)}, bf16[2,464,640]{2,1,0:T(8,128)(2,1)S(1)}, u32[]{:S(2)}, u32[]{:S(2)}) collective-permute-start(bf16[2,464,640]{2,1,0:T(8,128)(2,1)} %get-tuple-element.189), channel_id=1, source_target_pairs={{0,16},{4,20},{8,24},{12,28},{16,0},{20,4},{24,8},{28,12},{1,17},{... | collective-permute-start | bytes 3563528 | tf_op jit(solution)/shard_map/ppermute | solution.py:884
  250.1 26.7 %collective-permute-start.28 = (bf16[2,448,640]{2,1,0:T(8,128)(2,1)}, bf16[2,448,640]{2,1,0:T(8,128)(2,1)}, u32[]{:S(2)}, u32[]{:S(2)}) collective-permute-start(bf16[2,448,640]{2,1,0:T(8,128)(2,1)} %get-tuple-element.187), channel_id=1, source_target_pairs={{0,8},{4,12},{8,0},{12,4},{16,24},{20,28},{24,16},{28,20},{1,9},{5... | collective-permute-start | bytes 3440648 | tf_op jit(solution)/shard_map/ppermute | solution.py:884
  255.1 22.1 %collective-permute-start.32 = (bf16[144,640]{1,0:T(8,128)(2,1)S(1)}, bf16[144,640]{1,0:T(8,128)(2,1)S(1)}, u32[]{:S(2)}, u32[]{:S(2)}) collective-permute-start(bf16[144,640]{1,0:T(8,128)(2,1)S(1)} %get-tuple-element.222), channel_id=1, source_target_pairs={{0,3},{1,0},{2,1},{3,2},{4,7},{5,4},{6,5},{7,6},{8,11},{9,8},{10,9... | collective-permute-start | bytes 552968 | tf_op jit(solution)/shard_map/ppermute | solution.py:902
  255.4 21.8 %collective-permute-start.31 = (bf16[144,640]{1,0:T(8,128)(2,1)S(1)}, bf16[144,640]{1,0:T(8,128)(2,1)S(1)}, u32[]{:S(2)}, u32[]{:S(2)}) collective-permute-start(bf16[144,640]{1,0:T(8,128)(2,1)S(1)} %get-tuple-element.223), channel_id=1, source_target_pairs={{0,2},{1,3},{2,0},{3,1},{4,6},{5,7},{6,4},{7,5},{8,10},{9,11},{10,... | collective-permute-start | bytes 552968 | tf_op jit(solution)/shard_map/ppermute | solution.py:902
  259.2 17.9 %collective-permute-start.30 = (bf16[144,640]{1,0:T(8,128)(2,1)S(1)}, bf16[144,640]{1,0:T(8,128)(2,1)S(1)}, u32[]{:S(2)}, u32[]{:S(2)}) collective-permute-start(bf16[144,640]{1,0:T(8,128)(2,1)S(1)} %get-tuple-element.224), channel_id=1, source_target_pairs={{0,1},{1,2},{2,3},{3,0},{4,5},{5,6},{6,7},{7,4},{8,9},{9,10},{10,1... | collective-permute-start | bytes 552968 | tf_op jit(solution)/shard_map/ppermute | solution.py:902
  279.0 14.1 %collective-permute-start.34 = (bf16[464,640]{1,0:T(8,128)(2,1)S(1)}, bf16[464,640]{1,0:T(8,128)(2,1)S(1)}, u32[]{:S(2)}, u32[]{:S(2)}) collective-permute-start(bf16[464,640]{1,0:T(8,128)(2,1)S(1)} %get-tuple-element.199), channel_id=1, source_target_pairs={{0,8},{4,12},{8,0},{12,4},{16,24},{20,28},{24,16},{28,20},{1,9},{5... | collective-permute-start | bytes 1781768 | tf_op jit(solution)/shard_map/ppermute | solution.py:884
  279.6 13.4 %collective-permute-start.33 = (bf16[448,640]{1,0:T(8,128)(2,1)S(1)}, bf16[448,640]{1,0:T(8,128)(2,1)S(1)}, u32[]{:S(2)}, u32[]{:S(2)}) collective-permute-start(bf16[448,640]{1,0:T(8,128)(2,1)S(1)} %get-tuple-element.197), channel_id=1, source_target_pairs={{0,16},{4,20},{8,24},{12,28},{16,0},{20,4},{24,8},{28,12},{1,17},{... | collective-permute-start | bytes 1720328 | tf_op jit(solution)/shard_map/ppermute | solution.py:884
  295.0 24.5 %collective-permute-start.36 = (bf16[240,640]{1,0:T(8,128)(2,1)S(1)}, bf16[240,640]{1,0:T(8,128)(2,1)S(1)}, u32[]{:S(2)}, u32[]{:S(2)}) collective-permute-start(bf16[240,640]{1,0:T(8,128)(2,1)S(1)} %get-tuple-element.219), channel_id=1, source_target_pairs={{0,2},{1,3},{2,0},{3,1},{4,6},{5,7},{6,4},{7,5},{8,10},{9,11},{10,... | collective-permute-start | bytes 921608 | tf_op jit(solution)/shard_map/ppermute | solution.py:902
  298.1 25.8 %collective-permute-start.35 = (bf16[240,640]{1,0:T(8,128)(2,1)S(1)}, bf16[240,640]{1,0:T(8,128)(2,1)S(1)}, u32[]{:S(2)}, u32[]{:S(2)}) collective-permute-start(bf16[240,640]{1,0:T(8,128)(2,1)S(1)} %get-tuple-element.220), channel_id=1, source_target_pairs={{0,1},{1,2},{2,3},{3,0},{4,5},{5,6},{6,7},{7,4},{8,9},{9,10},{10,1... | collective-permute-start | bytes 921608 | tf_op jit(solution)/shard_map/ppermute | solution.py:902
  (88 other events, 697.1 us)
Sparse Core Ops, SparseCore 0:
  30.4 54.9 all-gather.4
  87.9 41.6 all-gather.6
  188.7 64.1 reduce-scatter.1

commit v2 on v1

--- a/solution.py
+++ b/solution.py
@@ -420,7 +420,10 @@
             ref[block : block + 1, :] = row[:, : ref.shape[1]]
 
 
-def main_pack_kernel(w_conv, w_out, early_ref, late_ref):
+def shard_pack_kernel(w_in, w_conv, w_out, lead_ref, early_ref, late_ref):
+    count = lead_ref.shape[1] // w_in.shape[2]
+    lead = jnp.concatenate([w_in[0], w_in[1]], axis=0)
+    lead_ref[...] = lane_packed(lead, lead_ref.shape[0], count)
     width = w_conv.shape[3]
     count = early_ref.shape[1] // width
     for block, ref in ((0, early_ref), (1, late_ref)):
@@ -429,10 +432,7 @@
         ref[...] = lane_packed(jnp.concatenate(rows, axis=0), ref.shape[0], count)
 
 
-def lead_pack_kernel(w_in, wide, narrow, lead_ref, vector_ref):
-    count = lead_ref.shape[1] // w_in.shape[2]
-    lead = jnp.concatenate([w_in[0], w_in[1]], axis=0)
-    lead_ref[...] = lane_packed(lead, lead_ref.shape[0], count)
+def vector_pack_kernel(wide, narrow, vector_ref):
     hidden = vector_ref.shape[1]
     for block in range(2):
         rows = []
@@ -585,10 +585,10 @@
     )(inputs, weights.first[0], weights.wide, weights.narrow)
 
 
-def convolve(act_two, flags, inputs, weights, dilation_step, next_dtype):
+def convolve(act_two, halos, flags, inputs, weights, dilation_step, next_dtype):
     rows, length, hidden = act_two.shape
     tokens, model = inputs.shape
-    low, high = seq_neighbours(act_two, KER // 2 * dilation_step)
+    low, high = halos
     return call(
         functools.partial(convolve_kernel, dilation_step),
         rows,
@@ -1045,11 +1045,11 @@
     )
 
 
-def block_forward(inputs, weights, flags, dilation_step, next_dtype):
+def block_forward(inputs, projected, halos, weights, flags, dilation_step, next_dtype):
     rows, length, _ = flags.shape
-    act_one, u, act_two = project(inputs, weights)
+    act_one, u, act_two = projected
     tap_rows, conv_out, act_three, output = convolve(
-        act_two.reshape(rows, length, -1), flags, inputs, weights, dilation_step, next_dtype
+        act_two.reshape(rows, length, -1), halos, flags, inputs, weights, dilation_step, next_dtype
     )
     return output, (act_one, u, tap_rows, conv_out, act_three)
 
@@ -1075,38 +1075,37 @@
     return result, reduce_dp(grad_pack, wide, narrow), before
 
 
-def main_pack(w_conv, w_out):
+def shard_pack(w_in, w_conv, w_out):
     count = lax.axis_size("seq")
     depth, width = w_conv.shape[2:]
-    rows = packed_depth((KER + w_out.shape[2] // width) * depth, count)
-    out = shape_of((rows, width * count), jnp.bfloat16)
+    ins = (w_in, w_conv, w_out)
+    rest = packed_depth((KER + w_out.shape[2] // width) * depth, count)
+    lead = packed_depth(2 * w_in.shape[1], count)
+    outs = [shape_of((n, width * count), jnp.bfloat16) for n in (lead, rest, rest)]
     return call(
-        main_pack_kernel,
-        1,
-        [fixed(*w_conv.shape), fixed(*w_out.shape)],
-        [fixed(*out.shape)] * 2,
-        [out, out],
-        out.size,
-        8 * out.size,
-        "main_pack",
-    )(w_conv, w_out)
-
-
-def lead_pack(w_in, wide, narrow):
-    count = lax.axis_size("seq")
-    hidden = w_in.shape[2] * count
-    ins = (w_in, jnp.stack(wide, axis=1), jnp.stack(narrow, axis=1))
-    rows = packed_depth(2 * w_in.shape[1], count)
-    outs = [shape_of((n, hidden), jnp.bfloat16) for n in (rows, 2 * VECTOR_ROWS)]
-    return call(
-        lead_pack_kernel,
+        shard_pack_kernel,
         1,
         [fixed(*array.shape) for array in ins],
         [fixed(*out.shape) for out in outs],
         outs,
-        rows * hidden,
-        8 * rows * hidden,
-        "lead_pack",
+        rest * width,
+        8 * rest * width,
+        "shard_pack",
+    )(*ins)
+
+
+def pack_vectors(wide, narrow, hidden):
+    ins = (jnp.stack(wide, axis=1), jnp.stack(narrow, axis=1))
+    out = (2 * VECTOR_ROWS, hidden)
+    return call(
+        vector_pack_kernel,
+        1,
+        [fixed(*array.shape) for array in ins],
+        fixed(*out),
+        shape_of(out, jnp.bfloat16),
+        hidden,
+        hidden,
+        "pack_vectors",
     )(*ins)
 
 
@@ -1135,11 +1134,13 @@
 
 
 class Exchange:
-    def __init__(self, block):
+    def __init__(self, block, beside):
         self.block = block
         self.cut = block.shape[0] // 32 * 16
         a, b = block[: self.cut], block[self.cut :]
-        got_a, got_b = lax.optimization_barrier((dp_swapped(a, 1), dp_swapped(b, 2)))
+        got_a, got_b, *self.beside = lax.optimization_barrier(
+            (dp_swapped(a, 1), dp_swapped(b, 2), *beside)
+        )
         self.near = (jnp.stack([a, got_a]), jnp.stack([b, got_b]))
 
     def finish(self, where, beside):
@@ -1174,27 +1175,29 @@
     folds = w_out.shape[2] // width
     folded = (KER * depth, (KER + folds) * depth)
     plain = (2 * first_rows, 2 * first_rows)
-    early, late = main_pack(w_conv, w_out)
+    lead, early, late = shard_pack(w_in, w_conv, w_out)
     wide = [shards[i] for i in (0, 1, 11)]
-    lead, vectors = lead_pack(w_in, wide, [shards[i] for i in (3, 4, 5, 7, 8, 9)])
-
-    early = seq_join(where, folded, seq_shares(early))
+    narrow = [shards[i] for i in (3, 4, 5, 7, 8, 9)]
+    vectors = pack_vectors(wide, narrow, width * lax.axis_size("seq"))
+    lead = seq_join(where, plain, seq_shares(lead), vectors)
+    exchange = Exchange(lead, seq_shares(after(early, lead)))
+    early = seq_join(where, folded, exchange.beside)
     early_whole = lax.all_gather(early, "dp")
-    exchange = Exchange(seq_join(where, plain, seq_shares(after(lead, early)), vectors))
-    late = seq_shares(after(late, *exchange.near))
-    lead, late = exchange.finish(where, late)
-    late = seq_join(where, folded, late)
-    late_whole = lax.all_gather(after(late, early_whole), "dp")
-
+    lead, late = exchange.finish(where, seq_shares(after(late, early)))
     tail = lead[:, 2 * first_rows :].astype(jnp.float32)
-    out = []
-    for block, whole in ((0, early_whole), (1, late_whole)):
+
+    def weights(block, whole):
         start = block * VECTOR_ROWS
         wide = tail[:, start : start + 3, :first_rows].transpose(1, 0, 2).reshape(3, -1)
         narrow = tail[:, start + 3 : start + 9, :depth].transpose(1, 0, 2).reshape(6, -1)
         units = [(whole, i) for i in range(KER + folds)]
-        out.append(Weights((lead, block), units[:KER], units[KER:], wide, narrow))
-    return out
+        return Weights((lead, block), units[:KER], units[KER:], wide, narrow)
+
+    def late_weights(projected):
+        rows = seq_join(where, folded, list(after(tuple(late), lead)))
+        return weights(1, lax.all_gather(after(rows, early_whole, projected), "dp"))
+
+    return weights(0, early_whole), late_weights
 
 
 def exchanged_backward(inputs, weights, kept, flags, dilations, cotangent, out_shapes):
@@ -1314,11 +1317,17 @@
         early_weights = gathered_params(0, device_shards)
         late_weights = gathered_params(1, device_shards, early_weights.first[0])
     flat_tokens = tokens.reshape(rows * seq_len, model)
+    projected = project(flat_tokens, early_weights)
+    halos = seq_neighbours(projected[2].reshape(rows, seq_len, -1), KER // 2 * FIRST_DILATION)
+    if fast:
+        late_weights = late_weights(halos)
     middle, early_kept = block_forward(
-        flat_tokens, early_weights, early_flags, FIRST_DILATION, jnp.float32
-    )
+        flat_tokens, projected, halos, early_weights, early_flags, FIRST_DILATION, jnp.float32
+    )
+    projected = project(middle, late_weights)
+    halos = seq_neighbours(projected[2].reshape(rows, seq_len, -1), KER // 2 * SECOND_DILATION)
     output, late_kept = block_forward(
-        middle, late_weights, later_flags, SECOND_DILATION, jnp.bfloat16
+        middle, projected, halos, late_weights, later_flags, SECOND_DILATION, jnp.bfloat16
     )
     hidden = early_weights.hidden
     if fast:

time: 335 us -> 319 us (0.952)
  waiting for transfers between devices: 139 us -> 117 us
    ppermute x15, waiting for transfers between devices: 67.3 us -> 54.8 us  [shifted(): lax.ppermute(block, 'seq', [(i, (i + step) % count) for i in range(count)])]
    ppermute x15, waiting for transfers between devices: 44.4 us -> 36.1 us  [dp_swapped(): return lax.ppermute(block, 'dp', [(i, i ^ 1 << bit) for i in range(count)])]
    all_gather x1, waiting for transfers between devices: 8.16 us -> 0.01 us  [exchanged_weights(): early_whole = lax.all_gather(early, 'dp')]
    another operation x10, local copies, waits for them, and re-layouts: 0.08 us -> 6.03 us  [pack_vectors(): ins = (jnp.stack(wide, axis=1), jnp.stack(narrow, axis=1))]
    unnamed x142 -> x122, local copies, waits for them, and re-layouts: 35.8 us -> 35.6 us
  transfers between devices with their start and end apart: 41 -> 41, of which waited for: 28 -> 25; matrix products, arithmetic and copies ran while one was open for 3% -> 5% of each run, Pallas kernels for 19% -> 20%
where the time goes in v2:
time: 319 us; the launch traced here: 315 us
  waiting for transfers between devices  117 us (37%)
  Pallas kernels  80.7 us (25%)
  starting transfers between devices  52.5 us (16%)
  local copies, waits for them, and re-layouts  47.1 us (15%)
  between operations  14.6 us (5%)
    ppermute x15, waiting for transfers between devices, shifted(): lax.ppermute(block, 'seq', [(i, (i + step) % count) for i in range(count)])  54.8 us
    ppermute x15, waiting for transfers between devices, dp_swapped(): return lax.ppermute(block, 'dp', [(i, i ^ 1 << bit) for i in range(count)])  36.1 us
    unnamed x122, local copies, waits for them, and re-layouts  35.6 us
    pallas_call x2, Pallas kernels, conv_back_with(): call(functools.partial(conv_back_kernel, dilation_step), rows, [row_block...  19.2 us
    ppermute x15, starting transfers between devices, dp_swapped(): return lax.ppermute(block, 'dp', [(i, i ^ 1 << bit) for i in range(count)])  14.6 us
    ppermute x15, starting transfers between devices, shifted(): lax.ppermute(block, 'seq', [(i, (i + step) % count) for i in range(count)])  14.3 us
    ppermute x4, waiting for transfers between devices, seq_neighbours(): high = lax.ppermute(block[:, :width], 'seq', backward)  13.9 us
    ppermute x4, starting transfers between devices, seq_neighbours(): low = lax.ppermute(block[:, block.shape[1] - width:], 'seq', forward)  13.7 us
  transfers between devices with their start and end apart: 41, of which 25 were waited for; matrix products, arithmetic and copies ran while one was open for 5% of the time, Pallas kernels for 20%

profile of v2, /device:TPU:17, one launch (start us, length us, event | category | flops | bytes accessed | tf_op | source)
XLA Modules:
  0.0 315.2 jit_solution(6086270664128212394)
XLA Ops:
  30.3 9.4 %collective-permute-done.6.refs_2_ = bf16[144,640]{1,0:T(8,128)(2,1)S(1)} collective-permute-done((bf16[144,640]{1,0:T(8,128)(2,1)S(1)}, bf16[144,640]{1,0:T(8,128)(2,1)S(1)}, u32[]{:S(2)}, u32[]{:S(2)}) %collective-permute-start.6) | collective-permute-done | bytes 184352 | tf_op jit(solution)/shard_map/ppermute | solution.py:902
  39.7 3.9 %collective-permute-done.5.refs_1_ = bf16[144,640]{1,0:T(8,128)(2,1)S(1)} collective-permute-done((bf16[144,640]{1,0:T(8,128)(2,1)S(1)}, bf16[144,640]{1,0:T(8,128)(2,1)S(1)}, u32[]{:S(2)}, u32[]{:S(2)}) %collective-permute-start.5) | collective-permute-done | bytes 184352 | tf_op jit(solution)/shard_map/ppermute | solution.py:902
  47.9 3.6 %collective-permute-done.12.refs_3_ = bf16[144,640]{1,0:T(8,128)(2,1)S(1)} collective-permute-done((bf16[144,640]{1,0:T(8,128)(2,1)S(1)}, bf16[144,640]{1,0:T(8,128)(2,1)S(1)}, u32[]{:S(2)}, u32[]{:S(2)}) %collective-permute-start.12) | collective-permute-done | bytes 184352 | tf_op jit(solution)/shard_map/ppermute | solution.py:902
  51.5 3.5 %collective-permute-start.15 = (bf16[2,176,640]{2,1,0:T(8,128)(2,1)S(1)}, bf16[2,176,640]{2,1,0:T(8,128)(2,1)S(1)}, u32[]{:S(2)}, u32[]{:S(2)}) collective-permute-start(bf16[2,176,640]{2,1,0:T(8,128)(2,1)S(1)} %pad_maximum_fusion.1.refs_2_), channel_id=1, source_target_pairs={{0,4},{4,0},{8,12},{12,8},{16,20},{20,16},{24,28},{28,24},{1,5},{5... | collective-permute-start | bytes 1351688 | tf_op jit(solution)/shard_map/ppermute | solution.py:884
  55.0 6.4 %collective-permute-done.11.refs_2_ = bf16[144,640]{1,0:T(8,128)(2,1)S(1)} collective-permute-done((bf16[144,640]{1,0:T(8,128)(2,1)S(1)}, bf16[144,640]{1,0:T(8,128)(2,1)S(1)}, u32[]{:S(2)}, u32[]{:S(2)}) %collective-permute-start.11) | collective-permute-done | bytes 184352 | tf_op jit(solution)/shard_map/ppermute | solution.py:902
  72.4 4.3 %project.2 = (bf16[512,1280]{1,0:T(8,128)(2,1)S(1)}, f32[512,640]{1,0:T(8,128)S(1)}, bf16[512,640]{1,0:T(8,128)(2,1)S(1)}) custom-call(bf16[512,1280]{1,0:T(8,128)(2,1)S(1)} %bitcast.86, bf16[8,352,640]{2,1,0:T(8,128)(2,1)S(1)} %copy-done.5, f32[3,1280]{1,0:T(4,128)S(1)} %reshape.818.wide_ref, f32[6,640]{1,0:T(8,128)S(1)} %reshape.819.narrow_ref), custom_call_target="tpu_custom_call" | custom-call | flops 1677721600 | bytes 7864320 | tf_op jit(solution)/shard_map/project/pallas_call | solution.py:572
  79.9 3.4 %collective-permute-start.17 = (bf16[2,128,640]{2,1,0:T(8,128)(2,1)S(1)}, bf16[2,128,640]{2,1,0:T(8,128)(2,1)S(1)}, u32[]{:S(2)}, u32[]{:S(2)}) collective-permute-start(bf16[2,128,640]{2,1,0:T(8,128)(2,1)S(1)} %get-tuple-element.247), channel_id=1, source_target_pairs={{0,1},{1,2},{2,3},{4,5},{5,6},{6,7},{8,9},{9,10},{10,11},{12,13},{... | collective-permute-start | bytes 983048 | tf_op jit(solution)/shard_map/ppermute | solution.py:26
  85.3 3.5 %collective-permute-done.18.high_ref = bf16[2,128,640]{2,1,0:T(8,128)(2,1)S(1)} collective-permute-done((bf16[2,128,640]{2,1,0:T(8,128)(2,1)S(1)}, bf16[2,128,640]{2,1,0:T(8,128)(2,1)S(1)}, u32[]{:S(2)}, u32[]{:S(2)}) %collective-permute-start.18) | collective-permute-done | bytes 327712 | tf_op jit(solution)/shard_map/ppermute | solution.py:27
  102.6 6.0 %convolve.2 = (bf16[512,3200]{1,0:T(8,128)(2,1)S(1)}, f32[512,640]{1,0:T(8,128)S(1)}, bf16[512,640]{1,0:T(8,128)(2,1)S(1)}, f32[512,1280]{1,0:T(8,128)S(1)}) custom-call(bf16[2,128,640]{2,1,0:T(8,128)(2,1)S(1)} %copy-done.31, bf16[2,256,640]{2,1,0:T(8,128)(2,1)S(1)} %bitcast.93, bf16[2,128,640]{2,1,0:T(8,128)(2,1)S(1)} %copy-done.29, ...), custom_call_target="tpu_custom_call" | custom-call | flops 2936012800 | bytes 10485760 | tf_op jit(solution)/shard_map/convolve/pallas_call | solution.py:592
  108.7 4.2 %project.3 = (bf16[512,1280]{1,0:T(8,128)(2,1)S(1)}, f32[512,640]{1,0:T(8,128)S(1)}, bf16[512,640]{1,0:T(8,128)(2,1)S(1)}) custom-call(f32[512,1280]{1,0:T(8,128)S(1)} %get-tuple-element.136.x_ref, bf16[8,352,640]{2,1,0:T(8,128)(2,1)S(1)} %copy-done.6, f32[3,1280]{1,0:T(4,128)S(1)} %reshape.821.wide_ref, f32[6,640]{1,0:T(8,128)S(1)} %reshape.822.narrow_ref), custom_call_target="tpu_custom_call" | custom-call | flops 1677721600 | bytes 7864320 | tf_op jit(solution)/shard_map/project/pallas_call | solution.py:572
  124.5 7.6 %collective-permute-done.20.high_ref = bf16[2,256,640]{2,1,0:T(8,128)(2,1)} collective-permute-done((bf16[2,256,640]{2,1,0:T(8,128)(2,1)S(1)}, bf16[2,256,640]{2,1,0:T(8,128)(2,1)}, u32[]{:S(2)}, u32[]{:S(2)}) %collective-permute-start.20) | collective-permute-done | bytes 655392 | tf_op jit(solution)/shard_map/ppermute | solution.py:27
  140.7 7.5 %convolve.3 = (bf16[512,3200]{1,0:T(8,128)(2,1)S(1)}, f32[512,640]{1,0:T(8,128)S(1)}, bf16[512,640]{1,0:T(8,128)(2,1)S(1)}, bf16[512,1280]{1,0:T(8,128)(2,1)}) custom-call(bf16[2,256,640]{2,1,0:T(8,128)(2,1)} %collective-permute-done.19.low_ref, bf16[2,256,640]{2,1,0:T(8,128)(2,1)S(1)} %bitcast.99, bf16[2,256,640]{2,1,0:T(8,128)(2,1)} %collective-permute-done.20.high_ref, ...), custom_call_target="tpu_custom_call" | custom-call | flops 2936012800 | bytes 10485760 | tf_op jit(solution)/shard_map/convolve/pallas_call | solution.py:592
  148.2 3.5 %out_back.2 = (bf16[512,1280]{1,0:T(8,128)(2,1)S(1)}, bf16[512,640]{1,0:T(8,128)(2,1)S(1)}, f32[8,640]{1,0:T(8,128)S(1)}, f32[8,1280]{1,0:T(8,128)S(1)}) custom-call(bf16[512,1280]{1,0:T(8,128)(2,1)S(1)} %bitcast.84, f32[512,640]{1,0:T(8,128)S(1)} %get-tuple-element.149.v_ref, bf16[8,560,640]{2,1,0:T(8,128)(2,1)S(1)} %bitcast.77, ...), custom_call_target="tpu_custom_call" | custom-call | flops 1677721600 | bytes 6553600 | tf_op jit(solution)/shard_map/out_back/pallas_call | solution.py:636
  155.1 4.0 %collective-permute-start.21 = (bf16[2,256,640]{2,1,0:T(8,128)(2,1)S(1)}, bf16[2,256,640]{2,1,0:T(8,128)(2,1)}, u32[]{:S(2)}, u32[]{:S(2)}) collective-permute-start(bf16[2,256,640]{2,1,0:T(8,128)(2,1)S(1)} %bitcast.90), channel_id=1, source_target_pairs={{0,1},{1,2},{2,3},{4,5},{5,6},{6,7},{8,9},{9,10},{10,11},{12,13},{... | collective-permute-start | bytes 1966088 | tf_op jit(solution)/shard_map/ppermute | solution.py:26
  159.1 6.1 %weight_grads.1 = bf16[8,560,640]{2,1,0:T(8,128)(2,1)S(1)} custom-call(bf16[512,3200]{1,0:T(8,128)(2,1)S(1)} %get-tuple-element.148.tap_ref, bf16[512,640]{1,0:T(8,128)(2,1)S(1)} %get-tuple-element.150.gv_ref, bf16[512,640]{1,0:T(8,128)(2,1)S(1)} %get-tuple-element.151.act_three_ref, bf16[512,1280]{1,0:T(8,128)(2,1)S(1)} %get-tuple-element.152.short_ref), custom_call_target="tpu_custom_call" | custom-call | flops 2936012800 | bytes 5242880 | tf_op jit(solution)/shard_map/weight_grads/pallas_call | solution.py:664
  181.7 9.4 %conv_back.2 = (bf16[512,640]{1,0:T(8,128)(2,1)S(1)}, f32[512,1280]{1,0:T(8,128)S(1)}, f32[8,640]{1,0:T(8,128)S(1)}, f32[8,1280]{1,0:T(8,128)S(1)}) custom-call(bf16[2,256,640]{2,1,0:T(8,128)(2,1)} %collective-permute-done.21.low_ref, bf16[2,256,640]{2,1,0:T(8,128)(2,1)S(1)} %bitcast.91, bf16[2,256,640]{2,1,0:T(8,128)(2,1)} %collective-permute-done.22.high_ref, ...), custom_call_target="tpu_custom_call" | custom-call | flops 2936012800 | bytes 10485760 | tf_op jit(solution)/shard_map/conv_back/pallas_call | solution.py:691
  193.7 3.6 %out_back.3 = (bf16[512,1280]{1,0:T(8,128)(2,1)S(1)}, bf16[512,640]{1,0:T(8,128)(2,1)S(1)}, f32[8,640]{1,0:T(8,128)S(1)}, f32[8,1280]{1,0:T(8,128)S(1)}) custom-call(f32[512,1280]{1,0:T(8,128)S(1)} %get-tuple-element.162.g_ref, f32[512,640]{1,0:T(8,128)S(1)} %copy-done.16, bf16[8,560,640]{2,1,0:T(8,128)(2,1)S(1)} %bitcast.63, ...), custom_call_target="tpu_custom_call" | custom-call | flops 1677721600 | bytes 6553600 | tf_op jit(solution)/shard_map/out_back/pallas_call | solution.py:636
  203.2 7.8 %share_grads.1 = (bf16[4,560,640]{2,1,0:T(8,128)(2,1)S(1)}, bf16[4,560,640]{2,1,0:T(8,128)(2,1)}) custom-call(s32[2]{0:T(128)S(1)} %pad_add_fusion.place_ref, bf16[512,3200]{1,0:T(8,128)(2,1)S(1)} %copy-done.40, bf16[512,640]{1,0:T(8,128)(2,1)S(1)} %get-tuple-element.164.gv_ref, bf16[512,640]{1,0:T(8,128)(2,1)S(1)} %copy-done.44, ...), custom_call_target="tpu_custom_call" | custom-call | flops 2936012800 | bytes 5242880 | tf_op jit(solution)/shard_map/share_grads/pallas_call | solution.py:766
  213.5 9.8 %conv_back.3 = (bf16[512,640]{1,0:T(8,128)(2,1)S(1)}, f32[512,1280]{1,0:T(8,128)}, f32[8,640]{1,0:T(8,128)S(1)}, f32[8,1280]{1,0:T(8,128)S(1)}) custom-call(bf16[2,128,640]{2,1,0:T(8,128)(2,1)S(1)} %collective-permute-done.23.low_ref, bf16[2,256,640]{2,1,0:T(8,128)(2,1)S(1)} %bitcast.95, bf16[2,128,640]{2,1,0:T(8,128)(2,1)S(1)} %collective-permute-done.24.high_ref, ...), custom_call_target="tpu_custom_call" | custom-call | flops 2936012800 | bytes 10485760 | tf_op jit(solution)/shard_map/conv_back/pallas_call | solution.py:691
  238.7 3.5 %collective-permute-start.31 = (bf16[144,640]{1,0:T(8,128)(2,1)S(1)}, bf16[144,640]{1,0:T(8,128)(2,1)S(1)}, u32[]{:S(2)}, u32[]{:S(2)}) collective-permute-start(bf16[144,640]{1,0:T(8,128)(2,1)S(1)} %get-tuple-element.237), channel_id=1, source_target_pairs={{0,2},{1,3},{2,0},{3,1},{4,6},{5,7},{6,4},{7,5},{8,10},{9,11},{10,... | collective-permute-start | bytes 552968 | tf_op jit(solution)/shard_map/ppermute | solution.py:902
  242.2 18.0 %collective-permute-done.28.got_a = bf16[2,448,640]{2,1,0:T(8,128)(2,1)} collective-permute-done((bf16[2,448,640]{2,1,0:T(8,128)(2,1)}, bf16[2,448,640]{2,1,0:T(8,128)(2,1)}, u32[]{:S(2)}, u32[]{:S(2)}) %collective-permute-start.28) | collective-permute-done | bytes 1146912 | tf_op jit(solution)/shard_map/ppermute | solution.py:884
  263.7 12.8 %collective-permute-done.33.refs_1_ = bf16[448,640]{1,0:T(8,128)(2,1)S(1)} collective-permute-done((bf16[448,640]{1,0:T(8,128)(2,1)S(1)}, bf16[448,640]{1,0:T(8,128)(2,1)S(1)}, u32[]{:S(2)}, u32[]{:S(2)}) %collective-permute-start.33) | collective-permute-done | bytes 573472 | tf_op jit(solution)/shard_map/ppermute | solution.py:884
  284.5 17.8 %collective-permute-done.36.refs_2_ = bf16[240,640]{1,0:T(8,128)(2,1)S(1)} collective-permute-done((bf16[240,640]{1,0:T(8,128)(2,1)S(1)}, bf16[240,640]{1,0:T(8,128)(2,1)S(1)}, u32[]{:S(2)}, u32[]{:S(2)}) %collective-permute-start.36) | collective-permute-done | bytes 307232 | tf_op jit(solution)/shard_map/ppermute | solution.py:902
  302.3 4.9 %collective-permute-done.35.refs_1_ = bf16[240,640]{1,0:T(8,128)(2,1)S(1)} collective-permute-done((bf16[240,640]{1,0:T(8,128)(2,1)S(1)}, bf16[240,640]{1,0:T(8,128)(2,1)S(1)}, u32[]{:S(2)}, u32[]{:S(2)}) %collective-permute-start.35) | collective-permute-done | bytes 307232 | tf_op jit(solution)/shard_map/ppermute | solution.py:902
  (252 shorter events, 136.0 us)
Async XLA Ops:
  7.2 84.7 %all-gather.5.cloned.1.call-start = ((), (), s32[]{:S(2)}) async-start(), calls=%async_computation.2 | async-start | bytes 6451200 | tf_op jit(solution)/shard_map/all_gather | solution.py:1185
  23.1 20.5 %collective-permute-start.4 = (bf16[176,640]{1,0:T(8,128)(2,1)S(1)}, bf16[176,640]{1,0:T(8,128)(2,1)S(1)}, u32[]{:S(2)}, u32[]{:S(2)}) collective-permute-start(bf16[176,640]{1,0:T(8,128)(2,1)S(1)} %get-tuple-element.257), channel_id=1, source_target_pairs={{0,16},{4,20},{8,24},{12,28},{16,0},{20,4},{24,8},{28,12},{1,17},{... | collective-permute-start | bytes 675848 | tf_op jit(solution)/shard_map/ppermute | solution.py:884
  24.4 19.2 %collective-permute-start.3 = (bf16[176,640]{1,0:T(8,128)(2,1)S(1)}, bf16[176,640]{1,0:T(8,128)(2,1)S(1)}, u32[]{:S(2)}, u32[]{:S(2)}) collective-permute-start(bf16[176,640]{1,0:T(8,128)(2,1)S(1)} %get-tuple-element.258), channel_id=1, source_target_pairs={{0,8},{4,12},{8,0},{12,4},{16,24},{20,28},{24,16},{28,20},{1,9},{5... | collective-permute-start | bytes 675848 | tf_op jit(solution)/shard_map/ppermute | solution.py:884
  25.6 14.1 %collective-permute-start.6 = (bf16[144,640]{1,0:T(8,128)(2,1)S(1)}, bf16[144,640]{1,0:T(8,128)(2,1)S(1)}, u32[]{:S(2)}, u32[]{:S(2)}) collective-permute-start(bf16[144,640]{1,0:T(8,128)(2,1)S(1)} %get-tuple-element.128.refs_0_), channel_id=1, source_target_pairs={{0,2},{1,3},{2,0},{3,1},{4,6},{5,7},{6,4},{7,5},{8,10},{9,11},{10,... | collective-permute-start | bytes 552968 | tf_op jit(solution)/shard_map/ppermute | solution.py:902
  26.7 17.0 %collective-permute-start.5 = (bf16[144,640]{1,0:T(8,128)(2,1)S(1)}, bf16[144,640]{1,0:T(8,128)(2,1)S(1)}, u32[]{:S(2)}, u32[]{:S(2)}) collective-permute-start(bf16[144,640]{1,0:T(8,128)(2,1)S(1)} %get-tuple-element.128.refs_0_), channel_id=1, source_target_pairs={{0,1},{1,2},{2,3},{3,0},{4,5},{5,6},{6,7},{7,4},{8,9},{9,10},{10,1... | collective-permute-start | bytes 552968 | tf_op jit(solution)/shard_map/ppermute | solution.py:902
  45.6 90.9 %all-gather.7.cloned.1.call-start = ((), (), s32[]{:S(2)}) async-start(), calls=%async_computation.3 | async-start | bytes 6451200 | tf_op jit(solution)/shard_map/all_gather | solution.py:1198
  45.7 18.1 %collective-permute-start.9 = (bf16[2,176,640]{2,1,0:T(8,128)(2,1)S(1)}, bf16[2,176,640]{2,1,0:T(8,128)(2,1)S(1)}, u32[]{:S(2)}, u32[]{:S(2)}) collective-permute-start(bf16[2,176,640]{2,1,0:T(8,128)(2,1)S(1)} %pad_maximum_fusion.1.refs_2_), channel_id=1, source_target_pairs={{0,8},{4,12},{8,0},{12,4},{16,24},{20,28},{24,16},{28,20},{1,9},{5... | collective-permute-start | bytes 1351688 | tf_op jit(solution)/shard_map/ppermute | solution.py:884
  46.1 17.7 %collective-permute-start.8 = (bf16[2,176,640]{2,1,0:T(8,128)(2,1)S(1)}, bf16[2,176,640]{2,1,0:T(8,128)(2,1)S(1)}, u32[]{:S(2)}, u32[]{:S(2)}) collective-permute-start(bf16[2,176,640]{2,1,0:T(8,128)(2,1)S(1)} %pad_maximum_fusion.refs_0_), channel_id=1, source_target_pairs={{0,16},{4,20},{8,24},{12,28},{16,0},{20,4},{24,8},{28,12},{1,17},{... | collective-permute-start | bytes 1351688 | tf_op jit(solution)/shard_map/ppermute | solution.py:884
  46.4 15.0 %collective-permute-start.11 = (bf16[144,640]{1,0:T(8,128)(2,1)S(1)}, bf16[144,640]{1,0:T(8,128)(2,1)S(1)}, u32[]{:S(2)}, u32[]{:S(2)}) collective-permute-start(bf16[144,640]{1,0:T(8,128)(2,1)S(1)} %get-tuple-element.142.refs_0_), channel_id=1, source_target_pairs={{0,2},{1,3},{2,0},{3,1},{4,6},{5,7},{6,4},{7,5},{8,10},{9,11},{10,... | collective-permute-start | bytes 552968 | tf_op jit(solution)/shard_map/ppermute | solution.py:902
  46.4 17.4 %collective-permute-start.10 = (bf16[144,640]{1,0:T(8,128)(2,1)S(1)}, bf16[144,640]{1,0:T(8,128)(2,1)S(1)}, u32[]{:S(2)}, u32[]{:S(2)}) collective-permute-start(bf16[144,640]{1,0:T(8,128)(2,1)S(1)} %get-tuple-element.142.refs_0_), channel_id=1, source_target_pairs={{0,1},{1,2},{2,3},{3,0},{4,5},{5,6},{6,7},{7,4},{8,9},{9,10},{10,1... | collective-permute-start | bytes 552968 | tf_op jit(solution)/shard_map/ppermute | solution.py:902
  92.0 144.3 %reduce-scatter.2.cloned.1.call-start = ((), (), s32[]{:S(2)}) async-start(), calls=%async_computation.1 | async-start | bytes 6451200 | tf_op jit(solution)/shard_map/reduce_scatter | solution.py:1219
  115.1 17.0 %collective-permute-start.20 = (bf16[2,256,640]{2,1,0:T(8,128)(2,1)S(1)}, bf16[2,256,640]{2,1,0:T(8,128)(2,1)}, u32[]{:S(2)}, u32[]{:S(2)}) collective-permute-start(bf16[2,256,640]{2,1,0:T(8,128)(2,1)S(1)} %bitcast.97), channel_id=1, source_target_pairs={{1,0},{2,1},{3,2},{5,4},{6,5},{7,6},{9,8},{10,9},{11,10},{13,12},{... | collective-permute-start | bytes 1966088 | tf_op jit(solution)/shard_map/ppermute | solution.py:27
  118.1 16.0 %collective-permute-start.19 = (bf16[2,256,640]{2,1,0:T(8,128)(2,1)S(1)}, bf16[2,256,640]{2,1,0:T(8,128)(2,1)}, u32[]{:S(2)}, u32[]{:S(2)}) collective-permute-start(bf16[2,256,640]{2,1,0:T(8,128)(2,1)S(1)} %bitcast.98), channel_id=1, source_target_pairs={{0,1},{1,2},{2,3},{4,5},{5,6},{6,7},{8,9},{9,10},{10,11},{12,13},{... | collective-permute-start | bytes 1966088 | tf_op jit(solution)/shard_map/ppermute | solution.py:26
  152.9 17.6 %collective-permute-start.22 = (bf16[2,256,640]{2,1,0:T(8,128)(2,1)S(1)}, bf16[2,256,640]{2,1,0:T(8,128)(2,1)}, u32[]{:S(2)}, u32[]{:S(2)}) collective-permute-start(bf16[2,256,640]{2,1,0:T(8,128)(2,1)S(1)} %bitcast.89), channel_id=1, source_target_pairs={{1,0},{2,1},{3,2},{5,4},{6,5},{7,6},{9,8},{10,9},{11,10},{13,12},{... | collective-permute-start | bytes 1966088 | tf_op jit(solution)/shard_map/ppermute | solution.py:27
  155.1 17.5 %collective-permute-start.21 = (bf16[2,256,640]{2,1,0:T(8,128)(2,1)S(1)}, bf16[2,256,640]{2,1,0:T(8,128)(2,1)}, u32[]{:S(2)}, u32[]{:S(2)}) collective-permute-start(bf16[2,256,640]{2,1,0:T(8,128)(2,1)S(1)} %bitcast.90), channel_id=1, source_target_pairs={{0,1},{1,2},{2,3},{4,5},{5,6},{6,7},{8,9},{9,10},{10,11},{12,13},{... | collective-permute-start | bytes 1966088 | tf_op jit(solution)/shard_map/ppermute | solution.py:26
  211.0 18.1 %collective-permute-start.25 = (bf16[4,560,640]{2,1,0:T(8,128)(2,1)}, bf16[4,560,640]{2,1,0:T(8,128)(2,1)S(1)}, u32[]{:S(2)}, u32[]{:S(2)}) collective-permute-start(bf16[4,560,640]{2,1,0:T(8,128)(2,1)} %get-tuple-element.191), channel_id=1, source_target_pairs={{0,4},{4,0},{8,12},{12,8},{16,20},{20,16},{24,28},{28,24},{1,5},{5... | collective-permute-start | bytes 8601608 | tf_op jit(solution)/shard_map/ppermute | solution.py:884
  232.4 27.9 %collective-permute-start.29 = (bf16[2,464,640]{2,1,0:T(8,128)(2,1)}, bf16[2,464,640]{2,1,0:T(8,128)(2,1)S(1)}, u32[]{:S(2)}, u32[]{:S(2)}) collective-permute-start(bf16[2,464,640]{2,1,0:T(8,128)(2,1)} %get-tuple-element.203), channel_id=1, source_target_pairs={{0,16},{4,20},{8,24},{12,28},{16,0},{20,4},{24,8},{28,12},{1,17},{... | collective-permute-start | bytes 3563528 | tf_op jit(solution)/shard_map/ppermute | solution.py:884
  233.5 26.7 %collective-permute-start.28 = (bf16[2,448,640]{2,1,0:T(8,128)(2,1)}, bf16[2,448,640]{2,1,0:T(8,128)(2,1)}, u32[]{:S(2)}, u32[]{:S(2)}) collective-permute-start(bf16[2,448,640]{2,1,0:T(8,128)(2,1)} %get-tuple-element.201), channel_id=1, source_target_pairs={{0,8},{4,12},{8,0},{12,4},{16,24},{20,28},{24,16},{28,20},{1,9},{5... | collective-permute-start | bytes 3440648 | tf_op jit(solution)/shard_map/ppermute | solution.py:884
  238.4 21.9 %collective-permute-start.32 = (bf16[144,640]{1,0:T(8,128)(2,1)S(1)}, bf16[144,640]{1,0:T(8,128)(2,1)S(1)}, u32[]{:S(2)}, u32[]{:S(2)}) collective-permute-start(bf16[144,640]{1,0:T(8,128)(2,1)S(1)} %get-tuple-element.236), channel_id=1, source_target_pairs={{0,3},{1,0},{2,1},{3,2},{4,7},{5,4},{6,5},{7,6},{8,11},{9,8},{10,9... | collective-permute-start | bytes 552968 | tf_op jit(solution)/shard_map/ppermute | solution.py:902
  238.7 21.6 %collective-permute-start.31 = (bf16[144,640]{1,0:T(8,128)(2,1)S(1)}, bf16[144,640]{1,0:T(8,128)(2,1)S(1)}, u32[]{:S(2)}, u32[]{:S(2)}) collective-permute-start(bf16[144,640]{1,0:T(8,128)(2,1)S(1)} %get-tuple-element.237), channel_id=1, source_target_pairs={{0,2},{1,3},{2,0},{3,1},{4,6},{5,7},{6,4},{7,5},{8,10},{9,11},{10,... | collective-permute-start | bytes 552968 | tf_op jit(solution)/shard_map/ppermute | solution.py:902
  242.2 18.1 %collective-permute-start.30 = (bf16[144,640]{1,0:T(8,128)(2,1)S(1)}, bf16[144,640]{1,0:T(8,128)(2,1)S(1)}, u32[]{:S(2)}, u32[]{:S(2)}) collective-permute-start(bf16[144,640]{1,0:T(8,128)(2,1)S(1)} %get-tuple-element.238), channel_id=1, source_target_pairs={{0,1},{1,2},{2,3},{3,0},{4,5},{5,6},{6,7},{7,4},{8,9},{9,10},{10,1... | collective-permute-start | bytes 552968 | tf_op jit(solution)/shard_map/ppermute | solution.py:902
  262.1 14.4 %collective-permute-start.34 = (bf16[464,640]{1,0:T(8,128)(2,1)S(1)}, bf16[464,640]{1,0:T(8,128)(2,1)S(1)}, u32[]{:S(2)}, u32[]{:S(2)}) collective-permute-start(bf16[464,640]{1,0:T(8,128)(2,1)S(1)} %get-tuple-element.213), channel_id=1, source_target_pairs={{0,8},{4,12},{8,0},{12,4},{16,24},{20,28},{24,16},{28,20},{1,9},{5... | collective-permute-start | bytes 1781768 | tf_op jit(solution)/shard_map/ppermute | solution.py:884
  278.2 24.2 %collective-permute-start.36 = (bf16[240,640]{1,0:T(8,128)(2,1)S(1)}, bf16[240,640]{1,0:T(8,128)(2,1)S(1)}, u32[]{:S(2)}, u32[]{:S(2)}) collective-permute-start(bf16[240,640]{1,0:T(8,128)(2,1)S(1)} %get-tuple-element.233), channel_id=1, source_target_pairs={{0,2},{1,3},{2,0},{3,1},{4,6},{5,7},{6,4},{7,5},{8,10},{9,11},{10,... | collective-permute-start | bytes 921608 | tf_op jit(solution)/shard_map/ppermute | solution.py:902
  281.4 25.8 %collective-permute-start.35 = (bf16[240,640]{1,0:T(8,128)(2,1)S(1)}, bf16[240,640]{1,0:T(8,128)(2,1)S(1)}, u32[]{:S(2)}, u32[]{:S(2)}) collective-permute-start(bf16[240,640]{1,0:T(8,128)(2,1)S(1)} %get-tuple-element.234), channel_id=1, source_target_pairs={{0,1},{1,2},{2,3},{3,0},{4,5},{5,6},{6,7},{7,4},{8,9},{9,10},{10,1... | collective-permute-start | bytes 921608 | tf_op jit(solution)/shard_map/ppermute | solution.py:902
  (78 other events, 476.1 us)
Sparse Core Ops, SparseCore 0:
  45.8 44.5 all-gather.4
  92.8 43.7 all-gather.6
  172.8 63.4 reduce-scatter.1

commit v3 on v2

--- a/solution.py
+++ b/solution.py
@@ -35,7 +35,8 @@
 
 
 def gelu(h):
-    return 0.5 * h * (1.0 + jnp.tanh(SLOPE * (h + CUBIC * (h * h * h))))
+    half = 0.5 * h
+    return half + half * jnp.tanh(h * (SLOPE + (SLOPE * CUBIC) * (h * h)))
 
 
 def norm_gelu(values, gain_vector, bias_vector):
@@ -46,8 +47,9 @@
     n, scale = normalized(values)
     h = n * gain_vector + bias_vector
     square = h * h
-    t = jnp.tanh(SLOPE * (h + CUBIC * (square * h)))
-    slope = 0.5 * (1.0 + t) + (0.5 * SLOPE) * h * (1.0 - t * t) * (1.0 + (3.0 * CUBIC) * square)
+    rise = 0.5 + 0.5 * jnp.tanh(h * (SLOPE + (SLOPE * CUBIC) * square))
+    bend = h * (2.0 * SLOPE + (6.0 * SLOPE * CUBIC) * square)
+    slope = rise + (rise - rise * rise) * bend
     dh = incoming * slope
     dn = dh * gain_vector
     back = dn - jnp.mean(dn, -1, keepdims=True) - n * jnp.mean(dn * n, -1, keepdims=True)
@@ -506,7 +508,7 @@
     return pl.CostEstimate(flops=flops, bytes_accessed=width, transcendentals=0)
 
 
-def call(kernel, grid, in_specs, out_specs, out_shape, flops, moved, name, aliases=None, scratch=()):
+def call(kernel, grid, in_specs, out_specs, out_shape, flops, moved, name, aliases=None, scratch=(), room=32):
     return pl.pallas_call(
         kernel,
         grid=(grid,),
@@ -516,7 +518,7 @@
         scratch_shapes=list(scratch),
         input_output_aliases=aliases or {},
         cost_estimate=cost(flops, moved),
-        compiler_params=pltpu.CompilerParams(vmem_limit_bytes=32 * 1024 * 1024),
+        compiler_params=pltpu.CompilerParams(vmem_limit_bytes=room * 1024 * 1024),
         name=name,
     )
 
@@ -714,6 +716,7 @@
         2 * tokens * hidden * (KER * hidden + model),
         16 * tokens * model,
         "conv_back",
+        room=56 if dilation_step == SECOND_DILATION else 32,
     )(
         low,
         gv,
@@ -1091,6 +1094,7 @@
         rest * width,
         8 * rest * width,
         "shard_pack",
+        room=60,
     )(*ins)
 
 

time: 319 us -> 315 us (0.987)
  local copies, waits for them, and re-layouts: 47.1 us -> 37.9 us
  Pallas kernels: 80.7 us -> 86 us
    unnamed x122 -> x116, local copies, waits for them, and re-layouts: 35.6 us -> 28.6 us
    pallas_call x2, Pallas kernels: 19.2 us -> 22.4 us  [conv_back_with(): call(functools.partial(conv_back_kernel, dilation_step), rows, [row_block...]
  transfers between devices with their start and end apart: 41 -> 41, of which waited for: 25 -> 26; matrix products, arithmetic and copies ran while one was open for 5% -> 4% of each run, Pallas kernels for 20% -> 21%
where the time goes in v3:
time: 315 us; the launch traced here: 312 us
  waiting for transfers between devices  117 us (37%)
  Pallas kernels  86 us (27%)
  starting transfers between devices  54.7 us (17%)
  local copies, waits for them, and re-layouts  37.9 us (12%)
  between operations  14.5 us (5%)
    ppermute x15, waiting for transfers between devices, shifted(): lax.ppermute(block, 'seq', [(i, (i + step) % count) for i in range(count)])  55.7 us
    ppermute x15, waiting for transfers between devices, dp_swapped(): return lax.ppermute(block, 'dp', [(i, i ^ 1 << bit) for i in range(count)])  34.9 us
    unnamed x116, local copies, waits for them, and re-layouts  28.6 us
    pallas_call x2, Pallas kernels, conv_back_with(): call(functools.partial(conv_back_kernel, dilation_step), rows, [row_block...  22.4 us
    ppermute x15, starting transfers between devices, dp_swapped(): return lax.ppermute(block, 'dp', [(i, i ^ 1 << bit) for i in range(count)])  16.6 us
    ppermute x15, starting transfers between devices, shifted(): lax.ppermute(block, 'seq', [(i, (i + step) % count) for i in range(count)])  15.3 us
    ppermute x4, waiting for transfers between devices, seq_neighbours(): high = lax.ppermute(block[:, :width], 'seq', backward)  15 us
    pallas_call x2, Pallas kernels, convolve(): call(functools.partial(convolve_kernel, dilation_step), rows, [row_block(...  13.5 us
  transfers between devices with their start and end apart: 41, of which 26 were waited for; matrix products, arithmetic and copies ran while one was open for 4% of the time, Pallas kernels for 21%

profile of v3, /device:TPU:17, one launch (start us, length us, event | category | flops | bytes accessed | tf_op | source)
XLA Modules:
  0.0 312.4 jit_solution(15743516666351081682)
XLA Ops:
  30.3 9.4 %collective-permute-done.6.refs_2_ = bf16[144,640]{1,0:T(8,128)(2,1)S(1)} collective-permute-done((bf16[144,640]{1,0:T(8,128)(2,1)S(1)}, bf16[144,640]{1,0:T(8,128)(2,1)S(1)}, u32[]{:S(2)}, u32[]{:S(2)}) %collective-permute-start.6) | collective-permute-done | bytes 184352 | tf_op jit(solution)/shard_map/ppermute | solution.py:905
  39.7 3.8 %collective-permute-done.5.refs_1_ = bf16[144,640]{1,0:T(8,128)(2,1)S(1)} collective-permute-done((bf16[144,640]{1,0:T(8,128)(2,1)S(1)}, bf16[144,640]{1,0:T(8,128)(2,1)S(1)}, u32[]{:S(2)}, u32[]{:S(2)}) %collective-permute-start.5) | collective-permute-done | bytes 184352 | tf_op jit(solution)/shard_map/ppermute | solution.py:905
  47.9 3.7 %collective-permute-done.12.refs_3_ = bf16[144,640]{1,0:T(8,128)(2,1)S(1)} collective-permute-done((bf16[144,640]{1,0:T(8,128)(2,1)S(1)}, bf16[144,640]{1,0:T(8,128)(2,1)S(1)}, u32[]{:S(2)}, u32[]{:S(2)}) %collective-permute-start.12) | collective-permute-done | bytes 184352 | tf_op jit(solution)/shard_map/ppermute | solution.py:905
  54.9 6.7 %collective-permute-done.11.refs_2_ = bf16[144,640]{1,0:T(8,128)(2,1)S(1)} collective-permute-done((bf16[144,640]{1,0:T(8,128)(2,1)S(1)}, bf16[144,640]{1,0:T(8,128)(2,1)S(1)}, u32[]{:S(2)}, u32[]{:S(2)}) %collective-permute-start.11) | collective-permute-done | bytes 184352 | tf_op jit(solution)/shard_map/ppermute | solution.py:905
  72.5 4.2 %project.2 = (bf16[512,1280]{1,0:T(8,128)(2,1)S(1)}, f32[512,640]{1,0:T(8,128)S(1)}, bf16[512,640]{1,0:T(8,128)(2,1)S(1)}) custom-call(bf16[512,1280]{1,0:T(8,128)(2,1)S(1)} %bitcast.86, bf16[8,352,640]{2,1,0:T(8,128)(2,1)S(1)} %copy-done.4, f32[3,1280]{1,0:T(4,128)S(1)} %reshape.818.wide_ref, f32[6,640]{1,0:T(8,128)S(1)} %reshape.819.narrow_ref), custom_call_target="tpu_custom_call" | custom-call | flops 1677721600 | bytes 7864320 | tf_op jit(solution)/shard_map/project/pallas_call | solution.py:574
  85.2 3.4 %collective-permute-done.18.high_ref = bf16[2,128,640]{2,1,0:T(8,128)(2,1)S(1)} collective-permute-done((bf16[2,128,640]{2,1,0:T(8,128)(2,1)S(1)}, bf16[2,128,640]{2,1,0:T(8,128)(2,1)S(1)}, u32[]{:S(2)}, u32[]{:S(2)}) %collective-permute-start.18) | collective-permute-done | bytes 327712 | tf_op jit(solution)/shard_map/ppermute | solution.py:27
  101.7 6.0 %convolve.2 = (bf16[512,3200]{1,0:T(8,128)(2,1)S(1)}, f32[512,640]{1,0:T(8,128)S(1)}, bf16[512,640]{1,0:T(8,128)(2,1)S(1)}, f32[512,1280]{1,0:T(8,128)S(1)}) custom-call(bf16[2,128,640]{2,1,0:T(8,128)(2,1)S(1)} %copy-done.28, bf16[2,256,640]{2,1,0:T(8,128)(2,1)S(1)} %bitcast.93, bf16[2,128,640]{2,1,0:T(8,128)(2,1)S(1)} %copy-done.26, ...), custom_call_target="tpu_custom_call" | custom-call | flops 2936012800 | bytes 10485760 | tf_op jit(solution)/shard_map/convolve/pallas_call | solution.py:594
  109.5 4.8 %project.3 = (bf16[512,1280]{1,0:T(8,128)(2,1)S(1)}, f32[512,640]{1,0:T(8,128)S(1)}, bf16[512,640]{1,0:T(8,128)(2,1)}) custom-call(f32[512,1280]{1,0:T(8,128)S(1)} %get-tuple-element.136.x_ref, bf16[8,352,640]{2,1,0:T(8,128)(2,1)S(1)} %copy-done.5, f32[3,1280]{1,0:T(4,128)S(1)} %reshape.821.wide_ref, f32[6,640]{1,0:T(8,128)S(1)} %reshape.822.narrow_ref), custom_call_target="tpu_custom_call" | custom-call | flops 1677721600 | bytes 7864320 | tf_op jit(solution)/shard_map/project/pallas_call | solution.py:574
  123.5 9.9 %collective-permute-done.20.high_ref = bf16[2,256,640]{2,1,0:T(8,128)(2,1)} collective-permute-done((bf16[2,256,640]{2,1,0:T(8,128)(2,1)}, bf16[2,256,640]{2,1,0:T(8,128)(2,1)}, u32[]{:S(2)}, u32[]{:S(2)}) %collective-permute-start.20) | collective-permute-done | bytes 655392 | tf_op jit(solution)/shard_map/ppermute | solution.py:27
  139.0 7.6 %convolve.3 = (bf16[512,3200]{1,0:T(8,128)(2,1)S(1)}, f32[512,640]{1,0:T(8,128)S(1)}, bf16[512,640]{1,0:T(8,128)(2,1)S(1)}, bf16[512,1280]{1,0:T(8,128)(2,1)}) custom-call(bf16[2,256,640]{2,1,0:T(8,128)(2,1)} %collective-permute-done.19.low_ref, bf16[2,256,640]{2,1,0:T(8,128)(2,1)} %bitcast.24.own_ref, ...), custom_call_target="tpu_custom_call" | custom-call | flops 2936012800 | bytes 10485760 | tf_op jit(solution)/shard_map/convolve/pallas_call | solution.py:594
  146.6 3.5 %out_back.2 = (bf16[512,1280]{1,0:T(8,128)(2,1)S(1)}, bf16[512,640]{1,0:T(8,128)(2,1)S(1)}, f32[8,640]{1,0:T(8,128)S(1)}, f32[8,1280]{1,0:T(8,128)S(1)}) custom-call(bf16[512,1280]{1,0:T(8,128)(2,1)S(1)} %bitcast.85, f32[512,640]{1,0:T(8,128)S(1)} %get-tuple-element.149.v_ref, bf16[8,560,640]{2,1,0:T(8,128)(2,1)S(1)} %bitcast.82, ...), custom_call_target="tpu_custom_call" | custom-call | flops 1677721600 | bytes 6553600 | tf_op jit(solution)/shard_map/out_back/pallas_call | solution.py:638
  155.4 6.1 %weight_grads.1 = bf16[8,560,640]{2,1,0:T(8,128)(2,1)S(1)} custom-call(bf16[512,3200]{1,0:T(8,128)(2,1)S(1)} %get-tuple-element.148.tap_ref, bf16[512,640]{1,0:T(8,128)(2,1)S(1)} %get-tuple-element.150.gv_ref, bf16[512,640]{1,0:T(8,128)(2,1)S(1)} %get-tuple-element.151.act_three_ref, bf16[512,1280]{1,0:T(8,128)(2,1)S(1)} %get-tuple-element.152.short_ref), custom_call_target="tpu_custom_call" | custom-call | flops 2936012800 | bytes 5242880 | tf_op jit(solution)/shard_map/weight_grads/pallas_call | solution.py:666
  168.5 12.9 %conv_back.2 = (bf16[512,640]{1,0:T(8,128)(2,1)}, f32[512,1280]{1,0:T(8,128)}, f32[8,640]{1,0:T(8,128)}, f32[8,1280]{1,0:T(8,128)}) custom-call(bf16[2,256,640]{2,1,0:T(8,128)(2,1)} %copy-done.48, bf16[2,256,640]{2,1,0:T(8,128)(2,1)} %bitcast.91, bf16[2,256,640]{2,1,0:T(8,128)(2,1)} %copy-done.47, bf16[2,256,8]{2,1,0:T(8,128)(2,1)} %copy-done.20, ...), custom_call_target="tpu_custom_call" | custom-call | flops 2936012800 | bytes 10485760 | tf_op jit(solution)/shard_map/conv_back/pallas_call | solution.py:693
  185.9 3.5 %out_back.3 = (bf16[512,1280]{1,0:T(8,128)(2,1)S(1)}, bf16[512,640]{1,0:T(8,128)(2,1)S(1)}, f32[8,640]{1,0:T(8,128)S(1)}, f32[8,1280]{1,0:T(8,128)S(1)}) custom-call(f32[512,1280]{1,0:T(8,128)S(1)} %copy-done.9, f32[512,640]{1,0:T(8,128)S(1)} %copy-done.16, bf16[8,560,640]{2,1,0:T(8,128)(2,1)S(1)} %bitcast.63, bf16[8,560,640]{2,1,0:T(8,128)(2,1)S(1)} %bitcast.64, ...), custom_call_target="tpu_custom_call" | custom-call | flops 1677721600 | bytes 6553600 | tf_op jit(solution)/shard_map/out_back/pallas_call | solution.py:638
  197.3 7.8 %share_grads.1 = (bf16[4,560,640]{2,1,0:T(8,128)(2,1)S(1)}, bf16[4,560,640]{2,1,0:T(8,128)(2,1)}) custom-call(s32[2]{0:T(128)S(1)} %pad_add_fusion.place_ref, bf16[512,3200]{1,0:T(8,128)(2,1)S(1)} %copy-done.34, bf16[512,640]{1,0:T(8,128)(2,1)S(1)} %get-tuple-element.164.gv_ref, bf16[512,640]{1,0:T(8,128)(2,1)S(1)} %copy-done.38, ...), custom_call_target="tpu_custom_call" | custom-call | flops 2936012800 | bytes 5242880 | tf_op jit(solution)/shard_map/share_grads/pallas_call | solution.py:769
  205.1 4.1 %collective-permute-start.25 = (bf16[4,560,640]{2,1,0:T(8,128)(2,1)}, bf16[4,560,640]{2,1,0:T(8,128)(2,1)S(1)}, u32[]{:S(2)}, u32[]{:S(2)}) collective-permute-start(bf16[4,560,640]{2,1,0:T(8,128)(2,1)} %get-tuple-element.191), channel_id=1, source_target_pairs={{0,4},{4,0},{8,12},{12,8},{16,20},{20,16},{24,28},{28,24},{1,5},{5... | collective-permute-start | bytes 8601608 | tf_op jit(solution)/shard_map/ppermute | solution.py:887
  209.2 9.6 %conv_back.3 = (bf16[512,640]{1,0:T(8,128)(2,1)S(1)}, f32[512,1280]{1,0:T(8,128)}, f32[8,640]{1,0:T(8,128)S(1)}, f32[8,1280]{1,0:T(8,128)S(1)}) custom-call(bf16[2,128,640]{2,1,0:T(8,128)(2,1)S(1)} %collective-permute-done.23.low_ref, bf16[2,256,640]{2,1,0:T(8,128)(2,1)S(1)} %bitcast.95, bf16[2,128,640]{2,1,0:T(8,128)(2,1)S(1)} %collective-permute-done.24.high_ref, ...), custom_call_target="tpu_custom_call" | custom-call | flops 2936012800 | bytes 10485760 | tf_op jit(solution)/shard_map/conv_back/pallas_call | solution.py:693
  230.1 3.5 %reduce-scatter.2.cloned.1.call-done = bf16[1,560,640]{2,1,0:T(8,128)(2,1)} async-done(((bf16[8,560,640]{2,1,0:T(8,128)(2,1)}), bf16[1,560,640]{2,1,0:T(8,128)(2,1)}) %reduce-scatter.2.cloned.1.call-update) | async-done | bytes 716816 | tf_op jit(solution)/shard_map/reduce_scatter | solution.py:1223
  236.0 4.7 %collective-permute-start.31 = (bf16[144,640]{1,0:T(8,128)(2,1)S(1)}, bf16[144,640]{1,0:T(8,128)(2,1)S(1)}, u32[]{:S(2)}, u32[]{:S(2)}) collective-permute-start(bf16[144,640]{1,0:T(8,128)(2,1)S(1)} %get-tuple-element.237), channel_id=1, source_target_pairs={{0,2},{1,3},{2,0},{3,1},{4,6},{5,7},{6,4},{7,5},{8,10},{9,11},{10,... | collective-permute-start | bytes 552968 | tf_op jit(solution)/shard_map/ppermute | solution.py:905
  240.7 14.8 %collective-permute-done.28.got_a = bf16[2,448,640]{2,1,0:T(8,128)(2,1)} collective-permute-done((bf16[2,448,640]{2,1,0:T(8,128)(2,1)}, bf16[2,448,640]{2,1,0:T(8,128)(2,1)}, u32[]{:S(2)}, u32[]{:S(2)}) %collective-permute-start.28) | collective-permute-done | bytes 1146912 | tf_op jit(solution)/shard_map/ppermute | solution.py:887
  260.1 13.6 %collective-permute-done.33.refs_1_ = bf16[448,640]{1,0:T(8,128)(2,1)S(1)} collective-permute-done((bf16[448,640]{1,0:T(8,128)(2,1)S(1)}, bf16[448,640]{1,0:T(8,128)(2,1)S(1)}, u32[]{:S(2)}, u32[]{:S(2)}) %collective-permute-start.33) | collective-permute-done | bytes 573472 | tf_op jit(solution)/shard_map/ppermute | solution.py:887
  278.3 3.7 %collective-permute-done.37.refs_3_ = bf16[240,640]{1,0:T(8,128)(2,1)S(1)} collective-permute-done((bf16[240,640]{1,0:T(8,128)(2,1)S(1)}, bf16[240,640]{1,0:T(8,128)(2,1)S(1)}, u32[]{:S(2)}, u32[]{:S(2)}) %collective-permute-start.37) | collective-permute-done | bytes 307232 | tf_op jit(solution)/shard_map/ppermute | solution.py:905
  282.0 17.8 %collective-permute-done.36.refs_2_ = bf16[240,640]{1,0:T(8,128)(2,1)S(1)} collective-permute-done((bf16[240,640]{1,0:T(8,128)(2,1)S(1)}, bf16[240,640]{1,0:T(8,128)(2,1)S(1)}, u32[]{:S(2)}, u32[]{:S(2)}) %collective-permute-start.36) | collective-permute-done | bytes 307232 | tf_op jit(solution)/shard_map/ppermute | solution.py:905
  299.8 4.7 %collective-permute-done.35.refs_1_ = bf16[240,640]{1,0:T(8,128)(2,1)S(1)} collective-permute-done((bf16[240,640]{1,0:T(8,128)(2,1)S(1)}, bf16[240,640]{1,0:T(8,128)(2,1)S(1)}, u32[]{:S(2)}, u32[]{:S(2)}) %collective-permute-start.35) | collective-permute-done | bytes 307232 | tf_op jit(solution)/shard_map/ppermute | solution.py:905
  (246 shorter events, 128.2 us)
Async XLA Ops:
  7.2 84.6 %all-gather.5.cloned.1.call-start = ((), (), s32[]{:S(2)}) async-start(), calls=%async_computation.2 | async-start | bytes 6451200 | tf_op jit(solution)/shard_map/all_gather | solution.py:1189
  23.1 20.4 %collective-permute-start.4 = (bf16[176,640]{1,0:T(8,128)(2,1)S(1)}, bf16[176,640]{1,0:T(8,128)(2,1)S(1)}, u32[]{:S(2)}, u32[]{:S(2)}) collective-permute-start(bf16[176,640]{1,0:T(8,128)(2,1)S(1)} %get-tuple-element.257), channel_id=1, source_target_pairs={{0,16},{4,20},{8,24},{12,28},{16,0},{20,4},{24,8},{28,12},{1,17},{... | collective-permute-start | bytes 675848 | tf_op jit(solution)/shard_map/ppermute | solution.py:887
  24.4 19.1 %collective-permute-start.3 = (bf16[176,640]{1,0:T(8,128)(2,1)S(1)}, bf16[176,640]{1,0:T(8,128)(2,1)S(1)}, u32[]{:S(2)}, u32[]{:S(2)}) collective-permute-start(bf16[176,640]{1,0:T(8,128)(2,1)S(1)} %get-tuple-element.258), channel_id=1, source_target_pairs={{0,8},{4,12},{8,0},{12,4},{16,24},{20,28},{24,16},{28,20},{1,9},{5... | collective-permute-start | bytes 675848 | tf_op jit(solution)/shard_map/ppermute | solution.py:887
  26.6 17.0 %collective-permute-start.5 = (bf16[144,640]{1,0:T(8,128)(2,1)S(1)}, bf16[144,640]{1,0:T(8,128)(2,1)S(1)}, u32[]{:S(2)}, u32[]{:S(2)}) collective-permute-start(bf16[144,640]{1,0:T(8,128)(2,1)S(1)} %copy-done.31), channel_id=1, source_target_pairs={{0,1},{1,2},{2,3},{3,0},{4,5},{5,6},{6,7},{7,4},{8,9},{9,10},{10,1... | collective-permute-start | bytes 552968 | tf_op jit(solution)/shard_map/ppermute | solution.py:905
  45.5 90.8 %all-gather.7.cloned.1.call-start = ((), (), s32[]{:S(2)}) async-start(), calls=%async_computation.3 | async-start | bytes 6451200 | tf_op jit(solution)/shard_map/all_gather | solution.py:1202
  45.6 18.2 %collective-permute-start.9 = (bf16[2,176,640]{2,1,0:T(8,128)(2,1)S(1)}, bf16[2,176,640]{2,1,0:T(8,128)(2,1)S(1)}, u32[]{:S(2)}, u32[]{:S(2)}) collective-permute-start(bf16[2,176,640]{2,1,0:T(8,128)(2,1)S(1)} %pad_maximum_fusion.1.refs_2_), channel_id=1, source_target_pairs={{0,8},{4,12},{8,0},{12,4},{16,24},{20,28},{24,16},{28,20},{1,9},{5... | collective-permute-start | bytes 1351688 | tf_op jit(solution)/shard_map/ppermute | solution.py:887
  46.0 17.9 %collective-permute-start.8 = (bf16[2,176,640]{2,1,0:T(8,128)(2,1)S(1)}, bf16[2,176,640]{2,1,0:T(8,128)(2,1)S(1)}, u32[]{:S(2)}, u32[]{:S(2)}) collective-permute-start(bf16[2,176,640]{2,1,0:T(8,128)(2,1)S(1)} %pad_maximum_fusion.refs_0_), channel_id=1, source_target_pairs={{0,16},{4,20},{8,24},{12,28},{16,0},{20,4},{24,8},{28,12},{1,17},{... | collective-permute-start | bytes 1351688 | tf_op jit(solution)/shard_map/ppermute | solution.py:887
  46.4 15.2 %collective-permute-start.11 = (bf16[144,640]{1,0:T(8,128)(2,1)S(1)}, bf16[144,640]{1,0:T(8,128)(2,1)S(1)}, u32[]{:S(2)}, u32[]{:S(2)}) collective-permute-start(bf16[144,640]{1,0:T(8,128)(2,1)S(1)} %copy-done.30), channel_id=1, source_target_pairs={{0,2},{1,3},{2,0},{3,1},{4,6},{5,7},{6,4},{7,5},{8,10},{9,11},{10,... | collective-permute-start | bytes 552968 | tf_op jit(solution)/shard_map/ppermute | solution.py:905
  46.4 17.4 %collective-permute-start.10 = (bf16[144,640]{1,0:T(8,128)(2,1)S(1)}, bf16[144,640]{1,0:T(8,128)(2,1)S(1)}, u32[]{:S(2)}, u32[]{:S(2)}) collective-permute-start(bf16[144,640]{1,0:T(8,128)(2,1)S(1)} %copy-done.30), channel_id=1, source_target_pairs={{0,1},{1,2},{2,3},{3,0},{4,5},{5,6},{6,7},{7,4},{8,9},{9,10},{10,1... | collective-permute-start | bytes 552968 | tf_op jit(solution)/shard_map/ppermute | solution.py:905
  91.8 141.7 %reduce-scatter.2.cloned.1.call-start = ((), (), s32[]{:S(2)}) async-start(), calls=%async_computation.1 | async-start | bytes 6451200 | tf_op jit(solution)/shard_map/reduce_scatter | solution.py:1223
  116.4 17.1 %collective-permute-start.20 = (bf16[2,256,640]{2,1,0:T(8,128)(2,1)}, bf16[2,256,640]{2,1,0:T(8,128)(2,1)}, u32[]{:S(2)}, u32[]{:S(2)}) collective-permute-start(bf16[2,256,640]{2,1,0:T(8,128)(2,1)} %bitcast.24.own_ref), channel_id=1, source_target_pairs={{1,0},{2,1},{3,2},{5,4},{6,5},{7,6},{9,8},{10,9},{11,10},{13,12},{... | collective-permute-start | bytes 1966088 | tf_op jit(solution)/shard_map/ppermute | solution.py:27
  119.6 16.6 %collective-permute-start.19 = (bf16[2,256,640]{2,1,0:T(8,128)(2,1)}, bf16[2,256,640]{2,1,0:T(8,128)(2,1)}, u32[]{:S(2)}, u32[]{:S(2)}) collective-permute-start(bf16[2,256,640]{2,1,0:T(8,128)(2,1)} %bitcast.24.own_ref), channel_id=1, source_target_pairs={{0,1},{1,2},{2,3},{4,5},{5,6},{6,7},{8,9},{9,10},{10,11},{12,13},{... | collective-permute-start | bytes 1966088 | tf_op jit(solution)/shard_map/ppermute | solution.py:26
  150.0 15.5 %collective-permute-start.22 = (bf16[2,256,640]{2,1,0:T(8,128)(2,1)S(1)}, bf16[2,256,640]{2,1,0:T(8,128)(2,1)S(1)}, u32[]{:S(2)}, u32[]{:S(2)}) collective-permute-start(bf16[2,256,640]{2,1,0:T(8,128)(2,1)S(1)} %bitcast.89), channel_id=1, source_target_pairs={{1,0},{2,1},{3,2},{5,4},{6,5},{7,6},{9,8},{10,9},{11,10},{13,12},{... | collective-permute-start | bytes 1966088 | tf_op jit(solution)/shard_map/ppermute | solution.py:27
  152.2 15.5 %collective-permute-start.21 = (bf16[2,256,640]{2,1,0:T(8,128)(2,1)S(1)}, bf16[2,256,640]{2,1,0:T(8,128)(2,1)S(1)}, u32[]{:S(2)}, u32[]{:S(2)}) collective-permute-start(bf16[2,256,640]{2,1,0:T(8,128)(2,1)S(1)} %bitcast.90), channel_id=1, source_target_pairs={{0,1},{1,2},{2,3},{4,5},{5,6},{6,7},{8,9},{9,10},{10,11},{12,13},{... | collective-permute-start | bytes 1966088 | tf_op jit(solution)/shard_map/ppermute | solution.py:26
  189.5 15.6 %collective-permute-start.24 = (bf16[2,128,640]{2,1,0:T(8,128)(2,1)S(1)}, bf16[2,128,640]{2,1,0:T(8,128)(2,1)S(1)}, u32[]{:S(2)}, u32[]{:S(2)}) collective-permute-start(bf16[2,128,640]{2,1,0:T(8,128)(2,1)S(1)} %get-tuple-element.240), channel_id=1, source_target_pairs={{1,0},{2,1},{3,2},{5,4},{6,5},{7,6},{9,8},{10,9},{11,10},{13,12},{... | collective-permute-start | bytes 983048 | tf_op jit(solution)/shard_map/ppermute | solution.py:27
  205.1 19.5 %collective-permute-start.25 = (bf16[4,560,640]{2,1,0:T(8,128)(2,1)}, bf16[4,560,640]{2,1,0:T(8,128)(2,1)S(1)}, u32[]{:S(2)}, u32[]{:S(2)}) collective-permute-start(bf16[4,560,640]{2,1,0:T(8,128)(2,1)} %get-tuple-element.191), channel_id=1, source_target_pairs={{0,4},{4,0},{8,12},{12,8},{16,20},{20,16},{24,28},{28,24},{1,5},{5... | collective-permute-start | bytes 8601608 | tf_op jit(solution)/shard_map/ppermute | solution.py:887
  227.8 29.1 %collective-permute-start.29 = (bf16[2,464,640]{2,1,0:T(8,128)(2,1)}, bf16[2,464,640]{2,1,0:T(8,128)(2,1)S(1)}, u32[]{:S(2)}, u32[]{:S(2)}) collective-permute-start(bf16[2,464,640]{2,1,0:T(8,128)(2,1)} %get-tuple-element.203), channel_id=1, source_target_pairs={{0,16},{4,20},{8,24},{12,28},{16,0},{20,4},{24,8},{28,12},{1,17},{... | collective-permute-start | bytes 3563528 | tf_op jit(solution)/shard_map/ppermute | solution.py:887
  228.8 26.7 %collective-permute-start.28 = (bf16[2,448,640]{2,1,0:T(8,128)(2,1)}, bf16[2,448,640]{2,1,0:T(8,128)(2,1)}, u32[]{:S(2)}, u32[]{:S(2)}) collective-permute-start(bf16[2,448,640]{2,1,0:T(8,128)(2,1)} %get-tuple-element.201), channel_id=1, source_target_pairs={{0,8},{4,12},{8,0},{12,4},{16,24},{20,28},{24,16},{28,20},{1,9},{5... | collective-permute-start | bytes 3440648 | tf_op jit(solution)/shard_map/ppermute | solution.py:887
  235.7 21.2 %collective-permute-start.32 = (bf16[144,640]{1,0:T(8,128)(2,1)S(1)}, bf16[144,640]{1,0:T(8,128)(2,1)S(1)}, u32[]{:S(2)}, u32[]{:S(2)}) collective-permute-start(bf16[144,640]{1,0:T(8,128)(2,1)S(1)} %get-tuple-element.236), channel_id=1, source_target_pairs={{0,3},{1,0},{2,1},{3,2},{4,7},{5,4},{6,5},{7,6},{8,11},{9,8},{10,9... | collective-permute-start | bytes 552968 | tf_op jit(solution)/shard_map/ppermute | solution.py:905
  236.0 20.9 %collective-permute-start.31 = (bf16[144,640]{1,0:T(8,128)(2,1)S(1)}, bf16[144,640]{1,0:T(8,128)(2,1)S(1)}, u32[]{:S(2)}, u32[]{:S(2)}) collective-permute-start(bf16[144,640]{1,0:T(8,128)(2,1)S(1)} %get-tuple-element.237), channel_id=1, source_target_pairs={{0,2},{1,3},{2,0},{3,1},{4,6},{5,7},{6,4},{7,5},{8,10},{9,11},{10,... | collective-permute-start | bytes 552968 | tf_op jit(solution)/shard_map/ppermute | solution.py:905
  240.7 16.2 %collective-permute-start.30 = (bf16[144,640]{1,0:T(8,128)(2,1)S(1)}, bf16[144,640]{1,0:T(8,128)(2,1)S(1)}, u32[]{:S(2)}, u32[]{:S(2)}) collective-permute-start(bf16[144,640]{1,0:T(8,128)(2,1)S(1)} %get-tuple-element.238), channel_id=1, source_target_pairs={{0,1},{1,2},{2,3},{3,0},{4,5},{5,6},{6,7},{7,4},{8,9},{9,10},{10,1... | collective-permute-start | bytes 552968 | tf_op jit(solution)/shard_map/ppermute | solution.py:905
  258.8 14.9 %collective-permute-start.34 = (bf16[464,640]{1,0:T(8,128)(2,1)S(1)}, bf16[464,640]{1,0:T(8,128)(2,1)S(1)}, u32[]{:S(2)}, u32[]{:S(2)}) collective-permute-start(bf16[464,640]{1,0:T(8,128)(2,1)S(1)} %get-tuple-element.213), channel_id=1, source_target_pairs={{0,8},{4,12},{8,0},{12,4},{16,24},{20,28},{24,16},{28,20},{1,9},{5... | collective-permute-start | bytes 1781768 | tf_op jit(solution)/shard_map/ppermute | solution.py:887
  275.3 24.5 %collective-permute-start.36 = (bf16[240,640]{1,0:T(8,128)(2,1)S(1)}, bf16[240,640]{1,0:T(8,128)(2,1)S(1)}, u32[]{:S(2)}, u32[]{:S(2)}) collective-permute-start(bf16[240,640]{1,0:T(8,128)(2,1)S(1)} %get-tuple-element.233), channel_id=1, source_target_pairs={{0,2},{1,3},{2,0},{3,1},{4,6},{5,7},{6,4},{7,5},{8,10},{9,11},{10,... | collective-permute-start | bytes 921608 | tf_op jit(solution)/shard_map/ppermute | solution.py:905
  278.3 26.2 %collective-permute-start.35 = (bf16[240,640]{1,0:T(8,128)(2,1)S(1)}, bf16[240,640]{1,0:T(8,128)(2,1)S(1)}, u32[]{:S(2)}, u32[]{:S(2)}) collective-permute-start(bf16[240,640]{1,0:T(8,128)(2,1)S(1)} %get-tuple-element.234), channel_id=1, source_target_pairs={{0,1},{1,2},{2,3},{3,0},{4,5},{5,6},{6,7},{7,4},{8,9},{9,10},{10,1... | collective-permute-start | bytes 921608 | tf_op jit(solution)/shard_map/ppermute | solution.py:905
  (75 other events, 597.2 us)
Sparse Core Ops, SparseCore 0:
  45.7 44.5 all-gather.4
  92.7 43.6 all-gather.6
  167.9 65.6 reduce-scatter.1

commit v4 on v3

--- a/solution.py
+++ b/solution.py
@@ -570,7 +570,7 @@
 def project(inputs, weights):
     tokens, model = inputs.shape
     hidden = weights.hidden
-    tile = min(128, tokens)
+    tile = min(256, tokens)
     return call(
         project_kernel,
         tokens // tile,
@@ -634,7 +634,7 @@
 def out_back(upstream, conv_out, weights):
     tokens, model = upstream.shape
     hidden = weights.hidden
-    tile = min(128, tokens)
+    tile = min(256, tokens)
     return call(
         out_back_kernel,
         tokens // tile,

time: 315 us -> 319 us (1.013)
  the two profiles are of different devices: /device:TPU:17 before, /device:TPU:0 now
where the time goes in v4:
time: 319 us; the launch traced here: 313 us
  waiting for transfers between devices  116 us (36%)
  Pallas kernels  82.9 us (26%)
  starting transfers between devices  59.9 us (19%)
  local copies, waits for them, and re-layouts  37.6 us (12%)
  between operations  15 us (5%)
    ppermute x15, waiting for transfers between devices, shifted(): lax.ppermute(block, 'seq', [(i, (i + step) % count) for i in range(count)])  53.8 us
    ppermute x15, waiting for transfers between devices, dp_swapped(): return lax.ppermute(block, 'dp', [(i, i ^ 1 << bit) for i in range(count)])  34.6 us
    unnamed x116, local copies, waits for them, and re-layouts  28.3 us
    ppermute x15, starting transfers between devices, shifted(): lax.ppermute(block, 'seq', [(i, (i + step) % count) for i in range(count)])  23.3 us
    pallas_call x2, Pallas kernels, conv_back_with(): call(functools.partial(conv_back_kernel, dilation_step), rows, [row_block...  22.4 us
    ppermute x4, starting transfers between devices, seq_neighbours(): low = lax.ppermute(block[:, block.shape[1] - width:], 'seq', forward)  21 us
    ppermute x4, waiting for transfers between devices, seq_neighbours(): high = lax.ppermute(block[:, :width], 'seq', backward)  17.9 us
    pallas_call x2, Pallas kernels, convolve(): call(functools.partial(convolve_kernel, dilation_step), rows, [row_block(...  13.5 us
  transfers between devices with their start and end apart: 41, of which 22 were waited for; matrix products, arithmetic and copies ran while one was open for 4% of the time, Pallas kernels for 20%

profile of v4, /device:TPU:0, one launch (start us, length us, event | category | flops | bytes accessed | tf_op | source)
XLA Modules:
  0.0 312.9 jit_solution(4306251505088312095)
XLA Ops:
  9.3 5.0 %collective-permute-start.2 = (bf16[80,640]{1,0:T(8,128)(2,1)}, bf16[80,640]{1,0:T(8,128)(2,1)S(1)}, u32[]{:S(2)}, u32[]{:S(2)}) collective-permute-start(bf16[80,640]{1,0:T(8,128)(2,1)} %get-tuple-element.122.refs_0_), channel_id=1, source_target_pairs={{0,3},{1,0},{2,1},{3,2},{4,7},{5,4},{6,5},{7,6},{8,11},{9,8},{10,9... | collective-permute-start | bytes 307208 | tf_op jit(solution)/shard_map/ppermute | solution.py:905
  35.6 10.6 %collective-permute-done.6.refs_2_ = bf16[144,640]{1,0:T(8,128)(2,1)S(1)} collective-permute-done((bf16[144,640]{1,0:T(8,128)(2,1)S(1)}, bf16[144,640]{1,0:T(8,128)(2,1)S(1)}, u32[]{:S(2)}, u32[]{:S(2)}) %collective-permute-start.6) | collective-permute-done | bytes 184352 | tf_op jit(solution)/shard_map/ppermute | solution.py:905
  55.7 11.3 %collective-permute-done.11.refs_2_ = bf16[144,640]{1,0:T(8,128)(2,1)S(1)} collective-permute-done((bf16[144,640]{1,0:T(8,128)(2,1)S(1)}, bf16[144,640]{1,0:T(8,128)(2,1)S(1)}, u32[]{:S(2)}, u32[]{:S(2)}) %collective-permute-start.11) | collective-permute-done | bytes 184352 | tf_op jit(solution)/shard_map/ppermute | solution.py:905
  81.8 4.6 %collective-permute-start.17 = (bf16[2,128,640]{2,1,0:T(8,128)(2,1)S(1)}, bf16[2,128,640]{2,1,0:T(8,128)(2,1)S(1)}, u32[]{:S(2)}, u32[]{:S(2)}) collective-permute-start(bf16[2,128,640]{2,1,0:T(8,128)(2,1)S(1)} %get-tuple-element.247), channel_id=1, source_target_pairs={{0,1},{1,2},{2,3},{4,5},{5,6},{6,7},{8,9},{9,10},{10,11},{12,13},{... | collective-permute-start | bytes 983048 | tf_op jit(solution)/shard_map/ppermute | solution.py:26
  88.3 3.8 %collective-permute-done.18.high_ref = bf16[2,128,640]{2,1,0:T(8,128)(2,1)S(1)} collective-permute-done((bf16[2,128,640]{2,1,0:T(8,128)(2,1)S(1)}, bf16[2,128,640]{2,1,0:T(8,128)(2,1)S(1)}, u32[]{:S(2)}, u32[]{:S(2)}) %collective-permute-start.18) | collective-permute-done | bytes 327712 | tf_op jit(solution)/shard_map/ppermute | solution.py:27
  103.4 6.0 %convolve.2 = (bf16[512,3200]{1,0:T(8,128)(2,1)S(1)}, f32[512,640]{1,0:T(8,128)S(1)}, bf16[512,640]{1,0:T(8,128)(2,1)S(1)}, f32[512,1280]{1,0:T(8,128)S(1)}) custom-call(bf16[2,128,640]{2,1,0:T(8,128)(2,1)S(1)} %copy-done.28, bf16[2,256,640]{2,1,0:T(8,128)(2,1)S(1)} %bitcast.93, bf16[2,128,640]{2,1,0:T(8,128)(2,1)S(1)} %copy-done.26, ...), custom_call_target="tpu_custom_call" | custom-call | flops 2936012800 | bytes 10485760 | tf_op jit(solution)/shard_map/convolve/pallas_call | solution.py:594
  111.2 3.9 %project.3 = (bf16[512,1280]{1,0:T(8,128)(2,1)S(1)}, f32[512,640]{1,0:T(8,128)S(1)}, bf16[512,640]{1,0:T(8,128)(2,1)}) custom-call(f32[512,1280]{1,0:T(8,128)S(1)} %get-tuple-element.136.x_ref, bf16[8,352,640]{2,1,0:T(8,128)(2,1)S(1)} %copy-done.5, f32[3,1280]{1,0:T(4,128)S(1)} %reshape.821.wide_ref, f32[6,640]{1,0:T(8,128)S(1)} %reshape.822.narrow_ref), custom_call_target="tpu_custom_call" | custom-call | flops 1677721600 | bytes 7864320 | tf_op jit(solution)/shard_map/project/pallas_call | solution.py:574
  118.6 6.0 %collective-permute-start.19 = (bf16[2,256,640]{2,1,0:T(8,128)(2,1)}, bf16[2,256,640]{2,1,0:T(8,128)(2,1)}, u32[]{:S(2)}, u32[]{:S(2)}) collective-permute-start(bf16[2,256,640]{2,1,0:T(8,128)(2,1)} %bitcast.24.own_ref), channel_id=1, source_target_pairs={{0,1},{1,2},{2,3},{4,5},{5,6},{6,7},{8,9},{9,10},{10,11},{12,13},{... | collective-permute-start | bytes 1966088 | tf_op jit(solution)/shard_map/ppermute | solution.py:26
  125.4 10.4 %collective-permute-done.20.high_ref = bf16[2,256,640]{2,1,0:T(8,128)(2,1)} collective-permute-done((bf16[2,256,640]{2,1,0:T(8,128)(2,1)}, bf16[2,256,640]{2,1,0:T(8,128)(2,1)}, u32[]{:S(2)}, u32[]{:S(2)}) %collective-permute-start.20) | collective-permute-done | bytes 655392 | tf_op jit(solution)/shard_map/ppermute | solution.py:27
  139.7 7.6 %convolve.3 = (bf16[512,3200]{1,0:T(8,128)(2,1)S(1)}, f32[512,640]{1,0:T(8,128)S(1)}, bf16[512,640]{1,0:T(8,128)(2,1)S(1)}, bf16[512,1280]{1,0:T(8,128)(2,1)}) custom-call(bf16[2,256,640]{2,1,0:T(8,128)(2,1)} %collective-permute-done.19.low_ref, bf16[2,256,640]{2,1,0:T(8,128)(2,1)} %bitcast.24.own_ref, ...), custom_call_target="tpu_custom_call" | custom-call | flops 2936012800 | bytes 10485760 | tf_op jit(solution)/shard_map/convolve/pallas_call | solution.py:594
  151.4 5.2 %collective-permute-start.21 = (bf16[2,256,640]{2,1,0:T(8,128)(2,1)S(1)}, bf16[2,256,640]{2,1,0:T(8,128)(2,1)S(1)}, u32[]{:S(2)}, u32[]{:S(2)}) collective-permute-start(bf16[2,256,640]{2,1,0:T(8,128)(2,1)S(1)} %bitcast.90), channel_id=1, source_target_pairs={{0,1},{1,2},{2,3},{4,5},{5,6},{6,7},{8,9},{9,10},{10,11},{12,13},{... | collective-permute-start | bytes 1966088 | tf_op jit(solution)/shard_map/ppermute | solution.py:26
  156.6 6.1 %weight_grads.1 = bf16[8,560,640]{2,1,0:T(8,128)(2,1)S(1)} custom-call(bf16[512,3200]{1,0:T(8,128)(2,1)S(1)} %get-tuple-element.148.tap_ref, bf16[512,640]{1,0:T(8,128)(2,1)S(1)} %get-tuple-element.150.gv_ref, bf16[512,640]{1,0:T(8,128)(2,1)S(1)} %get-tuple-element.151.act_three_ref, bf16[512,1280]{1,0:T(8,128)(2,1)S(1)} %get-tuple-element.152.short_ref), custom_call_target="tpu_custom_call" | custom-call | flops 2936012800 | bytes 5242880 | tf_op jit(solution)/shard_map/weight_grads/pallas_call | solution.py:666
  165.2 3.7 %collective-permute-done.22.high_ref = bf16[2,256,640]{2,1,0:T(8,128)(2,1)S(1)} collective-permute-done((bf16[2,256,640]{2,1,0:T(8,128)(2,1)S(1)}, bf16[2,256,640]{2,1,0:T(8,128)(2,1)S(1)}, u32[]{:S(2)}, u32[]{:S(2)}) %collective-permute-start.22) | collective-permute-done | bytes 655392 | tf_op jit(solution)/shard_map/ppermute | solution.py:27
  170.9 12.9 %conv_back.2 = (bf16[512,640]{1,0:T(8,128)(2,1)}, f32[512,1280]{1,0:T(8,128)}, f32[8,640]{1,0:T(8,128)}, f32[8,1280]{1,0:T(8,128)}) custom-call(bf16[2,256,640]{2,1,0:T(8,128)(2,1)} %copy-done.48, bf16[2,256,640]{2,1,0:T(8,128)(2,1)} %bitcast.91, bf16[2,256,640]{2,1,0:T(8,128)(2,1)} %copy-done.47, bf16[2,256,8]{2,1,0:T(8,128)(2,1)} %copy-done.20, ...), custom_call_target="tpu_custom_call" | custom-call | flops 2936012800 | bytes 10485760 | tf_op jit(solution)/shard_map/conv_back/pallas_call | solution.py:693
  192.8 5.2 %collective-permute-start.23 = (bf16[2,128,640]{2,1,0:T(8,128)(2,1)S(1)}, bf16[2,128,640]{2,1,0:T(8,128)(2,1)S(1)}, u32[]{:S(2)}, u32[]{:S(2)}) collective-permute-start(bf16[2,128,640]{2,1,0:T(8,128)(2,1)S(1)} %get-tuple-element.241), channel_id=1, source_target_pairs={{0,1},{1,2},{2,3},{4,5},{5,6},{6,7},{8,9},{9,10},{10,11},{12,13},{... | collective-permute-start | bytes 983048 | tf_op jit(solution)/shard_map/ppermute | solution.py:26
  200.0 7.8 %share_grads.1 = (bf16[4,560,640]{2,1,0:T(8,128)(2,1)S(1)}, bf16[4,560,640]{2,1,0:T(8,128)(2,1)}) custom-call(s32[2]{0:T(128)S(1)} %pad_add_fusion.place_ref, bf16[512,3200]{1,0:T(8,128)(2,1)S(1)} %copy-done.34, bf16[512,640]{1,0:T(8,128)(2,1)S(1)} %get-tuple-element.164.gv_ref, bf16[512,640]{1,0:T(8,128)(2,1)S(1)} %copy-done.38, ...), custom_call_target="tpu_custom_call" | custom-call | flops 2936012800 | bytes 5242880 | tf_op jit(solution)/shard_map/share_grads/pallas_call | solution.py:769
  207.8 9.6 %conv_back.3 = (bf16[512,640]{1,0:T(8,128)(2,1)S(1)}, f32[512,1280]{1,0:T(8,128)}, f32[8,640]{1,0:T(8,128)S(1)}, f32[8,1280]{1,0:T(8,128)S(1)}) custom-call(bf16[2,128,640]{2,1,0:T(8,128)(2,1)S(1)} %collective-permute-done.23.low_ref, bf16[2,256,640]{2,1,0:T(8,128)(2,1)S(1)} %bitcast.95, bf16[2,128,640]{2,1,0:T(8,128)(2,1)S(1)} %collective-permute-done.24.high_ref, ...), custom_call_target="tpu_custom_call" | custom-call | flops 2936012800 | bytes 10485760 | tf_op jit(solution)/shard_map/conv_back/pallas_call | solution.py:693
  228.8 5.6 %reduce-scatter.2.cloned.1.call-done = bf16[1,560,640]{2,1,0:T(8,128)(2,1)} async-done(((bf16[8,560,640]{2,1,0:T(8,128)(2,1)}), bf16[1,560,640]{2,1,0:T(8,128)(2,1)}) %reduce-scatter.2.cloned.1.call-update) | async-done | bytes 716816 | tf_op jit(solution)/shard_map/reduce_scatter | solution.py:1223
  236.5 4.6 %collective-permute-start.32 = (bf16[144,640]{1,0:T(8,128)(2,1)S(1)}, bf16[144,640]{1,0:T(8,128)(2,1)S(1)}, u32[]{:S(2)}, u32[]{:S(2)}) collective-permute-start(bf16[144,640]{1,0:T(8,128)(2,1)S(1)} %get-tuple-element.236), channel_id=1, source_target_pairs={{0,3},{1,0},{2,1},{3,2},{4,7},{5,4},{6,5},{7,6},{8,11},{9,8},{10,9... | collective-permute-start | bytes 552968 | tf_op jit(solution)/shard_map/ppermute | solution.py:905
  241.7 14.2 %collective-permute-done.28.got_a = bf16[2,448,640]{2,1,0:T(8,128)(2,1)} collective-permute-done((bf16[2,448,640]{2,1,0:T(8,128)(2,1)}, bf16[2,448,640]{2,1,0:T(8,128)(2,1)}, u32[]{:S(2)}, u32[]{:S(2)}) %collective-permute-start.28) | collective-permute-done | bytes 1146912 | tf_op jit(solution)/shard_map/ppermute | solution.py:887
  260.6 14.0 %collective-permute-done.33.refs_1_ = bf16[448,640]{1,0:T(8,128)(2,1)S(1)} collective-permute-done((bf16[448,640]{1,0:T(8,128)(2,1)S(1)}, bf16[448,640]{1,0:T(8,128)(2,1)S(1)}, u32[]{:S(2)}, u32[]{:S(2)}) %collective-permute-start.33) | collective-permute-done | bytes 573472 | tf_op jit(solution)/shard_map/ppermute | solution.py:887
  275.9 3.4 %collective-permute-start.37 = (bf16[240,640]{1,0:T(8,128)(2,1)S(1)}, bf16[240,640]{1,0:T(8,128)(2,1)S(1)}, u32[]{:S(2)}, u32[]{:S(2)}) collective-permute-start(bf16[240,640]{1,0:T(8,128)(2,1)S(1)} %get-tuple-element.232), channel_id=1, source_target_pairs={{0,3},{1,0},{2,1},{3,2},{4,7},{5,4},{6,5},{7,6},{8,11},{9,8},{10,9... | collective-permute-start | bytes 921608 | tf_op jit(solution)/shard_map/ppermute | solution.py:905
  280.3 6.7 %collective-permute-done.37.refs_3_ = bf16[240,640]{1,0:T(8,128)(2,1)S(1)} collective-permute-done((bf16[240,640]{1,0:T(8,128)(2,1)S(1)}, bf16[240,640]{1,0:T(8,128)(2,1)S(1)}, u32[]{:S(2)}, u32[]{:S(2)}) %collective-permute-start.37) | collective-permute-done | bytes 307232 | tf_op jit(solution)/shard_map/ppermute | solution.py:905
  287.0 17.5 %collective-permute-done.36.refs_2_ = bf16[240,640]{1,0:T(8,128)(2,1)S(1)} collective-permute-done((bf16[240,640]{1,0:T(8,128)(2,1)S(1)}, bf16[240,640]{1,0:T(8,128)(2,1)S(1)}, u32[]{:S(2)}, u32[]{:S(2)}) %collective-permute-start.36) | collective-permute-done | bytes 307232 | tf_op jit(solution)/shard_map/ppermute | solution.py:905
  (246 shorter events, 112.4 us)
Async XLA Ops:
  7.2 86.1 %all-gather.5.cloned.1.call-start = ((), (), s32[]{:S(2)}) async-start(), calls=%async_computation.2 | async-start | bytes 6451200 | tf_op jit(solution)/shard_map/all_gather | solution.py:1189
  25.5 20.7 %collective-permute-start.4 = (bf16[176,640]{1,0:T(8,128)(2,1)S(1)}, bf16[176,640]{1,0:T(8,128)(2,1)S(1)}, u32[]{:S(2)}, u32[]{:S(2)}) collective-permute-start(bf16[176,640]{1,0:T(8,128)(2,1)S(1)} %get-tuple-element.257), channel_id=1, source_target_pairs={{0,16},{4,20},{8,24},{12,28},{16,0},{20,4},{24,8},{28,12},{1,17},{... | collective-permute-start | bytes 675848 | tf_op jit(solution)/shard_map/ppermute | solution.py:887
  27.0 19.1 %collective-permute-start.3 = (bf16[176,640]{1,0:T(8,128)(2,1)S(1)}, bf16[176,640]{1,0:T(8,128)(2,1)S(1)}, u32[]{:S(2)}, u32[]{:S(2)}) collective-permute-start(bf16[176,640]{1,0:T(8,128)(2,1)S(1)} %get-tuple-element.258), channel_id=1, source_target_pairs={{0,8},{4,12},{8,0},{12,4},{16,24},{20,28},{24,16},{28,20},{1,9},{5... | collective-permute-start | bytes 675848 | tf_op jit(solution)/shard_map/ppermute | solution.py:887
  30.4 15.7 %collective-permute-start.6 = (bf16[144,640]{1,0:T(8,128)(2,1)S(1)}, bf16[144,640]{1,0:T(8,128)(2,1)S(1)}, u32[]{:S(2)}, u32[]{:S(2)}) collective-permute-start(bf16[144,640]{1,0:T(8,128)(2,1)S(1)} %copy-done.31), channel_id=1, source_target_pairs={{0,2},{1,3},{2,0},{3,1},{4,6},{5,7},{6,4},{7,5},{8,10},{9,11},{10,... | collective-permute-start | bytes 552968 | tf_op jit(solution)/shard_map/ppermute | solution.py:905
  48.2 88.9 %all-gather.7.cloned.1.call-start = ((), (), s32[]{:S(2)}) async-start(), calls=%async_computation.3 | async-start | bytes 6451200 | tf_op jit(solution)/shard_map/all_gather | solution.py:1202
  48.3 18.7 %collective-permute-start.9 = (bf16[2,176,640]{2,1,0:T(8,128)(2,1)S(1)}, bf16[2,176,640]{2,1,0:T(8,128)(2,1)S(1)}, u32[]{:S(2)}, u32[]{:S(2)}) collective-permute-start(bf16[2,176,640]{2,1,0:T(8,128)(2,1)S(1)} %pad_maximum_fusion.1.refs_2_), channel_id=1, source_target_pairs={{0,8},{4,12},{8,0},{12,4},{16,24},{20,28},{24,16},{28,20},{1,9},{5... | collective-permute-start | bytes 1351688 | tf_op jit(solution)/shard_map/ppermute | solution.py:887
  48.9 18.0 %collective-permute-start.8 = (bf16[2,176,640]{2,1,0:T(8,128)(2,1)S(1)}, bf16[2,176,640]{2,1,0:T(8,128)(2,1)S(1)}, u32[]{:S(2)}, u32[]{:S(2)}) collective-permute-start(bf16[2,176,640]{2,1,0:T(8,128)(2,1)S(1)} %pad_maximum_fusion.refs_0_), channel_id=1, source_target_pairs={{0,16},{4,20},{8,24},{12,28},{16,0},{20,4},{24,8},{28,12},{1,17},{... | collective-permute-start | bytes 1351688 | tf_op jit(solution)/shard_map/ppermute | solution.py:887
  49.5 17.4 %collective-permute-start.11 = (bf16[144,640]{1,0:T(8,128)(2,1)S(1)}, bf16[144,640]{1,0:T(8,128)(2,1)S(1)}, u32[]{:S(2)}, u32[]{:S(2)}) collective-permute-start(bf16[144,640]{1,0:T(8,128)(2,1)S(1)} %copy-done.30), channel_id=1, source_target_pairs={{0,2},{1,3},{2,0},{3,1},{4,6},{5,7},{6,4},{7,5},{8,10},{9,11},{10,... | collective-permute-start | bytes 552968 | tf_op jit(solution)/shard_map/ppermute | solution.py:905
  50.7 16.2 %collective-permute-start.10 = (bf16[144,640]{1,0:T(8,128)(2,1)S(1)}, bf16[144,640]{1,0:T(8,128)(2,1)S(1)}, u32[]{:S(2)}, u32[]{:S(2)}) collective-permute-start(bf16[144,640]{1,0:T(8,128)(2,1)S(1)} %copy-done.30), channel_id=1, source_target_pairs={{0,1},{1,2},{2,3},{3,0},{4,5},{5,6},{6,7},{7,4},{8,9},{9,10},{10,1... | collective-permute-start | bytes 552968 | tf_op jit(solution)/shard_map/ppermute | solution.py:905
  93.3 141.1 %reduce-scatter.2.cloned.1.call-start = ((), (), s32[]{:S(2)}) async-start(), calls=%async_computation.1 | async-start | bytes 6451200 | tf_op jit(solution)/shard_map/reduce_scatter | solution.py:1223
  117.3 18.6 %collective-permute-start.20 = (bf16[2,256,640]{2,1,0:T(8,128)(2,1)}, bf16[2,256,640]{2,1,0:T(8,128)(2,1)}, u32[]{:S(2)}, u32[]{:S(2)}) collective-permute-start(bf16[2,256,640]{2,1,0:T(8,128)(2,1)} %bitcast.24.own_ref), channel_id=1, source_target_pairs={{1,0},{2,1},{3,2},{5,4},{6,5},{7,6},{9,8},{10,9},{11,10},{13,12},{... | collective-permute-start | bytes 1966088 | tf_op jit(solution)/shard_map/ppermute | solution.py:27
  118.6 18.5 %collective-permute-start.19 = (bf16[2,256,640]{2,1,0:T(8,128)(2,1)}, bf16[2,256,640]{2,1,0:T(8,128)(2,1)}, u32[]{:S(2)}, u32[]{:S(2)}) collective-permute-start(bf16[2,256,640]{2,1,0:T(8,128)(2,1)} %bitcast.24.own_ref), channel_id=1, source_target_pairs={{0,1},{1,2},{2,3},{4,5},{5,6},{6,7},{8,9},{9,10},{10,11},{12,13},{... | collective-permute-start | bytes 1966088 | tf_op jit(solution)/shard_map/ppermute | solution.py:26
  150.1 18.8 %collective-permute-start.22 = (bf16[2,256,640]{2,1,0:T(8,128)(2,1)S(1)}, bf16[2,256,640]{2,1,0:T(8,128)(2,1)S(1)}, u32[]{:S(2)}, u32[]{:S(2)}) collective-permute-start(bf16[2,256,640]{2,1,0:T(8,128)(2,1)S(1)} %bitcast.89), channel_id=1, source_target_pairs={{1,0},{2,1},{3,2},{5,4},{6,5},{7,6},{9,8},{10,9},{11,10},{13,12},{... | collective-permute-start | bytes 1966088 | tf_op jit(solution)/shard_map/ppermute | solution.py:27
  151.4 18.7 %collective-permute-start.21 = (bf16[2,256,640]{2,1,0:T(8,128)(2,1)S(1)}, bf16[2,256,640]{2,1,0:T(8,128)(2,1)S(1)}, u32[]{:S(2)}, u32[]{:S(2)}) collective-permute-start(bf16[2,256,640]{2,1,0:T(8,128)(2,1)S(1)} %bitcast.90), channel_id=1, source_target_pairs={{0,1},{1,2},{2,3},{4,5},{5,6},{6,7},{8,9},{9,10},{10,11},{12,13},{... | collective-permute-start | bytes 1966088 | tf_op jit(solution)/shard_map/ppermute | solution.py:26
  191.4 16.4 %collective-permute-start.24 = (bf16[2,128,640]{2,1,0:T(8,128)(2,1)S(1)}, bf16[2,128,640]{2,1,0:T(8,128)(2,1)S(1)}, u32[]{:S(2)}, u32[]{:S(2)}) collective-permute-start(bf16[2,128,640]{2,1,0:T(8,128)(2,1)S(1)} %get-tuple-element.240), channel_id=1, source_target_pairs={{1,0},{2,1},{3,2},{5,4},{6,5},{7,6},{9,8},{10,9},{11,10},{13,12},{... | collective-permute-start | bytes 983048 | tf_op jit(solution)/shard_map/ppermute | solution.py:27
  207.7 15.5 %collective-permute-start.25 = (bf16[4,560,640]{2,1,0:T(8,128)(2,1)}, bf16[4,560,640]{2,1,0:T(8,128)(2,1)S(1)}, u32[]{:S(2)}, u32[]{:S(2)}) collective-permute-start(bf16[4,560,640]{2,1,0:T(8,128)(2,1)} %get-tuple-element.191), channel_id=1, source_target_pairs={{0,4},{4,0},{8,12},{12,8},{16,20},{20,16},{24,28},{28,24},{1,5},{5... | collective-permute-start | bytes 8601608 | tf_op jit(solution)/shard_map/ppermute | solution.py:887
  226.5 30.1 %collective-permute-start.29 = (bf16[2,464,640]{2,1,0:T(8,128)(2,1)}, bf16[2,464,640]{2,1,0:T(8,128)(2,1)S(1)}, u32[]{:S(2)}, u32[]{:S(2)}) collective-permute-start(bf16[2,464,640]{2,1,0:T(8,128)(2,1)} %get-tuple-element.203), channel_id=1, source_target_pairs={{0,16},{4,20},{8,24},{12,28},{16,0},{20,4},{24,8},{28,12},{1,17},{... | collective-permute-start | bytes 3563528 | tf_op jit(solution)/shard_map/ppermute | solution.py:887
  227.9 28.0 %collective-permute-start.28 = (bf16[2,448,640]{2,1,0:T(8,128)(2,1)}, bf16[2,448,640]{2,1,0:T(8,128)(2,1)}, u32[]{:S(2)}, u32[]{:S(2)}) collective-permute-start(bf16[2,448,640]{2,1,0:T(8,128)(2,1)} %get-tuple-element.201), channel_id=1, source_target_pairs={{0,8},{4,12},{8,0},{12,4},{16,24},{20,28},{24,16},{28,20},{1,9},{5... | collective-permute-start | bytes 3440648 | tf_op jit(solution)/shard_map/ppermute | solution.py:887
  236.5 20.2 %collective-permute-start.32 = (bf16[144,640]{1,0:T(8,128)(2,1)S(1)}, bf16[144,640]{1,0:T(8,128)(2,1)S(1)}, u32[]{:S(2)}, u32[]{:S(2)}) collective-permute-start(bf16[144,640]{1,0:T(8,128)(2,1)S(1)} %get-tuple-element.236), channel_id=1, source_target_pairs={{0,3},{1,0},{2,1},{3,2},{4,7},{5,4},{6,5},{7,6},{8,11},{9,8},{10,9... | collective-permute-start | bytes 552968 | tf_op jit(solution)/shard_map/ppermute | solution.py:905
  241.1 15.6 %collective-permute-start.31 = (bf16[144,640]{1,0:T(8,128)(2,1)S(1)}, bf16[144,640]{1,0:T(8,128)(2,1)S(1)}, u32[]{:S(2)}, u32[]{:S(2)}) collective-permute-start(bf16[144,640]{1,0:T(8,128)(2,1)S(1)} %get-tuple-element.237), channel_id=1, source_target_pairs={{0,2},{1,3},{2,0},{3,1},{4,6},{5,7},{6,4},{7,5},{8,10},{9,11},{10,... | collective-permute-start | bytes 552968 | tf_op jit(solution)/shard_map/ppermute | solution.py:905
  241.1 15.6 %collective-permute-start.30 = (bf16[144,640]{1,0:T(8,128)(2,1)S(1)}, bf16[144,640]{1,0:T(8,128)(2,1)S(1)}, u32[]{:S(2)}, u32[]{:S(2)}) collective-permute-start(bf16[144,640]{1,0:T(8,128)(2,1)S(1)} %get-tuple-element.238), channel_id=1, source_target_pairs={{0,1},{1,2},{2,3},{3,0},{4,5},{5,6},{6,7},{7,4},{8,9},{9,10},{10,1... | collective-permute-start | bytes 552968 | tf_op jit(solution)/shard_map/ppermute | solution.py:905
  258.5 16.1 %collective-permute-start.34 = (bf16[464,640]{1,0:T(8,128)(2,1)S(1)}, bf16[464,640]{1,0:T(8,128)(2,1)S(1)}, u32[]{:S(2)}, u32[]{:S(2)}) collective-permute-start(bf16[464,640]{1,0:T(8,128)(2,1)S(1)} %get-tuple-element.213), channel_id=1, source_target_pairs={{0,8},{4,12},{8,0},{12,4},{16,24},{20,28},{24,16},{28,20},{1,9},{5... | collective-permute-start | bytes 1781768 | tf_op jit(solution)/shard_map/ppermute | solution.py:887
  279.2 25.3 %collective-permute-start.36 = (bf16[240,640]{1,0:T(8,128)(2,1)S(1)}, bf16[240,640]{1,0:T(8,128)(2,1)S(1)}, u32[]{:S(2)}, u32[]{:S(2)}) collective-permute-start(bf16[240,640]{1,0:T(8,128)(2,1)S(1)} %get-tuple-element.233), channel_id=1, source_target_pairs={{0,2},{1,3},{2,0},{3,1},{4,6},{5,7},{6,4},{7,5},{8,10},{9,11},{10,... | collective-permute-start | bytes 921608 | tf_op jit(solution)/shard_map/ppermute | solution.py:905
  279.2 25.3 %collective-permute-start.35 = (bf16[240,640]{1,0:T(8,128)(2,1)S(1)}, bf16[240,640]{1,0:T(8,128)(2,1)S(1)}, u32[]{:S(2)}, u32[]{:S(2)}) collective-permute-start(bf16[240,640]{1,0:T(8,128)(2,1)S(1)} %get-tuple-element.234), channel_id=1, source_target_pairs={{0,1},{1,2},{2,3},{3,0},{4,5},{5,6},{6,7},{7,4},{8,9},{9,10},{10,1... | collective-permute-start | bytes 921608 | tf_op jit(solution)/shard_map/ppermute | solution.py:905
  (75 other events, 596.1 us)
Sparse Core Ops, SparseCore 0:
  48.3 43.0 all-gather.4
  93.9 43.1 all-gather.6
  170.2 64.0 reduce-scatter.1

commit v5 on v3

--- a/solution.py
+++ b/solution.py
@@ -21,11 +21,15 @@
 
 def seq_neighbours(block, width):
     count = lax.axis_size("seq")
-    forward = [(i, i + 1) for i in range(count - 1)]
-    backward = [(target, source) for source, target in forward]
-    low = lax.ppermute(block[:, block.shape[1] - width :], "seq", forward)
-    high = lax.ppermute(block[:, :width], "seq", backward)
-    return low, high
+    odd = lax.axis_index("seq") % 2 == 1
+    near = [(i, i ^ 1) for i in range(count)]
+    far = [(i, i + 1) for i in range(1, count - 1, 2)]
+    far += [(target, source) for source, target in far]
+    low_part, high_part = block[:, :width], block[:, block.shape[1] - width :]
+    whole = width == block.shape[1]
+    first = block if whole else jnp.where(odd, low_part, high_part)
+    second = block if whole else jnp.where(odd, high_part, low_part)
+    return lax.ppermute(first, "seq", near), lax.ppermute(second, "seq", far)
 
 
 def normalized(values):
@@ -107,10 +111,13 @@
     act_two_ref[...] = norm_gelu(u, narrow_ref[1:2, :], narrow_ref[2:3, :]).astype(jnp.bfloat16)
 
 
-def tap_slices(low_ref, own_ref, high_ref, flag_ref, dilation_step):
+def tap_slices(place_ref, first_ref, own_ref, second_ref, flag_ref, dilation_step):
     length = own_ref.shape[1]
-    width = low_ref.shape[1]
-    padded = jnp.concatenate([low_ref[0], own_ref[0], high_ref[0]], axis=0)
+    width = first_ref.shape[1]
+    odd = place_ref[1] % 2 == 1
+    low = jnp.where(odd, first_ref[0], second_ref[0])
+    high = jnp.where(odd, second_ref[0], first_ref[0])
+    padded = jnp.concatenate([low, own_ref[0], high], axis=0)
     for k in range(KER):
         start = width + (k - KER // 2) * dilation_step
         yield k, padded[start : start + length] * flag_ref[0][:, k : k + 1]
@@ -118,6 +125,7 @@
 
 def convolve_kernel(
     dilation_step,
+    place_ref,
     low_ref,
     own_ref,
     high_ref,
@@ -140,7 +148,7 @@
     taps = (k0_ref, k1_ref, k2_ref, k3_ref, k4_ref)
     hidden = own_ref.shape[2]
     total = narrow_ref[3:4, :]
-    for k, piece in tap_slices(low_ref, own_ref, high_ref, flag_ref, dilation_step):
+    for k, piece in tap_slices(place_ref, low_ref, own_ref, high_ref, flag_ref, dilation_step):
         tap_ref[:, k * hidden : (k + 1) * hidden] = piece
         total = total + matmul(piece, merged(taps[k]))
     v_ref[...] = total
@@ -196,6 +204,7 @@
 
 def conv_back_kernel(
     dilation_step,
+    place_ref,
     low_ref,
     own_ref,
     high_ref,
@@ -223,7 +232,7 @@
 
     taps = (k0_ref, k1_ref, k2_ref, k3_ref, k4_ref)
     total = None
-    for k, piece in tap_slices(low_ref, own_ref, high_ref, flag_ref, dilation_step):
+    for k, piece in tap_slices(place_ref, low_ref, own_ref, high_ref, flag_ref, dilation_step):
         term = matmul_back(piece, merged(taps[KER - 1 - k]))
         total = term if total is None else total + term
     gu, gain_sum, bias_sum = norm_gelu_back(
@@ -595,6 +604,7 @@
         functools.partial(convolve_kernel, dilation_step),
         rows,
         [
+            scalars(),
             row_block(low.shape),
             row_block(act_two.shape),
             row_block(high.shape),
@@ -620,6 +630,7 @@
         16 * tokens * model,
         "convolve",
     )(
+        place(),
         low,
         act_two,
         high,
@@ -694,6 +705,7 @@
         functools.partial(conv_back_kernel, dilation_step),
         rows,
         [
+            scalars(),
             row_block(low.shape),
             row_block(gv.shape),
             row_block(high.shape),
@@ -718,6 +730,7 @@
         "conv_back",
         room=56 if dilation_step == SECOND_DILATION else 32,
     )(
+        place(),
         low,
         gv,
         high,

time: 315 us -> 311 us (0.987)
  starting transfers between devices: 54.7 us -> 37.1 us
  waiting for transfers between devices: 117 us -> 128 us
    ppermute x8, starting transfers between devices: 22.7 us -> 10.5 us  [seq_neighbours(): return (lax.ppermute(first, 'seq', near), lax.ppermute(second, 'seq', far))]
    ppermute x8, waiting for transfers between devices: 22.9 us -> 27.8 us  [seq_neighbours(): return (lax.ppermute(first, 'seq', near), lax.ppermute(second, 'seq', far))]
    all_gather x1, waiting for transfers between devices: 0.2 us -> 3.48 us  [late_weights(): return weights(1, lax.all_gather(after(rows, early_whole, projected), 'dp'))]
    ppermute x15, starting transfers between devices: 16.6 us -> 13.5 us  [dp_swapped(): return lax.ppermute(block, 'dp', [(i, i ^ 1 << bit) for i in range(count)])]
    unnamed x116 -> x134, local copies, waits for them, and re-layouts: 28.6 us -> 30.9 us
  transfers between devices with their start and end apart: 41 -> 41, of which waited for: 26 -> 24; matrix products, arithmetic and copies ran while one was open for 4% -> 4% of each run, Pallas kernels for 21% -> 21%
where the time goes in v5:
time: 311 us; the launch traced here: 309 us
  waiting for transfers between devices  128 us (41%)
  Pallas kernels  86.7 us (28%)
  local copies, waits for them, and re-layouts  40.1 us (13%)
  starting transfers between devices  37.1 us (12%)
  between operations  14.6 us (5%)
    ppermute x15, waiting for transfers between devices, shifted(): lax.ppermute(block, 'seq', [(i, (i + step) % count) for i in range(count)])  54.3 us
    ppermute x15, waiting for transfers between devices, dp_swapped(): return lax.ppermute(block, 'dp', [(i, i ^ 1 << bit) for i in range(count)])  36.7 us
    unnamed x134, local copies, waits for them, and re-layouts  30.9 us
    ppermute x8, waiting for transfers between devices, seq_neighbours(): return (lax.ppermute(first, 'seq', near), lax.ppermute(second, 'seq', far))  27.8 us
    pallas_call x2, Pallas kernels, conv_back_with(): call(functools.partial(conv_back_kernel, dilation_step), rows, [scalars()...  22.6 us
    pallas_call x2, Pallas kernels, convolve(): call(functools.partial(convolve_kernel, dilation_step), rows, [scalars(),...  13.6 us
    ppermute x15, starting transfers between devices, dp_swapped(): return lax.ppermute(block, 'dp', [(i, i ^ 1 << bit) for i in range(count)])  13.5 us
    ppermute x15, starting transfers between devices, shifted(): lax.ppermute(block, 'seq', [(i, (i + step) % count) for i in range(count)])  13 us
  transfers between devices with their start and end apart: 41, of which 24 were waited for; matrix products, arithmetic and copies ran while one was open for 4% of the time, Pallas kernels for 21%

profile of v5, /device:TPU:17, one launch (start us, length us, event | category | flops | bytes accessed | tf_op | source)
XLA Modules:
  0.0 308.7 jit_solution(6088225503302301498)
XLA Ops:
  30.3 9.4 %collective-permute-done.6.refs_2_ = bf16[144,640]{1,0:T(8,128)(2,1)S(1)} collective-permute-done((bf16[144,640]{1,0:T(8,128)(2,1)S(1)}, bf16[144,640]{1,0:T(8,128)(2,1)S(1)}, u32[]{:S(2)}, u32[]{:S(2)}) %collective-permute-start.6) | collective-permute-done | bytes 184352 | tf_op jit(solution)/shard_map/ppermute | solution.py:918
  39.7 3.8 %collective-permute-done.5.refs_1_ = bf16[144,640]{1,0:T(8,128)(2,1)S(1)} collective-permute-done((bf16[144,640]{1,0:T(8,128)(2,1)S(1)}, bf16[144,640]{1,0:T(8,128)(2,1)S(1)}, u32[]{:S(2)}, u32[]{:S(2)}) %collective-permute-start.5) | collective-permute-done | bytes 184352 | tf_op jit(solution)/shard_map/ppermute | solution.py:918
  47.9 3.7 %collective-permute-done.12.refs_3_ = bf16[144,640]{1,0:T(8,128)(2,1)S(1)} collective-permute-done((bf16[144,640]{1,0:T(8,128)(2,1)S(1)}, bf16[144,640]{1,0:T(8,128)(2,1)S(1)}, u32[]{:S(2)}, u32[]{:S(2)}) %collective-permute-start.12) | collective-permute-done | bytes 184352 | tf_op jit(solution)/shard_map/ppermute | solution.py:918
  55.6 6.0 %collective-permute-done.11.refs_2_ = bf16[144,640]{1,0:T(8,128)(2,1)S(1)} collective-permute-done((bf16[144,640]{1,0:T(8,128)(2,1)S(1)}, bf16[144,640]{1,0:T(8,128)(2,1)S(1)}, u32[]{:S(2)}, u32[]{:S(2)}) %collective-permute-start.11) | collective-permute-done | bytes 184352 | tf_op jit(solution)/shard_map/ppermute | solution.py:918
  73.4 4.2 %project.2 = (bf16[512,1280]{1,0:T(8,128)(2,1)S(1)}, f32[512,640]{1,0:T(8,128)S(1)}, bf16[512,640]{1,0:T(8,128)(2,1)S(1)}) custom-call(bf16[512,1280]{1,0:T(8,128)(2,1)S(1)} %bitcast.84, bf16[8,352,640]{2,1,0:T(8,128)(2,1)S(1)} %copy-done.4, f32[3,1280]{1,0:T(4,128)S(1)} %reshape.818.wide_ref, f32[6,640]{1,0:T(8,128)S(1)} %reshape.819.narrow_ref), custom_call_target="tpu_custom_call" | custom-call | flops 1677721600 | bytes 7864320 | tf_op jit(solution)/shard_map/project/pallas_call | solution.py:583
  82.9 6.8 %collective-permute-done.18.high_ref = bf16[2,128,640]{2,1,0:T(8,128)(2,1)S(1)} collective-permute-done((bf16[2,128,640]{2,1,0:T(8,128)(2,1)S(1)}, bf16[2,128,640]{2,1,0:T(8,128)(2,1)S(1)}, u32[]{:S(2)}, u32[]{:S(2)}) %collective-permute-start.18) | collective-permute-done | bytes 327712 | tf_op jit(solution)/shard_map/ppermute | solution.py:32
  100.1 6.0 %convolve.2 = (bf16[512,3200]{1,0:T(8,128)(2,1)S(1)}, f32[512,640]{1,0:T(8,128)S(1)}, bf16[512,640]{1,0:T(8,128)(2,1)S(1)}, f32[512,1280]{1,0:T(8,128)S(1)}) custom-call(s32[2]{0:T(128)S(1)} %pad_add_fusion.place_ref, bf16[2,128,640]{2,1,0:T(8,128)(2,1)S(1)} %copy-done.28, bf16[2,256,640]{2,1,0:T(8,128)(2,1)S(1)} %bitcast.93, ...), custom_call_target="tpu_custom_call" | custom-call | flops 2936012800 | bytes 10485760 | tf_op jit(solution)/shard_map/convolve/pallas_call | solution.py:603
  107.9 4.8 %project.3 = (bf16[512,1280]{1,0:T(8,128)(2,1)S(1)}, f32[512,640]{1,0:T(8,128)S(1)}, bf16[512,640]{1,0:T(8,128)(2,1)}) custom-call(f32[512,1280]{1,0:T(8,128)S(1)} %get-tuple-element.136.x_ref, bf16[8,352,640]{2,1,0:T(8,128)(2,1)S(1)} %copy-done.5, f32[3,1280]{1,0:T(4,128)S(1)} %reshape.821.wide_ref, f32[6,640]{1,0:T(8,128)S(1)} %reshape.822.narrow_ref), custom_call_target="tpu_custom_call" | custom-call | flops 1677721600 | bytes 7864320 | tf_op jit(solution)/shard_map/project/pallas_call | solution.py:583
  118.6 13.8 %collective-permute-done.20.high_ref = bf16[2,256,640]{2,1,0:T(8,128)(2,1)} collective-permute-done((bf16[2,256,640]{2,1,0:T(8,128)(2,1)}, bf16[2,256,640]{2,1,0:T(8,128)(2,1)}, u32[]{:S(2)}, u32[]{:S(2)}) %collective-permute-start.20) | collective-permute-done | bytes 655392 | tf_op jit(solution)/shard_map/ppermute | solution.py:32
  132.4 3.5 %all-gather.7.cloned.1.call-done = bf16[4480,640]{1,0:T(8,128)(2,1)} async-done(((bf16[560,640]{1,0:T(8,128)(2,1)}), bf16[4480,640]{1,0:T(8,128)(2,1)}) %all-gather.7.cloned.1.call-update) | async-done | bytes 5734416 | tf_op jit(solution)/shard_map/all_gather | solution.py:1215
  138.6 7.6 %convolve.3 = (bf16[512,3200]{1,0:T(8,128)(2,1)S(1)}, f32[512,640]{1,0:T(8,128)S(1)}, bf16[512,640]{1,0:T(8,128)(2,1)S(1)}, bf16[512,1280]{1,0:T(8,128)(2,1)}) custom-call(s32[2]{0:T(128)S(1)} %pad_add_fusion.place_ref, bf16[2,256,640]{2,1,0:T(8,128)(2,1)} %collective-permute-done.19.low_ref, bf16[2,256,640]{2,1,0:T(8,128)(2,1)} %bitcast.24.own_ref, ...), custom_call_target="tpu_custom_call" | custom-call | flops 2936012800 | bytes 10485760 | tf_op jit(solution)/shard_map/convolve/pallas_call | solution.py:603
  146.2 3.5 %out_back.2 = (bf16[512,1280]{1,0:T(8,128)(2,1)S(1)}, bf16[512,640]{1,0:T(8,128)(2,1)S(1)}, f32[8,640]{1,0:T(8,128)S(1)}, f32[8,1280]{1,0:T(8,128)S(1)}) custom-call(bf16[512,1280]{1,0:T(8,128)(2,1)S(1)} %bitcast.88, f32[512,640]{1,0:T(8,128)S(1)} %get-tuple-element.149.v_ref, bf16[8,560,640]{2,1,0:T(8,128)(2,1)S(1)} %bitcast.82, ...), custom_call_target="tpu_custom_call" | custom-call | flops 1677721600 | bytes 6553600 | tf_op jit(solution)/shard_map/out_back/pallas_call | solution.py:649
  152.0 6.1 %weight_grads.1 = bf16[8,560,640]{2,1,0:T(8,128)(2,1)S(1)} custom-call(bf16[512,3200]{1,0:T(8,128)(2,1)S(1)} %get-tuple-element.148.tap_ref, bf16[512,640]{1,0:T(8,128)(2,1)S(1)} %get-tuple-element.150.gv_ref, bf16[512,640]{1,0:T(8,128)(2,1)S(1)} %get-tuple-element.151.act_three_ref, bf16[512,1280]{1,0:T(8,128)(2,1)S(1)} %get-tuple-element.152.short_ref), custom_call_target="tpu_custom_call" | custom-call | flops 2936012800 | bytes 5242880 | tf_op jit(solution)/shard_map/weight_grads/pallas_call | solution.py:677
  160.5 7.2 %collective-permute-done.22.high_ref = bf16[2,256,640]{2,1,0:T(8,128)(2,1)S(1)} collective-permute-done((bf16[2,256,640]{2,1,0:T(8,128)(2,1)S(1)}, bf16[2,256,640]{2,1,0:T(8,128)(2,1)S(1)}, u32[]{:S(2)}, u32[]{:S(2)}) %collective-permute-start.22) | collective-permute-done | bytes 655392 | tf_op jit(solution)/shard_map/ppermute | solution.py:32
  168.8 12.9 %conv_back.2 = (bf16[512,640]{1,0:T(8,128)(2,1)}, f32[512,1280]{1,0:T(8,128)}, f32[8,640]{1,0:T(8,128)}, f32[8,1280]{1,0:T(8,128)}) custom-call(s32[2]{0:T(128)} %copy-done.40, bf16[2,256,640]{2,1,0:T(8,128)(2,1)} %copy-done.57, bf16[2,256,640]{2,1,0:T(8,128)(2,1)} %bitcast.91, bf16[2,256,640]{2,1,0:T(8,128)(2,1)} %copy-done.56, ...), custom_call_target="tpu_custom_call" | custom-call | flops 2936012800 | bytes 10485760 | tf_op jit(solution)/shard_map/conv_back/pallas_call | solution.py:704
  186.4 3.5 %out_back.3 = (bf16[512,1280]{1,0:T(8,128)(2,1)S(1)}, bf16[512,640]{1,0:T(8,128)(2,1)S(1)}, f32[8,640]{1,0:T(8,128)S(1)}, f32[8,1280]{1,0:T(8,128)S(1)}) custom-call(f32[512,1280]{1,0:T(8,128)S(1)} %copy-done.9, f32[512,640]{1,0:T(8,128)S(1)} %copy-done.18, bf16[8,560,640]{2,1,0:T(8,128)(2,1)S(1)} %bitcast.63, bf16[8,560,640]{2,1,0:T(8,128)(2,1)S(1)} %bitcast.64, ...), custom_call_target="tpu_custom_call" | custom-call | flops 1677721600 | bytes 6553600 | tf_op jit(solution)/shard_map/out_back/pallas_call | solution.py:649
  195.5 7.7 %share_grads.1 = (bf16[4,560,640]{2,1,0:T(8,128)(2,1)S(1)}, bf16[4,560,640]{2,1,0:T(8,128)(2,1)}) custom-call(s32[2]{0:T(128)S(1)} %copy-done.41, bf16[512,3200]{1,0:T(8,128)(2,1)S(1)} %copy-done.43, bf16[512,640]{1,0:T(8,128)(2,1)S(1)} %get-tuple-element.164.gv_ref, bf16[512,640]{1,0:T(8,128)(2,1)S(1)} %copy-done.47, ...), custom_call_target="tpu_custom_call" | custom-call | flops 2936012800 | bytes 5242880 | tf_op jit(solution)/shard_map/share_grads/pallas_call | solution.py:782
  205.0 9.6 %conv_back.3 = (bf16[512,640]{1,0:T(8,128)(2,1)S(1)}, f32[512,1280]{1,0:T(8,128)}, f32[8,640]{1,0:T(8,128)S(1)}, f32[8,1280]{1,0:T(8,128)S(1)}) custom-call(s32[2]{0:T(128)S(1)} %copy-done.41, bf16[2,128,640]{2,1,0:T(8,128)(2,1)S(1)} %collective-permute-done.23.low_ref, bf16[2,256,640]{2,1,0:T(8,128)(2,1)S(1)} %bitcast.95, ...), custom_call_target="tpu_custom_call" | custom-call | flops 2936012800 | bytes 10485760 | tf_op jit(solution)/shard_map/conv_back/pallas_call | solution.py:704
  224.9 5.2 %reduce-scatter.2.cloned.1.call-done = bf16[1,560,640]{2,1,0:T(8,128)(2,1)} async-done(((bf16[8,560,640]{2,1,0:T(8,128)(2,1)}), bf16[1,560,640]{2,1,0:T(8,128)(2,1)}) %reduce-scatter.2.cloned.1.call-update) | async-done | bytes 716816 | tf_op jit(solution)/shard_map/reduce_scatter | solution.py:1236
  235.0 16.9 %collective-permute-done.28.got_a = bf16[2,448,640]{2,1,0:T(8,128)(2,1)} collective-permute-done((bf16[2,448,640]{2,1,0:T(8,128)(2,1)}, bf16[2,448,640]{2,1,0:T(8,128)(2,1)}, u32[]{:S(2)}, u32[]{:S(2)}) %collective-permute-start.28) | collective-permute-done | bytes 1146912 | tf_op jit(solution)/shard_map/ppermute | solution.py:900
  256.5 13.3 %collective-permute-done.33.refs_1_ = bf16[448,640]{1,0:T(8,128)(2,1)S(1)} collective-permute-done((bf16[448,640]{1,0:T(8,128)(2,1)S(1)}, bf16[448,640]{1,0:T(8,128)(2,1)S(1)}, u32[]{:S(2)}, u32[]{:S(2)}) %collective-permute-start.33) | collective-permute-done | bytes 573472 | tf_op jit(solution)/shard_map/ppermute | solution.py:900
  274.5 3.7 %collective-permute-done.37.refs_3_ = bf16[240,640]{1,0:T(8,128)(2,1)S(1)} collective-permute-done((bf16[240,640]{1,0:T(8,128)(2,1)S(1)}, bf16[240,640]{1,0:T(8,128)(2,1)S(1)}, u32[]{:S(2)}, u32[]{:S(2)}) %collective-permute-start.37) | collective-permute-done | bytes 307232 | tf_op jit(solution)/shard_map/ppermute | solution.py:918
  278.2 17.8 %collective-permute-done.36.refs_2_ = bf16[240,640]{1,0:T(8,128)(2,1)S(1)} collective-permute-done((bf16[240,640]{1,0:T(8,128)(2,1)S(1)}, bf16[240,640]{1,0:T(8,128)(2,1)S(1)}, u32[]{:S(2)}, u32[]{:S(2)}) %collective-permute-start.36) | collective-permute-done | bytes 307232 | tf_op jit(solution)/shard_map/ppermute | solution.py:918
  296.0 4.7 %collective-permute-done.35.refs_1_ = bf16[240,640]{1,0:T(8,128)(2,1)S(1)} collective-permute-done((bf16[240,640]{1,0:T(8,128)(2,1)S(1)}, bf16[240,640]{1,0:T(8,128)(2,1)S(1)}, u32[]{:S(2)}, u32[]{:S(2)}) %collective-permute-start.35) | collective-permute-done | bytes 307232 | tf_op jit(solution)/shard_map/ppermute | solution.py:918
  (264 shorter events, 112.2 us)
Async XLA Ops:
  7.2 83.0 %all-gather.5.cloned.1.call-start = ((), (), s32[]{:S(2)}) async-start(), calls=%async_computation.2 | async-start | bytes 6451200 | tf_op jit(solution)/shard_map/all_gather | solution.py:1202
  23.1 20.4 %collective-permute-start.4 = (bf16[176,640]{1,0:T(8,128)(2,1)S(1)}, bf16[176,640]{1,0:T(8,128)(2,1)S(1)}, u32[]{:S(2)}, u32[]{:S(2)}) collective-permute-start(bf16[176,640]{1,0:T(8,128)(2,1)S(1)} %get-tuple-element.257), channel_id=1, source_target_pairs={{0,16},{4,20},{8,24},{12,28},{16,0},{20,4},{24,8},{28,12},{1,17},{... | collective-permute-start | bytes 675848 | tf_op jit(solution)/shard_map/ppermute | solution.py:900
  24.4 19.1 %collective-permute-start.3 = (bf16[176,640]{1,0:T(8,128)(2,1)S(1)}, bf16[176,640]{1,0:T(8,128)(2,1)S(1)}, u32[]{:S(2)}, u32[]{:S(2)}) collective-permute-start(bf16[176,640]{1,0:T(8,128)(2,1)S(1)} %get-tuple-element.258), channel_id=1, source_target_pairs={{0,8},{4,12},{8,0},{12,4},{16,24},{20,28},{24,16},{28,20},{1,9},{5... | collective-permute-start | bytes 675848 | tf_op jit(solution)/shard_map/ppermute | solution.py:900
  25.7 14.1 %collective-permute-start.6 = (bf16[144,640]{1,0:T(8,128)(2,1)S(1)}, bf16[144,640]{1,0:T(8,128)(2,1)S(1)}, u32[]{:S(2)}, u32[]{:S(2)}) collective-permute-start(bf16[144,640]{1,0:T(8,128)(2,1)S(1)} %copy-done.38), channel_id=1, source_target_pairs={{0,2},{1,3},{2,0},{3,1},{4,6},{5,7},{6,4},{7,5},{8,10},{9,11},{10,... | collective-permute-start | bytes 552968 | tf_op jit(solution)/shard_map/ppermute | solution.py:918
  26.5 17.0 %collective-permute-start.5 = (bf16[144,640]{1,0:T(8,128)(2,1)S(1)}, bf16[144,640]{1,0:T(8,128)(2,1)S(1)}, u32[]{:S(2)}, u32[]{:S(2)}) collective-permute-start(bf16[144,640]{1,0:T(8,128)(2,1)S(1)} %copy-done.38), channel_id=1, source_target_pairs={{0,1},{1,2},{2,3},{3,0},{4,5},{5,6},{6,7},{7,4},{8,9},{9,10},{10,1... | collective-permute-start | bytes 552968 | tf_op jit(solution)/shard_map/ppermute | solution.py:918
  45.5 90.4 %all-gather.7.cloned.1.call-start = ((), (), s32[]{:S(2)}) async-start(), calls=%async_computation.3 | async-start | bytes 6451200 | tf_op jit(solution)/shard_map/all_gather | solution.py:1215
  45.6 18.9 %collective-permute-start.9 = (bf16[2,176,640]{2,1,0:T(8,128)(2,1)S(1)}, bf16[2,176,640]{2,1,0:T(8,128)(2,1)S(1)}, u32[]{:S(2)}, u32[]{:S(2)}) collective-permute-start(bf16[2,176,640]{2,1,0:T(8,128)(2,1)S(1)} %pad_maximum_fusion.1.refs_2_), channel_id=1, source_target_pairs={{0,8},{4,12},{8,0},{12,4},{16,24},{20,28},{24,16},{28,20},{1,9},{5... | collective-permute-start | bytes 1351688 | tf_op jit(solution)/shard_map/ppermute | solution.py:900
  46.0 18.5 %collective-permute-start.8 = (bf16[2,176,640]{2,1,0:T(8,128)(2,1)S(1)}, bf16[2,176,640]{2,1,0:T(8,128)(2,1)S(1)}, u32[]{:S(2)}, u32[]{:S(2)}) collective-permute-start(bf16[2,176,640]{2,1,0:T(8,128)(2,1)S(1)} %pad_maximum_fusion.refs_0_), channel_id=1, source_target_pairs={{0,16},{4,20},{8,24},{12,28},{16,0},{20,4},{24,8},{28,12},{1,17},{... | collective-permute-start | bytes 1351688 | tf_op jit(solution)/shard_map/ppermute | solution.py:900
  46.4 15.2 %collective-permute-start.11 = (bf16[144,640]{1,0:T(8,128)(2,1)S(1)}, bf16[144,640]{1,0:T(8,128)(2,1)S(1)}, u32[]{:S(2)}, u32[]{:S(2)}) collective-permute-start(bf16[144,640]{1,0:T(8,128)(2,1)S(1)} %copy-done.30), channel_id=1, source_target_pairs={{0,2},{1,3},{2,0},{3,1},{4,6},{5,7},{6,4},{7,5},{8,10},{9,11},{10,... | collective-permute-start | bytes 552968 | tf_op jit(solution)/shard_map/ppermute | solution.py:918
  46.4 17.4 %collective-permute-start.10 = (bf16[144,640]{1,0:T(8,128)(2,1)S(1)}, bf16[144,640]{1,0:T(8,128)(2,1)S(1)}, u32[]{:S(2)}, u32[]{:S(2)}) collective-permute-start(bf16[144,640]{1,0:T(8,128)(2,1)S(1)} %copy-done.30), channel_id=1, source_target_pairs={{0,1},{1,2},{2,3},{3,0},{4,5},{5,6},{6,7},{7,4},{8,9},{9,10},{10,1... | collective-permute-start | bytes 552968 | tf_op jit(solution)/shard_map/ppermute | solution.py:918
  90.2 139.9 %reduce-scatter.2.cloned.1.call-start = ((), (), s32[]{:S(2)}) async-start(), calls=%async_computation.1 | async-start | bytes 6451200 | tf_op jit(solution)/shard_map/reduce_scatter | solution.py:1236
  114.8 17.6 %collective-permute-start.20 = (bf16[2,256,640]{2,1,0:T(8,128)(2,1)}, bf16[2,256,640]{2,1,0:T(8,128)(2,1)}, u32[]{:S(2)}, u32[]{:S(2)}) collective-permute-start(bf16[2,256,640]{2,1,0:T(8,128)(2,1)} %bitcast.24.own_ref), channel_id=1, source_target_pairs={{1,2},{2,1},{5,6},{6,5},{9,10},{10,9},{13,14},{14,13},{17,18},{18,... | collective-permute-start | bytes 1966088 | tf_op jit(solution)/shard_map/ppermute | solution.py:32
  117.7 14.8 %collective-permute-start.19 = (bf16[2,256,640]{2,1,0:T(8,128)(2,1)}, bf16[2,256,640]{2,1,0:T(8,128)(2,1)}, u32[]{:S(2)}, u32[]{:S(2)}) collective-permute-start(bf16[2,256,640]{2,1,0:T(8,128)(2,1)} %bitcast.24.own_ref), channel_id=1, source_target_pairs={{0,1},{1,0},{2,3},{3,2},{4,5},{5,4},{6,7},{7,6},{8,9},{9,8},{10,11... | collective-permute-start | bytes 1966088 | tf_op jit(solution)/shard_map/ppermute | solution.py:32
  149.7 18.0 %collective-permute-start.22 = (bf16[2,256,640]{2,1,0:T(8,128)(2,1)S(1)}, bf16[2,256,640]{2,1,0:T(8,128)(2,1)S(1)}, u32[]{:S(2)}, u32[]{:S(2)}) collective-permute-start(bf16[2,256,640]{2,1,0:T(8,128)(2,1)S(1)} %bitcast.89), channel_id=1, source_target_pairs={{1,2},{2,1},{5,6},{6,5},{9,10},{10,9},{13,14},{14,13},{17,18},{18,... | collective-permute-start | bytes 1966088 | tf_op jit(solution)/shard_map/ppermute | solution.py:32
  151.9 15.8 %collective-permute-start.21 = (bf16[2,256,640]{2,1,0:T(8,128)(2,1)S(1)}, bf16[2,256,640]{2,1,0:T(8,128)(2,1)S(1)}, u32[]{:S(2)}, u32[]{:S(2)}) collective-permute-start(bf16[2,256,640]{2,1,0:T(8,128)(2,1)S(1)} %bitcast.90), channel_id=1, source_target_pairs={{0,1},{1,0},{2,3},{3,2},{4,5},{5,4},{6,7},{7,6},{8,9},{9,8},{10,11... | collective-permute-start | bytes 1966088 | tf_op jit(solution)/shard_map/ppermute | solution.py:32
  203.3 17.1 %collective-permute-start.25 = (bf16[4,560,640]{2,1,0:T(8,128)(2,1)}, bf16[4,560,640]{2,1,0:T(8,128)(2,1)S(1)}, u32[]{:S(2)}, u32[]{:S(2)}) collective-permute-start(bf16[4,560,640]{2,1,0:T(8,128)(2,1)} %get-tuple-element.191), channel_id=1, source_target_pairs={{0,4},{4,0},{8,12},{12,8},{16,20},{20,16},{24,28},{28,24},{1,5},{5... | collective-permute-start | bytes 8601608 | tf_op jit(solution)/shard_map/ppermute | solution.py:900
  223.7 29.4 %collective-permute-start.29 = (bf16[2,464,640]{2,1,0:T(8,128)(2,1)}, bf16[2,464,640]{2,1,0:T(8,128)(2,1)S(1)}, u32[]{:S(2)}, u32[]{:S(2)}) collective-permute-start(bf16[2,464,640]{2,1,0:T(8,128)(2,1)} %get-tuple-element.203), channel_id=1, source_target_pairs={{0,16},{4,20},{8,24},{12,28},{16,0},{20,4},{24,8},{28,12},{1,17},{... | collective-permute-start | bytes 3563528 | tf_op jit(solution)/shard_map/ppermute | solution.py:900
  224.6 27.4 %collective-permute-start.28 = (bf16[2,448,640]{2,1,0:T(8,128)(2,1)}, bf16[2,448,640]{2,1,0:T(8,128)(2,1)}, u32[]{:S(2)}, u32[]{:S(2)}) collective-permute-start(bf16[2,448,640]{2,1,0:T(8,128)(2,1)} %get-tuple-element.201), channel_id=1, source_target_pairs={{0,8},{4,12},{8,0},{12,4},{16,24},{20,28},{24,16},{28,20},{1,9},{5... | collective-permute-start | bytes 3440648 | tf_op jit(solution)/shard_map/ppermute | solution.py:900
  232.2 20.9 %collective-permute-start.32 = (bf16[144,640]{1,0:T(8,128)(2,1)S(1)}, bf16[144,640]{1,0:T(8,128)(2,1)S(1)}, u32[]{:S(2)}, u32[]{:S(2)}) collective-permute-start(bf16[144,640]{1,0:T(8,128)(2,1)S(1)} %get-tuple-element.236), channel_id=1, source_target_pairs={{0,3},{1,0},{2,1},{3,2},{4,7},{5,4},{6,5},{7,6},{8,11},{9,8},{10,9... | collective-permute-start | bytes 552968 | tf_op jit(solution)/shard_map/ppermute | solution.py:918
  233.1 20.1 %collective-permute-start.31 = (bf16[144,640]{1,0:T(8,128)(2,1)S(1)}, bf16[144,640]{1,0:T(8,128)(2,1)S(1)}, u32[]{:S(2)}, u32[]{:S(2)}) collective-permute-start(bf16[144,640]{1,0:T(8,128)(2,1)S(1)} %get-tuple-element.237), channel_id=1, source_target_pairs={{0,2},{1,3},{2,0},{3,1},{4,6},{5,7},{6,4},{7,5},{8,10},{9,11},{10,... | collective-permute-start | bytes 552968 | tf_op jit(solution)/shard_map/ppermute | solution.py:918
  235.0 18.1 %collective-permute-start.30 = (bf16[144,640]{1,0:T(8,128)(2,1)S(1)}, bf16[144,640]{1,0:T(8,128)(2,1)S(1)}, u32[]{:S(2)}, u32[]{:S(2)}) collective-permute-start(bf16[144,640]{1,0:T(8,128)(2,1)S(1)} %get-tuple-element.238), channel_id=1, source_target_pairs={{0,1},{1,2},{2,3},{3,0},{4,5},{5,6},{6,7},{7,4},{8,9},{9,10},{10,1... | collective-permute-start | bytes 552968 | tf_op jit(solution)/shard_map/ppermute | solution.py:918
  255.0 14.9 %collective-permute-start.34 = (bf16[464,640]{1,0:T(8,128)(2,1)S(1)}, bf16[464,640]{1,0:T(8,128)(2,1)S(1)}, u32[]{:S(2)}, u32[]{:S(2)}) collective-permute-start(bf16[464,640]{1,0:T(8,128)(2,1)S(1)} %get-tuple-element.213), channel_id=1, source_target_pairs={{0,8},{4,12},{8,0},{12,4},{16,24},{20,28},{24,16},{28,20},{1,9},{5... | collective-permute-start | bytes 1781768 | tf_op jit(solution)/shard_map/ppermute | solution.py:900
  271.5 24.5 %collective-permute-start.36 = (bf16[240,640]{1,0:T(8,128)(2,1)S(1)}, bf16[240,640]{1,0:T(8,128)(2,1)S(1)}, u32[]{:S(2)}, u32[]{:S(2)}) collective-permute-start(bf16[240,640]{1,0:T(8,128)(2,1)S(1)} %get-tuple-element.233), channel_id=1, source_target_pairs={{0,2},{1,3},{2,0},{3,1},{4,6},{5,7},{6,4},{7,5},{8,10},{9,11},{10,... | collective-permute-start | bytes 921608 | tf_op jit(solution)/shard_map/ppermute | solution.py:918
  274.5 26.2 %collective-permute-start.35 = (bf16[240,640]{1,0:T(8,128)(2,1)S(1)}, bf16[240,640]{1,0:T(8,128)(2,1)S(1)}, u32[]{:S(2)}, u32[]{:S(2)}) collective-permute-start(bf16[240,640]{1,0:T(8,128)(2,1)S(1)} %get-tuple-element.234), channel_id=1, source_target_pairs={{0,1},{1,2},{2,3},{3,0},{4,5},{5,6},{6,7},{7,4},{8,9},{9,10},{10,1... | collective-permute-start | bytes 921608 | tf_op jit(solution)/shard_map/ppermute | solution.py:918
  (84 other events, 708.7 us)
Sparse Core Ops, SparseCore 0:
  45.7 44.5 all-gather.4
  92.7 43.2 all-gather.6
  167.9 62.2 reduce-scatter.1
